TPU v7x, 32 devices: a whole 2x2x4 slice. The times are simulated.
32 devices in a mesh: grp: 2 (over x), qa: 16 (over z, y, core).
Axes of the slice: x: 2, y: 2, z: 4, core: 2. Of those that a mesh axis runs over, the one named last changes fastest.
Arguments:
- state: float32 [2, 2097152], P(None, ('grp', 'qa')), parts along dimension 1, may hold values from -6 to 6
- adjoint: float32 [2, 2097152], P(None, ('grp', 'qa')), parts along dimension 1, may hold values from -6 to 6
- gates: float32 [8, 3, 2, 128, 128], P('grp'), parts along dimension 0, may hold values from -0.375 to 0.375
Outputs:
- state_start: float32 [2, 2097152], P(None, ('grp', 'qa')), parts along dimension 1
- adjoint_start: float32 [2, 2097152], P(None, ('grp', 'qa')), parts along dimension 1
- grads: float32 [8, 3, 2, 128, 128], P('grp'), parts along dimension 0
There are 2 independent parts, one for each index of `grp`. A program takes and returns all parts, laid end to end along the dimension named above; each array names one. Nothing has to cross between parts.
All inputs are finite; a program needn't handle non-finite values.
Results may differ from a plain program's by a relative error of at most 0.00014.
Values sent between devices are 32-bit elements; how exact they have to be, the bound alone decides.
No kernel may reach another device: no remote copies, remote signals or barrier semaphores. Data moves between devices by JAX's collectives and lax.ppermute only.
A program may use at most 64 MiB of HBM per device.

v0:
```python
import functools
import math

import jax
import jax.numpy as jnp
from jax import lax
from jax.experimental import pallas as pl
from jax.experimental.pallas import tpu as pltpu
from jax.sharding import PartitionSpec as P

TILE = 8
VMEM = pl.BlockSpec(memory_space=pltpu.VMEM)
SMEM = pl.BlockSpec(memory_space=pltpu.SMEM)
F32 = jnp.float32
BF16 = jnp.bfloat16


def call(body, out_shape, operands, flops, in_specs=None, scratch=(), limit=24 << 20):
    outs = jax.tree.leaves(out_shape)
    moved = sum(math.prod(a.shape) * a.dtype.itemsize for a in (*operands, *outs))
    return pl.pallas_call(
        body,
        out_shape=out_shape,
        in_specs=in_specs or [VMEM] * len(operands),
        out_specs=jax.tree.map(lambda _: VMEM, out_shape),
        scratch_shapes=scratch,
        compiler_params=pltpu.CompilerParams(vmem_limit_bytes=limit),
        cost_estimate=pl.CostEstimate(flops=flops, bytes_accessed=moved, transcendentals=0),
    )(*operands)


def halves(x):
    high = x.astype(BF16)
    return high, (x - high.astype(F32)).astype(BF16)


def contract(first, second, dims):
    dot = functools.partial(
        lax.dot_general, dimension_numbers=(dims, ((), ())), preferred_element_type=F32
    )
    return dot(first[0], second[0]) + (dot(first[0], second[1]) + dot(first[1], second[0]))


def left(matrix, x):
    return contract((matrix[0], matrix[1]), halves(x), ((1,), (0,)))


def right(x, matrix):
    return contract(halves(x), (matrix[0], matrix[1]), ((1,), (0,)))


def order(gate, blocks):
    rows = lax.broadcasted_iota(jnp.int32, (gate, gate), 0)
    columns = lax.broadcasted_iota(jnp.int32, (gate, gate), 1)
    inside = columns % TILE
    middle = (columns // TILE) % blocks
    tile = columns // (TILE * blocks)
    return (rows == (tile * TILE + inside) * blocks + middle).astype(F32)


def exact(first, second, dims):
    return lax.dot_general(
        first, second, (dims, ((), ())), precision=lax.Precision.HIGHEST, preferred_element_type=F32
    )


def prepare_body(rounds, gate, blocks, gates_ref, out_ref):
    permutation = order(gate, blocks)
    for number in range(rounds):
        for position in range(3):
            real = gates_ref[number, position, 0]
            imag = gates_ref[number, position, 1]
            if position == 2:
                real, imag = (
                    exact(exact(permutation, u, ((0,), (0,))), permutation, ((1,), (0,))) for u in (real, imag)
                )
            if position == 1:
                quarters = ((real, -imag), (imag, real))
            else:
                real, imag = real.T, imag.T
                quarters = ((real, imag), (-imag, real))
            for i in range(2):
                for j in range(2):
                    for half, value in enumerate(halves(quarters[i][j])):
                        out_ref[number, position, half, pl.ds(i * gate, gate), pl.ds(j * gate, gate)] = value


def enter_body(gate, blocks, state_ref, adjoint_ref, out_ref):
    for array, ref in enumerate((state_ref, adjoint_ref)):
        for part in range(2):
            for c in range(blocks):
                rows = ref[pl.ds(c * 2 + part, gate, stride=2 * blocks), :]
                at = ((array * 2 + part) * blocks + c) * TILE
                out_ref[:, pl.ds(at, TILE), :] = rows.reshape(gate // TILE, TILE, gate)


def last_input(x_ref, array, gate, blocks):
    tiles = gate // TILE // blocks
    columns = []
    for a1 in range(blocks):
        parts = [
            x_ref[pl.ds(a1 * tiles, tiles), pl.ds((array * 2 + part) * blocks * TILE, blocks * TILE), :].reshape(gate, gate)
            for part in range(2)
        ]
        columns.append(jnp.concatenate(parts, axis=0))
    return jnp.concatenate(columns, axis=1)


def middle_input(x, gate, blocks):
    rows = []
    for a1 in range(blocks):
        columns = x[:, a1 * gate : (a1 + 1) * gate]
        rows.append(jnp.concatenate([columns[:gate], columns[gate:]], axis=1))
    return jnp.concatenate(rows, axis=0)


def first_input(x, gate, blocks):
    x = x.reshape(gate // TILE, blocks, TILE, 2 * gate)
    columns = []
    for c in range(blocks):
        rows = x[:, c].reshape(gate, 2 * gate)
        columns.append(jnp.concatenate([rows[:, :gate], rows[:, gate:]], axis=0))
    return jnp.concatenate(columns, axis=1)


def undo_body(gate, blocks, leave, x_ref, gates_ref, *out_refs):
    for array in range(2):
        x = left(gates_ref[2], last_input(x_ref, array, gate, blocks))
        x = right(middle_input(x, gate, blocks), gates_ref[1])
        x = left(gates_ref[0], first_input(x, gate, blocks))
        for part in range(2):
            for c in range(blocks):
                rows = x[part * gate : (part + 1) * gate, c * gate : (c + 1) * gate]
                if leave:
                    out_refs[array][pl.ds(c * 2 + part, gate, stride=2 * blocks), :] = rows
                else:
                    at = ((array * 2 + part) * blocks + c) * TILE
                    out_refs[0][:, pl.ds(at, TILE), :] = rows.reshape(gate // TILE, TILE, gate)


def pair(x, gate):
    real = x[:gate, :gate] + x[gate:, gate:]
    imag = x[gate:, :gate] - x[:gate, gate:]
    return real, imag


def gradient_body(gate, blocks, factor, x_ref, gates_ref, bit_ref, out_ref, all_ref):
    adjoint = last_input(x_ref, 1, gate, blocks)
    state = left(gates_ref[2], last_input(x_ref, 0, gate, blocks))
    permutation = order(gate, blocks)
    last = pair(contract(halves(adjoint), halves(state), ((1,), (1,))), gate)
    last = [exact(exact(permutation, u, ((1,), (0,))), permutation, ((1,), (1,))) for u in last]
    adjoint = middle_input(left(gates_ref[2], adjoint), gate, blocks)
    state = right(middle_input(state, gate, blocks), gates_ref[1])
    middle = pair(contract(halves(adjoint), halves(state), ((0,), (0,))), gate)
    adjoint = first_input(right(adjoint, gates_ref[1]), gate, blocks)
    state = left(gates_ref[0], first_input(state, gate, blocks))
    first = pair(contract(halves(adjoint), halves(state), ((1,), (1,))), gate)
    for position, grads in enumerate((first, middle, last)):
        for part in range(2):
            all_ref[pl.ds((position * 2 + part) * gate, gate), :] = factor * grads[part]
    part_out(all_ref, bit_ref[0], out_ref)


def part_out(ref, bit, out_ref):
    size = ref.shape[0] // 2
    out_ref[0] = ref[pl.ds(pl.multiple_of(bit * size, TILE), size), :]
    out_ref[1] = ref[pl.ds(pl.multiple_of((1 - bit) * size, TILE), size), :]


def add_body(kept_ref, got_ref, bit_ref, out_ref, all_ref):
    all_ref[...] = kept_ref[0] + got_ref[...]
    part_out(all_ref, bit_ref[0], out_ref)


def join_body(own_ref, got_ref, bit_ref, out_ref):
    out_ref[bit_ref[0]] = own_ref[...]
    out_ref[1 - bit_ref[0]] = got_ref[...]


def exchange(x, shards, step):
    return lax.ppermute(x, "qa", [(i, i ^ step) for i in range(shards)])


def bit_of(index, step):
    return ((index // step) % 2).astype(jnp.int32).reshape(1)


def summed(kept, shards, index):
    steps = [1 << k for k in range(shards.bit_length() - 1)]
    size = kept.shape[1]
    got = exchange(kept[1], shards, steps[0])
    shape = jax.ShapeDtypeStruct((2, size // 2, kept.shape[2]), F32)
    kept = call(
        add_body, shape, (kept, got, bit_of(index, steps[1])), 0, [VMEM, VMEM, SMEM],
        [pltpu.VMEM((size, kept.shape[2]), F32)],
    )
    total = kept[0] + exchange(kept[1], shards, steps[1])
    for step in steps[2:]:
        total = total + exchange(total, shards, step)
    for step in (steps[1], steps[0]):
        shape = jax.ShapeDtypeStruct((2, *total.shape), F32)
        joined = call(
            join_body, shape, (total, exchange(total, shards, step), bit_of(index, step)), 0, [VMEM, VMEM, SMEM]
        )
        total = joined.reshape(2 * total.shape[0], total.shape[1])
    return total


def swapped(x, shards, gate):
    tiles, rows, _ = x.shape
    groups = rows // TILE
    if shards != tiles:
        x = x.reshape(tiles, groups, TILE, gate).swapaxes(0, 1).reshape(groups, shards, gate // shards, gate).swapaxes(0, 1)
    x = lax.all_to_all(x, "qa", split_axis=0, concat_axis=0, tiled=True)
    if shards != tiles:
        x = x.swapaxes(0, 1).reshape(groups, tiles, TILE, gate).swapaxes(0, 1).reshape(tiles, rows, gate)
    return x


def on_device(state, adjoint, gates):
    rounds, _, _, _, gate = gates.shape
    local_size = state.shape[1]
    shards = lax.axis_size("qa")
    index = lax.axis_index("qa")
    blocks = local_size // (gate * gate)
    factor = 1.0 / math.sqrt(shards * local_size // gate)
    tiles = gate // TILE
    rows = blocks * gate
    flat = jax.ShapeDtypeStruct((2 * rows, gate), F32)
    tiled = jax.ShapeDtypeStruct((tiles, 4 * blocks * TILE, gate), F32)
    work = 12 * 2 * 3 * 4 * local_size * gate // 6

    matrices = call(
        functools.partial(prepare_body, rounds, gate, blocks),
        jax.ShapeDtypeStruct((rounds, 3, 2, 2 * gate, 2 * gate), BF16),
        (gates,),
        rounds * 12 * 2 * gate**3,
    )

    def entering(x):
        return x.reshape(2, rows, gate).swapaxes(0, 1).reshape(2 * rows, gate)

    def leaving(x):
        return x.reshape(rows, 2, gate).swapaxes(0, 1).reshape(2, local_size)

    x = call(functools.partial(enter_body, gate, blocks), tiled, (entering(state), entering(adjoint)), 0)
    grads = []
    for number in reversed(range(rounds)):
        x = swapped(x, shards, gate)
        matrix = matrices[number]
        parts = call(
            functools.partial(gradient_body, gate, blocks, factor),
            jax.ShapeDtypeStruct((2, 3 * gate, gate), F32),
            (x, matrix, bit_of(index, 1)),
            work,
            [VMEM, VMEM, SMEM],
            [pltpu.VMEM((6 * gate, gate), F32)],
        )
        grads.append(summed(parts, shards, index))
        x = call(
            functools.partial(undo_body, gate, blocks, number == 0),
            (flat, flat) if number == 0 else (tiled,),
            (x, matrix),
            work,
        )
        if number > 0:
            x = x[0]
    grads = jnp.stack(grads[::-1]).reshape(gates.shape)
    return leaving(x[0]), leaving(x[1]), grads


def solution(mesh):
    return jax.shard_map(
        on_device,
        mesh=mesh,
        in_specs=(P(None, ("grp", "qa")), P(None, ("grp", "qa")), P("grp", None, None, None, None)),
        out_specs=(
            P(None, ("grp", "qa")),
            P(None, ("grp", "qa")),
            P("grp", None, None, None, None),
        ),
        check_vma=False,
    )
```

profile of v0, /device:TPU:0, one launch (start us, length us, event | category | flops | bytes accessed | tf_op | source)
XLA Modules:
  0.0 178.8 jit_solution(11305483532476681885)
XLA Ops:
  3.9 7.4 %all-to-all-start = ((f32[16,128,128]{2,1,0:T(8,128)}), f32[16,128,128]{2,1,0:T(8,128)S(1)}, u32[]{:S(2)}, u32[]{:S(2)}) async-start(f32[16,128,128]{2,1,0:T(8,128)} %shard_map.58), calls=%async_computation | async-start | bytes 2097152 | tf_op jit(solution)/shard_map/all_to_all | solution.py:215
  11.3 1.5 shard_map.59
  12.8 1.4 slice_bitcast_fusion
  14.2 20.0 %all-to-all-done.x_ref = f32[16,128,128]{2,1,0:T(8,128)S(1)} async-done(((f32[16,128,128]{2,1,0:T(8,128)}), f32[16,128,128]{2,1,0:T(8,128)S(1)}, u32[]{:S(2)}, u32[]{:S(2)}) %all-to-all-start) | async-done | bytes 1048608 | tf_op jit(solution)/shard_map/all_to_all | solution.py:215
  34.2 2.6 %shard_map.60 = f32[16,128,128]{2,1,0:T(8,128)S(1)} custom-call(f32[16,128,128]{2,1,0:T(8,128)S(1)} %all-to-all-done.x_ref, bf16[3,2,256,256]{3,2,1,0:T(8,128)(2,1)S(1)} %get-tuple-element.10.gates_ref), custom_call_target="tpu_custom_call" | custom-call | flops 402653184 | bytes 2883584 | tf_op jit(solution)/shard_map/pallas_call | solution.py:21
  37.7 31.5 %all_to_all.20.x_ref = f32[16,128,128]{2,1,0:T(8,128)S(1)} all-to-all(f32[16,128,128]{2,1,0:T(8,128)S(1)} %shard_map.60), channel_id=1, replica_groups=mesh['grp'=2,'qa'=16] {'qa'}, dimensions={0} | all-to-all | bytes 2097152 | tf_op jit(solution)/shard_map/all_to_all | solution.py:215
  69.2 2.6 %shard_map.61 = f32[16,128,128]{2,1,0:T(8,128)S(1)} custom-call(f32[16,128,128]{2,1,0:T(8,128)S(1)} %all_to_all.20.x_ref, bf16[3,2,256,256]{3,2,1,0:T(8,128)(2,1)S(1)} %get-tuple-element.9.gates_ref), custom_call_target="tpu_custom_call" | custom-call | flops 402653184 | bytes 2883584 | tf_op jit(solution)/shard_map/pallas_call | solution.py:21
  71.8 29.8 %all_to_all.21.x_ref = f32[16,128,128]{2,1,0:T(8,128)S(1)} all-to-all(f32[16,128,128]{2,1,0:T(8,128)S(1)} %shard_map.61), channel_id=1, replica_groups=mesh['grp'=2,'qa'=16] {'qa'}, dimensions={0} | all-to-all | bytes 2097152 | tf_op jit(solution)/shard_map/all_to_all | solution.py:215
  101.5 2.6 %shard_map.62 = f32[16,128,128]{2,1,0:T(8,128)S(1)} custom-call(f32[16,128,128]{2,1,0:T(8,128)S(1)} %all_to_all.21.x_ref, bf16[3,2,256,256]{3,2,1,0:T(8,128)(2,1)S(1)} %copy-done.3), custom_call_target="tpu_custom_call" | custom-call | flops 402653184 | bytes 2883584 | tf_op jit(solution)/shard_map/pallas_call | solution.py:21
  105.1 5.2 %all-to-all-start.3 = ((f32[16,128,128]{2,1,0:T(8,128)}), f32[16,128,128]{2,1,0:T(8,128)S(1)}, u32[]{:S(2)}, u32[]{:S(2)}) async-start(f32[16,128,128]{2,1,0:T(8,128)} %copy-done.9), calls=%async_computation.3 | async-start | bytes 2097152 | tf_op jit(solution)/shard_map/all_to_all | solution.py:215
  110.3 1.2 copy-done.1
  112.7 3.5 %shard_map.76.kept_ref = f32[2,384,128]{2,1,0:T(8,128)S(1)} custom-call(f32[16,128,128]{2,1,0:T(8,128)S(1)} %copy-done.1, bf16[3,2,256,256]{3,2,1,0:T(8,128)(2,1)S(1)} %copy-done.8, s32[1]{0:T(128)} %bitcast.16.bit_ref), custom_call_target="tpu_custom_call" | custom-call | flops 402653184 | bytes 2228228 | tf_op jit(solution)/shard_map/pallas_call | solution.py:21
  117.1 1.6 collective-permute-done.18.got_ref
  119.6 1.8 %collective-permute-start.19 = (f32[192,128]{1,0:T(8,128)S(1)}, f32[192,128]{1,0:T(8,128)S(1)}, u32[]{:S(2)}, u32[]{:S(2)}) collective-permute-start(f32[192,128]{1,0:T(8,128)S(1)} %slice_bitcast_fusion.8), channel_id=1, source_target_pairs={{0,2},{1,3},{2,0},{3,1},{4,6},{5,7},{6,4},{7,5},{8,10},{9,11},{10,... | collective-permute-start | bytes 294920 | tf_op jit(solution)/shard_map/ppermute | solution.py:182
  122.6 3.5 %shard_map.72.kept_ref = f32[2,384,128]{2,1,0:T(8,128)S(1)} custom-call(f32[16,128,128]{2,1,0:T(8,128)S(1)} %all_to_all.20.x_ref, bf16[3,2,256,256]{3,2,1,0:T(8,128)(2,1)S(1)} %copy-done.6, s32[1]{0:T(128)} %bitcast.16.bit_ref), custom_call_target="tpu_custom_call" | custom-call | flops 402653184 | bytes 2228228 | tf_op jit(solution)/shard_map/pallas_call | solution.py:21
  127.8 1.5 collective-permute-start.13
  129.4 3.5 %shard_map.68.kept_ref = f32[2,384,128]{2,1,0:T(8,128)S(1)} custom-call(f32[16,128,128]{2,1,0:T(8,128)S(1)} %all_to_all.21.x_ref, bf16[3,2,256,256]{3,2,1,0:T(8,128)(2,1)S(1)} %copy-done.4, s32[1]{0:T(128)} %bitcast.16.bit_ref), custom_call_target="tpu_custom_call" | custom-call | flops 402653184 | bytes 2228228 | tf_op jit(solution)/shard_map/pallas_call | solution.py:21
  133.0 2.3 %collective-permute-done.13 = f32[192,128]{1,0:T(8,128)S(1)} collective-permute-done((f32[192,128]{1,0:T(8,128)S(1)}, f32[192,128]{1,0:T(8,128)S(1)}, u32[]{:S(2)}, u32[]{:S(2)}) %collective-permute-start.13) | collective-permute-done | bytes 98336 | tf_op jit(solution)/shard_map/ppermute | solution.py:182
  135.5 3.5 %shard_map.64.kept_ref = f32[2,384,128]{2,1,0:T(8,128)S(1)} custom-call(f32[16,128,128]{2,1,0:T(8,128)S(1)} %all-to-all-done.3.x_ref, bf16[3,2,256,256]{3,2,1,0:T(8,128)(2,1)S(1)} %copy-done.2, s32[1]{0:T(128)} %bitcast.16.bit_ref), custom_call_target="tpu_custom_call" | custom-call | flops 402653184 | bytes 2228228 | tf_op jit(solution)/shard_map/pallas_call | solution.py:21
  141.3 3.4 %collective-permute-done.7 = f32[192,128]{1,0:T(8,128)S(1)} collective-permute-done((f32[192,128]{1,0:T(8,128)S(1)}, f32[192,128]{1,0:T(8,128)S(1)}, u32[]{:S(2)}, u32[]{:S(2)}) %collective-permute-start.7) | collective-permute-done | bytes 98336 | tf_op jit(solution)/shard_map/ppermute | solution.py:182
  144.8 2.1 %collective-permute-start.8 = (f32[192,128]{1,0:T(8,128)S(1)}, f32[192,128]{1,0:T(8,128)S(1)}, u32[]{:S(2)}, u32[]{:S(2)}) collective-permute-start(f32[192,128]{1,0:T(8,128)S(1)} %fusion.2), channel_id=1, source_target_pairs={{0,4},{1,5},{2,6},{3,7},{4,0},{5,1},{6,2},{7,3},{8,12},{9,13},{10,... | collective-permute-start | bytes 294920 | tf_op jit(solution)/shard_map/ppermute | solution.py:182
  146.9 1.7 collective-permute-start.2
  149.7 1.9 %collective-permute-start.15 = (f32[192,128]{1,0:T(8,128)S(1)}, f32[192,128]{1,0:T(8,128)S(1)}, u32[]{:S(2)}, u32[]{:S(2)}) collective-permute-start(f32[192,128]{1,0:T(8,128)S(1)} %add.68), channel_id=1, source_target_pairs={{0,8},{1,9},{2,10},{3,11},{4,12},{5,13},{6,14},{7,15},{8,0},{9,1},... | collective-permute-start | bytes 294920 | tf_op jit(solution)/shard_map/ppermute | solution.py:182
  151.7 1.2 collective-permute-start.9
  152.9 2.1 %collective-permute-start.3 = (f32[192,128]{1,0:T(8,128)S(1)}, f32[192,128]{1,0:T(8,128)S(1)}, u32[]{:S(2)}, u32[]{:S(2)}) collective-permute-start(f32[192,128]{1,0:T(8,128)S(1)} %add.62), channel_id=1, source_target_pairs={{0,8},{1,9},{2,10},{3,11},{4,12},{5,13},{6,14},{7,15},{8,0},{9,1},... | collective-permute-start | bytes 294920 | tf_op jit(solution)/shard_map/ppermute | solution.py:182
  155.0 8.6 %collective-permute-done.21 = f32[192,128]{1,0:T(8,128)S(1)} collective-permute-done((f32[192,128]{1,0:T(8,128)S(1)}, f32[192,128]{1,0:T(8,128)S(1)}, u32[]{:S(2)}, u32[]{:S(2)}) %collective-permute-start.21) | collective-permute-done | bytes 98336 | tf_op jit(solution)/shard_map/ppermute | solution.py:182
  164.0 1.7 collective-permute-done.15
  166.1 1.2 collective-permute-done.9
  169.6 1.5 collective-permute-done.16.got_ref
  171.3 1.2 collective-permute-done.10.got_ref
  174.1 3.4 %shard_map.63 = (f32[1024,128]{1,0:T(8,128)}, f32[1024,128]{1,0:T(8,128)}) custom-call(f32[16,128,128]{2,1,0:T(8,128)S(1)} %all-to-all-done.3.x_ref, bf16[3,2,256,256]{3,2,1,0:T(8,128)(2,1)S(1)} %copy-done.2), custom_call_target="tpu_custom_call" | custom-call | flops 402653184 | bytes 2883584 | tf_op jit(solution)/shard_map/pallas_call | solution.py:21
  177.5 1.3 pad_maximum_fusion
  (92 shorter events, 19.3 us)
Async XLA Ops:
  2.7 8.6 %copy-start.10 = (f32[4,3,2,128,128]{4,3,2,1,0:T(8,128)S(1)}, f32[4,3,2,128,128]{4,3,2,1,0:T(8,128)}, u32[]{:S(2)}) copy-start(f32[4,3,2,128,128]{4,3,2,1,0:T(8,128)} %gates_ref.1) | copy-start | bytes 4718596
  3.9 30.3 %all-to-all-start = ((f32[16,128,128]{2,1,0:T(8,128)}), f32[16,128,128]{2,1,0:T(8,128)S(1)}, u32[]{:S(2)}, u32[]{:S(2)}) async-start(f32[16,128,128]{2,1,0:T(8,128)} %shard_map.58), calls=%async_computation | async-start | bytes 2097152 | tf_op jit(solution)/shard_map/all_to_all | solution.py:215
  14.2 55.0 %copy-start.5 = (bf16[3,2,256,256]{3,2,1,0:T(8,128)(2,1)}, bf16[3,2,256,256]{3,2,1,0:T(8,128)(2,1)S(1)}, u32[]{:S(2)}) copy-start(bf16[3,2,256,256]{3,2,1,0:T(8,128)(2,1)S(1)} %get-tuple-element.9.gates_ref) | copy-start | bytes 2359300
  34.2 35.0 %copy-start = (f32[16,128,128]{2,1,0:T(8,128)}, f32[16,128,128]{2,1,0:T(8,128)S(1)}, u32[]{:S(2)}) copy-start(f32[16,128,128]{2,1,0:T(8,128)S(1)} %all-to-all-done.x_ref) | copy-start | bytes 3145732
  71.8 29.8 %copy-start.3 = (bf16[3,2,256,256]{3,2,1,0:T(8,128)(2,1)S(1)}, bf16[3,2,256,256]{3,2,1,0:T(8,128)(2,1)}, u32[]{:S(2)}) copy-start(bf16[3,2,256,256]{3,2,1,0:T(8,128)(2,1)} %get-tuple-element.8.gates_ref) | copy-start | bytes 2359300
  105.1 30.3 %all-to-all-start.3 = ((f32[16,128,128]{2,1,0:T(8,128)}), f32[16,128,128]{2,1,0:T(8,128)S(1)}, u32[]{:S(2)}, u32[]{:S(2)}) async-start(f32[16,128,128]{2,1,0:T(8,128)} %copy-done.9), calls=%async_computation.3 | async-start | bytes 2097152 | tf_op jit(solution)/shard_map/all_to_all | solution.py:215
  116.9 1.8 collective-permute-start.18
  119.6 9.7 %copy-start.4 = (bf16[3,2,256,256]{3,2,1,0:T(8,128)(2,1)S(1)}, bf16[3,2,256,256]{3,2,1,0:T(8,128)(2,1)}, u32[]{:S(2)}) copy-start(bf16[3,2,256,256]{3,2,1,0:T(8,128)(2,1)} %get-tuple-element.8.gates_ref) | copy-start | bytes 2359300
  119.6 7.0 %collective-permute-start.19 = (f32[192,128]{1,0:T(8,128)S(1)}, f32[192,128]{1,0:T(8,128)S(1)}, u32[]{:S(2)}, u32[]{:S(2)}) collective-permute-start(f32[192,128]{1,0:T(8,128)S(1)} %slice_bitcast_fusion.8), channel_id=1, source_target_pairs={{0,2},{1,3},{2,0},{3,1},{4,6},{5,7},{6,4},{7,5},{8,10},{9,11},{10,... | collective-permute-start | bytes 294920 | tf_op jit(solution)/shard_map/ppermute | solution.py:182
  126.1 1.6 collective-permute-start.12
  126.7 21.9 %collective-permute-start.20 = (f32[192,128]{1,0:T(8,128)S(1)}, f32[192,128]{1,0:T(8,128)S(1)}, u32[]{:S(2)}, u32[]{:S(2)}) collective-permute-start(f32[192,128]{1,0:T(8,128)S(1)} %fusion), channel_id=1, source_target_pairs={{0,4},{1,5},{2,6},{3,7},{4,0},{5,1},{6,2},{7,3},{8,12},{9,13},{10,... | collective-permute-start | bytes 294920 | tf_op jit(solution)/shard_map/ppermute | solution.py:182
  127.8 7.6 %copy-start.2 = (bf16[3,2,256,256]{3,2,1,0:T(8,128)(2,1)S(1)}, bf16[3,2,256,256]{3,2,1,0:T(8,128)(2,1)}, u32[]{:S(2)}) copy-start(bf16[3,2,256,256]{3,2,1,0:T(8,128)(2,1)} %get-tuple-element.7.gates_ref) | copy-start | bytes 2359300
  127.8 7.5 %collective-permute-start.13 = (f32[192,128]{1,0:T(8,128)S(1)}, f32[192,128]{1,0:T(8,128)S(1)}, u32[]{:S(2)}, u32[]{:S(2)}) collective-permute-start(f32[192,128]{1,0:T(8,128)S(1)} %slice_bitcast_fusion.10), channel_id=1, source_target_pairs={{0,2},{1,3},{2,0},{3,1},{4,6},{5,7},{6,4},{7,5},{8,10},{9,11},{10,... | collective-permute-start | bytes 294920 | tf_op jit(solution)/shard_map/ppermute | solution.py:182
  132.9 2.5 %collective-permute-start.6 = (f32[384,128]{1,0:T(8,128)S(1)}, f32[384,128]{1,0:T(8,128)S(1)}, u32[]{:S(2)}, u32[]{:S(2)}) collective-permute-start(f32[384,128]{1,0:T(8,128)S(1)} %slice_bitcast_fusion.6), channel_id=1, source_target_pairs={{0,1},{1,0},{2,3},{3,2},{4,5},{5,4},{6,7},{7,6},{8,9},{9,8},{10,11... | collective-permute-start | bytes 589832 | tf_op jit(solution)/shard_map/ppermute | solution.py:182
  135.3 14.4 %collective-permute-start.14 = (f32[192,128]{1,0:T(8,128)S(1)}, f32[192,128]{1,0:T(8,128)S(1)}, u32[]{:S(2)}, u32[]{:S(2)}) collective-permute-start(f32[192,128]{1,0:T(8,128)S(1)} %fusion.1), channel_id=1, source_target_pairs={{0,4},{1,5},{2,6},{3,7},{4,0},{5,1},{6,2},{7,3},{8,12},{9,13},{10,... | collective-permute-start | bytes 294920 | tf_op jit(solution)/shard_map/ppermute | solution.py:182
  139.0 1.5 collective-permute-start
  139.1 5.7 %collective-permute-start.7 = (f32[192,128]{1,0:T(8,128)S(1)}, f32[192,128]{1,0:T(8,128)S(1)}, u32[]{:S(2)}, u32[]{:S(2)}) collective-permute-start(f32[192,128]{1,0:T(8,128)S(1)} %slice_bitcast_fusion.12), channel_id=1, source_target_pairs={{0,2},{1,3},{2,0},{3,1},{4,6},{5,7},{6,4},{7,5},{8,10},{9,11},{10,... | collective-permute-start | bytes 294920 | tf_op jit(solution)/shard_map/ppermute | solution.py:182
  140.6 6.3 %collective-permute-start.1 = (f32[192,128]{1,0:T(8,128)S(1)}, f32[192,128]{1,0:T(8,128)S(1)}, u32[]{:S(2)}, u32[]{:S(2)}) collective-permute-start(f32[192,128]{1,0:T(8,128)S(1)} %slice_bitcast_fusion.14), channel_id=1, source_target_pairs={{0,2},{1,3},{2,0},{3,1},{4,6},{5,7},{6,4},{7,5},{8,10},{9,11},{10,... | collective-permute-start | bytes 294920 | tf_op jit(solution)/shard_map/ppermute | solution.py:182
  144.8 6.9 %collective-permute-start.8 = (f32[192,128]{1,0:T(8,128)S(1)}, f32[192,128]{1,0:T(8,128)S(1)}, u32[]{:S(2)}, u32[]{:S(2)}) collective-permute-start(f32[192,128]{1,0:T(8,128)S(1)} %fusion.2), channel_id=1, source_target_pairs={{0,4},{1,5},{2,6},{3,7},{4,0},{5,1},{6,2},{7,3},{8,12},{9,13},{10,... | collective-permute-start | bytes 294920 | tf_op jit(solution)/shard_map/ppermute | solution.py:182
  146.9 6.0 %collective-permute-start.2 = (f32[192,128]{1,0:T(8,128)S(1)}, f32[192,128]{1,0:T(8,128)S(1)}, u32[]{:S(2)}, u32[]{:S(2)}) collective-permute-start(f32[192,128]{1,0:T(8,128)S(1)} %fusion.3), channel_id=1, source_target_pairs={{0,4},{1,5},{2,6},{3,7},{4,0},{5,1},{6,2},{7,3},{8,12},{9,13},{10,... | collective-permute-start | bytes 294920 | tf_op jit(solution)/shard_map/ppermute | solution.py:182
  148.6 15.1 %collective-permute-start.21 = (f32[192,128]{1,0:T(8,128)S(1)}, f32[192,128]{1,0:T(8,128)S(1)}, u32[]{:S(2)}, u32[]{:S(2)}) collective-permute-start(f32[192,128]{1,0:T(8,128)S(1)} %add.71), channel_id=1, source_target_pairs={{0,8},{1,9},{2,10},{3,11},{4,12},{5,13},{6,14},{7,15},{8,0},{9,1},... | collective-permute-start | bytes 294920 | tf_op jit(solution)/shard_map/ppermute | solution.py:182
  149.7 16.0 %collective-permute-start.15 = (f32[192,128]{1,0:T(8,128)S(1)}, f32[192,128]{1,0:T(8,128)S(1)}, u32[]{:S(2)}, u32[]{:S(2)}) collective-permute-start(f32[192,128]{1,0:T(8,128)S(1)} %add.68), channel_id=1, source_target_pairs={{0,8},{1,9},{2,10},{3,11},{4,12},{5,13},{6,14},{7,15},{8,0},{9,1},... | collective-permute-start | bytes 294920 | tf_op jit(solution)/shard_map/ppermute | solution.py:182
  151.7 15.7 %collective-permute-start.9 = (f32[192,128]{1,0:T(8,128)S(1)}, f32[192,128]{1,0:T(8,128)S(1)}, u32[]{:S(2)}, u32[]{:S(2)}) collective-permute-start(f32[192,128]{1,0:T(8,128)S(1)} %add.65), channel_id=1, source_target_pairs={{0,8},{1,9},{2,10},{3,11},{4,12},{5,13},{6,14},{7,15},{8,0},{9,1},... | collective-permute-start | bytes 294920 | tf_op jit(solution)/shard_map/ppermute | solution.py:182
  152.9 15.5 %collective-permute-start.3 = (f32[192,128]{1,0:T(8,128)S(1)}, f32[192,128]{1,0:T(8,128)S(1)}, u32[]{:S(2)}, u32[]{:S(2)}) collective-permute-start(f32[192,128]{1,0:T(8,128)S(1)} %add.62), channel_id=1, source_target_pairs={{0,8},{1,9},{2,10},{3,11},{4,12},{5,13},{6,14},{7,15},{8,0},{9,1},... | collective-permute-start | bytes 294920 | tf_op jit(solution)/shard_map/ppermute | solution.py:182
  163.6 5.9 %collective-permute-start.22 = (f32[192,128]{1,0:T(8,128)S(1)}, f32[192,128]{1,0:T(8,128)S(1)}, u32[]{:S(2)}, u32[]{:S(2)}) collective-permute-start(f32[192,128]{1,0:T(8,128)S(1)} %add.72.own_ref), channel_id=1, source_target_pairs={{0,2},{1,3},{2,0},{3,1},{4,6},{5,7},{6,4},{7,5},{8,10},{9,11},{10,... | collective-permute-start | bytes 294920 | tf_op jit(solution)/shard_map/ppermute | solution.py:182
  165.7 5.5 %collective-permute-start.16 = (f32[192,128]{1,0:T(8,128)S(1)}, f32[192,128]{1,0:T(8,128)S(1)}, u32[]{:S(2)}, u32[]{:S(2)}) collective-permute-start(f32[192,128]{1,0:T(8,128)S(1)} %add.69.own_ref), channel_id=1, source_target_pairs={{0,2},{1,3},{2,0},{3,1},{4,6},{5,7},{6,4},{7,5},{8,10},{9,11},{10,... | collective-permute-start | bytes 294920 | tf_op jit(solution)/shard_map/ppermute | solution.py:182
  167.4 5.2 %collective-permute-start.10 = (f32[192,128]{1,0:T(8,128)S(1)}, f32[192,128]{1,0:T(8,128)S(1)}, u32[]{:S(2)}, u32[]{:S(2)}) collective-permute-start(f32[192,128]{1,0:T(8,128)S(1)} %add.66.own_ref), channel_id=1, source_target_pairs={{0,2},{1,3},{2,0},{3,1},{4,6},{5,7},{6,4},{7,5},{8,10},{9,11},{10,... | collective-permute-start | bytes 294920 | tf_op jit(solution)/shard_map/ppermute | solution.py:182
  168.4 5.2 %collective-permute-start.4 = (f32[192,128]{1,0:T(8,128)S(1)}, f32[192,128]{1,0:T(8,128)S(1)}, u32[]{:S(2)}, u32[]{:S(2)}) collective-permute-start(f32[192,128]{1,0:T(8,128)S(1)} %add.63.own_ref), channel_id=1, source_target_pairs={{0,2},{1,3},{2,0},{3,1},{4,6},{5,7},{6,4},{7,5},{8,10},{9,11},{10,... | collective-permute-start | bytes 294920 | tf_op jit(solution)/shard_map/ppermute | solution.py:182
  169.6 4.1 %collective-permute-start.23 = (f32[384,128]{1,0:T(8,128)S(1)}, f32[384,128]{1,0:T(8,128)S(1)}, u32[]{:S(2)}, u32[]{:S(2)}) collective-permute-start(f32[384,128]{1,0:T(8,128)S(1)} %bitcast.74), channel_id=1, source_target_pairs={{0,1},{1,0},{2,3},{3,2},{4,5},{5,4},{6,7},{7,6},{8,9},{9,8},{10,11... | collective-permute-start | bytes 589832 | tf_op jit(solution)/shard_map/ppermute | solution.py:182
  171.2 2.5 %collective-permute-start.17 = (f32[384,128]{1,0:T(8,128)S(1)}, f32[384,128]{1,0:T(8,128)S(1)}, u32[]{:S(2)}, u32[]{:S(2)}) collective-permute-start(f32[384,128]{1,0:T(8,128)S(1)} %bitcast.76), channel_id=1, source_target_pairs={{0,1},{1,0},{2,3},{3,2},{4,5},{5,4},{6,7},{7,6},{8,9},{9,8},{10,11... | collective-permute-start | bytes 589832 | tf_op jit(solution)/shard_map/ppermute | solution.py:182
  172.5 1.5 collective-permute-start.11
  173.6 3.9 %collective-permute-start.5 = (f32[384,128]{1,0:T(8,128)S(1)}, f32[384,128]{1,0:T(8,128)S(1)}, u32[]{:S(2)}, u32[]{:S(2)}) collective-permute-start(f32[384,128]{1,0:T(8,128)S(1)} %bitcast.78), channel_id=1, source_target_pairs={{0,1},{1,0},{2,3},{3,2},{4,5},{5,4},{6,7},{7,6},{8,9},{9,8},{10,11... | collective-permute-start | bytes 589832 | tf_op jit(solution)/shard_map/ppermute | solution.py:182
  (7 other events, 7.4 us)
where the time goes:
time: 179 us
  blocking collectives  61.3 us (34%)
  waiting for transfers between devices  44.6 us (25%)
  starting transfers between devices  31.8 us (18%)
  Pallas kernels  29.1 us (16%)
  local copies, waits for them, and re-layouts  9.61 us (5%)
    all_to_all x2, blocking collectives, swapped(): x = lax.all_to_all(x, 'qa', split_axis=0, concat_axis=0, tiled=True)  61.3 us
    pallas_call x22, Pallas kernels, call(): pl.pallas_call(body, out_shape=out_shape, in_specs=in_specs or [VMEM] * l...  29.1 us
    ppermute x24, waiting for transfers between devices, exchange(): return lax.ppermute(x, 'qa', [(i, i ^ step) for i in range(shards)])  24.6 us
    all_to_all x2, waiting for transfers between devices, swapped(): x = lax.all_to_all(x, 'qa', split_axis=0, concat_axis=0, tiled=True)  20 us
    ppermute x24, starting transfers between devices, exchange(): return lax.ppermute(x, 'qa', [(i, i ^ step) for i in range(shards)])  19.2 us
    all_to_all x2, starting transfers between devices, swapped(): x = lax.all_to_all(x, 'qa', split_axis=0, concat_axis=0, tiled=True)  12.6 us
    unnamed x26, local copies, waits for them, and re-layouts  7.43 us
  transfers between devices with their start and end apart: 26, of which 14 were waited for; matrix products, arithmetic and copies ran while one was open for 1% of the time, Pallas kernels for 11%

commit v1 on v0

v1 whole, which is shorter than its diff:
```python
import functools
import math

import jax
import jax.numpy as jnp
from jax import lax
from jax.experimental import pallas as pl
from jax.experimental.pallas import tpu as pltpu
from jax.sharding import PartitionSpec as P

TILE = 8
VMEM = pl.BlockSpec(memory_space=pltpu.VMEM)
ANY = pl.BlockSpec(memory_space=pl.ANY)
SMEM = pl.BlockSpec(memory_space=pltpu.SMEM)
DEPTHS = (3, 2)
F32 = jnp.float32
BF16 = jnp.bfloat16


def call(body, out_shape, operands, flops, in_specs=None, out_spec=VMEM, scratch=(), after=(), aliases=None):
    outs = jax.tree.leaves(out_shape)
    moved = sum(math.prod(a.shape) * a.dtype.itemsize for a in (*operands, *outs))
    read = len(operands)

    def whole(*refs):
        body(*refs[:read], *refs[read + len(after) :])

    return pl.pallas_call(
        whole,
        out_shape=out_shape,
        in_specs=[*(in_specs or [VMEM] * read), *[ANY] * len(after)],
        out_specs=jax.tree.map(lambda _: out_spec, out_shape),
        scratch_shapes=scratch,
        input_output_aliases=aliases or {},
        compiler_params=pltpu.CompilerParams(vmem_limit_bytes=24 << 20),
        cost_estimate=pl.CostEstimate(flops=flops, bytes_accessed=moved, transcendentals=0),
    )(*operands, *after)


def halves(x):
    high = x.astype(BF16)
    return high, (x - high.astype(F32)).astype(BF16)


def contract(first, second, dims):
    dot = functools.partial(
        lax.dot_general, dimension_numbers=(dims, ((), ())), preferred_element_type=F32
    )
    return dot(first[0], second[0]) + (dot(first[0], second[1]) + dot(first[1], second[0]))


def left(matrix, x):
    return contract((matrix[0], matrix[1]), halves(x), ((1,), (0,)))


def right(x, matrix):
    return contract(halves(x), (matrix[0], matrix[1]), ((1,), (0,)))


def order(gate, blocks):
    rows = lax.broadcasted_iota(jnp.int32, (gate, gate), 0)
    columns = lax.broadcasted_iota(jnp.int32, (gate, gate), 1)
    inside = columns % TILE
    middle = (columns // TILE) % blocks
    tile = columns // (TILE * blocks)
    return jnp.where(rows == (tile * TILE + inside) * blocks + middle, 1.0, 0.0).astype(BF16)


def exact(first, second, dims):
    return lax.dot_general(
        first, second, (dims, ((), ())), precision=lax.Precision.HIGHEST, preferred_element_type=F32
    )


def prepare_body(rounds, gate, blocks, gates_ref, *out_refs):
    permutation = order(gate, blocks).astype(F32)
    for number in range(rounds):
        for position in range(3):
            real = gates_ref[number, position, 0]
            imag = gates_ref[number, position, 1]
            if position == 2:
                real, imag = (
                    exact(exact(permutation, u, ((0,), (0,))), permutation, ((1,), (0,))) for u in (real, imag)
                )
            if position == 1:
                quarters = ((real, -imag), (imag, real))
            else:
                real, imag = real.T, imag.T
                quarters = ((real, imag), (-imag, real))
            for i in range(2):
                for j in range(2):
                    for half, value in enumerate(halves(quarters[i][j])):
                        out_refs[number][position, half, pl.ds(i * gate, gate), pl.ds(j * gate, gate)] = value


def enter_body(gate, blocks, state_ref, adjoint_ref, out_ref, held_ref, tiles_ref, sems):
    size = 2 * blocks * TILE
    copies_in, copies_out = [], []
    for array, ref in enumerate((state_ref, adjoint_ref)):
        copies_in.append(pltpu.make_async_copy(ref, held_ref.at[array], sems.at[array]))
        at = pl.ds(array * size, size)
        copies_out.append(pltpu.make_async_copy(tiles_ref.at[:, at, :], out_ref.at[:, at, :], sems.at[2 + array]))
    for copy in copies_in:
        copy.start()
    for array in range(2):
        copies_in[array].wait()
        for part in range(2):
            for c in range(blocks):
                rows = held_ref[array, pl.ds(c * 2 + part, gate, stride=2 * blocks), :]
                at = ((array * 2 + part) * blocks + c) * TILE
                tiles_ref[:, pl.ds(at, TILE), :] = rows.reshape(gate // TILE, TILE, gate)
        copies_out[array].start()
    for copy in copies_out:
        copy.wait()


def last_input(x_ref, gate, blocks):
    tiles = gate // TILE // blocks
    size = blocks * TILE
    columns = []
    for array in range(2):
        for a1 in range(blocks):
            parts = [
                x_ref[pl.ds(a1 * tiles, tiles), pl.ds((array * 2 + part) * size, size), :].reshape(gate, gate)
                for part in range(2)
            ]
            columns.append(jnp.concatenate(parts, axis=0))
    return jnp.concatenate(columns, axis=1)


def middle_input(x, gate):
    rows = []
    for at in range(0, x.shape[1], gate):
        columns = x[:, at : at + gate]
        rows.append(jnp.concatenate([columns[:gate], columns[gate:]], axis=1))
    return jnp.concatenate(rows, axis=0)


def first_input(x, gate, blocks):
    columns = []
    for at in range(0, x.shape[0], blocks * gate):
        tiles = x[at : at + blocks * gate].reshape(gate // TILE, blocks, TILE, 2 * gate)
        for c in range(blocks):
            rows = tiles[:, c].reshape(gate, 2 * gate)
            columns.append(jnp.concatenate([rows[:, :gate], rows[:, gate:]], axis=0))
    return jnp.concatenate(columns, axis=1)


def undone(x_ref, gates_ref, gate, blocks):
    x = left(gates_ref[2], last_input(x_ref, gate, blocks))
    x = right(middle_input(x, gate), gates_ref[1])
    return left(gates_ref[0], first_input(x, gate, blocks))


def piece(x, gate, blocks, array, part, c):
    at = (array * blocks + c) * gate
    return x[part * gate : (part + 1) * gate, at : at + gate]


def undo_body(gate, blocks, x_ref, gates_ref, out_ref, tiles_ref, sems):
    x = undone(x_ref, gates_ref, gate, blocks)
    size = 2 * blocks * TILE
    copies = []
    for array in range(2):
        for part in range(2):
            for c in range(blocks):
                rows = piece(x, gate, blocks, array, part, c).reshape(gate // TILE, TILE, gate)
                tiles_ref[:, pl.ds(((array * 2 + part) * blocks + c) * TILE, TILE), :] = rows
        at = pl.ds(array * size, size)
        copies.append(pltpu.make_async_copy(tiles_ref.at[:, at, :], out_ref.at[:, at, :], sems.at[array]))
        copies[-1].start()
    for copy in copies:
        copy.wait()


def leave_body(gate, blocks, x_ref, gates_ref, state_ref, adjoint_ref, over_ref):
    x = undone(x_ref, gates_ref, gate, blocks)
    for array, ref in enumerate((state_ref, adjoint_ref)):
        for part in range(2):
            for c in range(blocks):
                ref[pl.ds(c * 2 + part, gate, stride=2 * blocks), :] = piece(x, gate, blocks, array, part, c)
    over_ref[...] = jnp.zeros_like(over_ref)


def pair(x, gate):
    real = x[:gate, :gate] + x[gate:, gate:]
    imag = x[gate:, :gate] - x[:gate, gate:]
    return real, imag


def gradient_body(gate, blocks, factor, depth, x_ref, gates_ref, bits_ref, own_ref, other_ref, all_ref):
    size = blocks * gate
    raw = last_input(x_ref, gate, blocks)
    x = left(gates_ref[2], raw)
    last = contract(halves(raw[:, size:]), halves(x[:, :size]), ((1,), (1,)))
    x = middle_input(x, gate)
    y = right(x, gates_ref[1])
    middle = contract(halves(x[size:]), halves(y[:size]), ((0,), (0,)))
    x = first_input(y, gate, blocks)
    first = contract(halves(x[:, size:]), halves(left(gates_ref[0], x[:, :size])), ((1,), (1,)))
    for position, grads in enumerate((first, middle)):
        for part, value in enumerate(pair(grads, gate)):
            all_ref[pl.ds((position * 2 + part) * gate, gate), :] = factor * value
    permutation = order(gate, blocks)
    last = halves(factor * jnp.concatenate(pair(last, gate), axis=0))
    dot = functools.partial(lax.dot_general, dimension_numbers=(((1,), (1,)), ((), ())), preferred_element_type=F32)
    last = dot(last[0], permutation) + dot(last[1], permutation)
    for part in range(2):
        for tile in range(gate // TILE // blocks):
            for c in range(blocks):
                at = part * gate + (tile * blocks + c) * TILE
                to = (4 + part) * gate + tile * TILE * blocks + c
                all_ref[pl.ds(to, TILE, stride=blocks), :] = last[at : at + TILE]
    for away, ref in enumerate((own_ref, other_ref)):
        for at, to, size in pieces(bits_ref, depth, away, all_ref.shape[0]):
            ref[pl.ds(at, size), :] = all_ref[pl.ds(to, size), :]


def pieces(bits_ref, depth, away, rows):
    size = rows >> depth
    for place in range(1 << (depth - 1)):
        at = bits_ref[0] ^ away
        for k in range(1, depth):
            at = 2 * at + (bits_ref[k] ^ (place >> (depth - 1 - k) & 1))
        yield place * size, pl.multiple_of(at * size, TILE), size


def place_body(groups, bits_ref, *refs):
    out_ref, sems = refs[-2:]
    copies = []
    for at, (rounds, depth) in enumerate(groups):
        for away in range(2):
            for start, to, size in pieces(bits_ref, depth, away, out_ref.shape[1]):
                for place, number in enumerate(rounds):
                    copies.append(
                        pltpu.make_async_copy(
                            refs[2 * at + away].at[pl.ds(start * len(rounds) + place * size, size), :],
                            out_ref.at[number, pl.ds(to, size), :],
                            sems.at[len(copies)],
                        )
                    )
    for copy in copies:
        copy.start()
    for copy in copies:
        copy.wait()


def add_body(first_ref, second_ref, out_ref):
    out_ref[...] = first_ref[...] + second_ref[...]


def add(first, second, *after):
    return call(add_body, jax.ShapeDtypeStruct(first.shape, F32), (first, second), 0, after=after)


def join_body(first_ref, second_ref, out_ref):
    size = first_ref.shape[0]
    out_ref[pl.ds(0, size), :] = first_ref[...]
    out_ref[pl.ds(size, size), :] = second_ref[...]


def join(first, second, *after):
    shape = jax.ShapeDtypeStruct((2 * first.shape[0], first.shape[1]), F32)
    return call(join_body, shape, (first, second), 0, after=after)


def exchange(x, shards, step):
    return lax.ppermute(x, "qa", [(i, i ^ step) for i in range(shards)])


def halved(total, shards, step):
    size = total.shape[0] // 2
    return total[:size] + exchange(total[size:], shards, step)


def doubled(total, shards, depth):
    for k in reversed(range(1, depth)):
        total = jnp.concatenate([total, exchange(total, shards, 1 << k)])
    return total, exchange(total, shards, 1)


def swapped(x, shards, gate):
    tiles, rows, _ = x.shape
    groups = rows // TILE
    if shards != tiles:
        x = x.reshape(tiles, groups, TILE, gate).swapaxes(0, 1).reshape(groups, shards, gate // shards, gate).swapaxes(0, 1)
    x = lax.all_to_all(x, "qa", split_axis=0, concat_axis=0, tiled=True)
    if shards != tiles:
        x = x.swapaxes(0, 1).reshape(groups, tiles, TILE, gate).swapaxes(0, 1).reshape(tiles, rows, gate)
    return x


def on_device(state, adjoint, gates):
    rounds, _, _, _, gate = gates.shape
    local_size = state.shape[1]
    shards = lax.axis_size("qa")
    index = lax.axis_index("qa")
    blocks = local_size // (gate * gate)
    factor = 1.0 / math.sqrt(shards * local_size // gate)
    tiles = gate // TILE
    rows = blocks * gate
    flat = jax.ShapeDtypeStruct((2 * rows, gate), F32)
    tiled = jax.ShapeDtypeStruct((tiles, 4 * blocks * TILE, gate), F32)
    work = 12 * 2 * 3 * 4 * local_size * gate // 6

    matrices = call(
        functools.partial(prepare_body, rounds, gate, blocks),
        [jax.ShapeDtypeStruct((3, 2, 2 * gate, 2 * gate), BF16)] * rounds,
        (gates,),
        rounds * 12 * 2 * gate**3,
    )
    bits = jnp.stack([index >> k & 1 for k in range(max(DEPTHS))]).astype(jnp.int32)

    def entering(x):
        return x.reshape(2, rows, gate).swapaxes(0, 1).reshape(2 * rows, gate)

    def leaving(x):
        return x.reshape(rows, 2, gate).swapaxes(0, 1).reshape(2, local_size)

    x = call(
        functools.partial(enter_body, gate, blocks),
        tiled,
        [pltpu.with_memory_space_constraint(entering(array), pltpu.HBM) for array in (state, adjoint)],
        0,
        [ANY, ANY],
        ANY,
        [
            pltpu.VMEM((2, 2 * rows, gate), F32),
            pltpu.VMEM(tiled.shape, F32),
            pltpu.SemaphoreType.DMA((4,)),
        ],
    )
    steps = [1 << k for k in range(shards.bit_length() - 1)]
    early_depth, late_depth = DEPTHS
    totals, left_over = [], []
    for number in reversed(range(rounds)):
        x = swapped(x, shards, gate)
        if number < rounds - 1:
            for at in range(len(totals)):
                if number == 0 or at < len(totals) - 1:
                    for step in left_over[at]:
                        totals[at] = halved(totals[at], shards, step)
                    left_over[at] = []
        own, other = call(
            functools.partial(gradient_body, gate, blocks, factor, early_depth if number > 0 else late_depth),
            [jax.ShapeDtypeStruct((3 * gate, gate), F32)] * 2,
            (x, matrices[number], bits),
            work,
            [VMEM, VMEM, SMEM],
            scratch=[pltpu.VMEM((6 * gate, gate), F32)],
            after=totals if number == 0 else (),
        )
        total = own + exchange(other, shards, steps[0])
        if number > 0:
            x = call(
                functools.partial(undo_body, gate, blocks),
                tiled,
                (x, matrices[number]),
                work,
                out_spec=ANY,
                scratch=[pltpu.VMEM(tiled.shape, F32), pltpu.SemaphoreType.DMA((2,))],
                after=totals,
            )
            totals.append(halved(total, shards, steps[1]))
            left_over.append(steps[2:early_depth])
    token = jax.ShapeDtypeStruct((TILE, gate), F32)
    state, adjoint, over = call(
        functools.partial(leave_body, gate, blocks), [flat, flat, token], (x, matrices[0]), work, after=totals
    )
    early, late = jnp.concatenate(totals), total
    for step in steps[1:late_depth]:
        late = halved(late, shards, step)
    for step in steps[early_depth:]:
        early = early + exchange(early, shards, step)
    for step in steps[late_depth:-1]:
        late = late + exchange(late, shards, step)
    late = add(late, exchange(late, shards, steps[-1]), over)
    groups = ((tuple(reversed(range(1, rounds))), early_depth), ((0,), late_depth))
    grads = call(
        functools.partial(place_body, groups),
        jax.ShapeDtypeStruct((rounds, 6 * gate, gate), F32),
        (bits, *doubled(early, shards, early_depth), *doubled(late, shards, late_depth)),
        0,
        [SMEM] + [ANY] * 4,
        ANY,
        [pltpu.SemaphoreType.DMA((rounds << early_depth,))],
    )
    return leaving(state), leaving(adjoint), grads.reshape(gates.shape)


def solution(mesh):
    return jax.shard_map(
        on_device,
        mesh=mesh,
        in_specs=(P(None, ("grp", "qa")), P(None, ("grp", "qa")), P("grp", None, None, None, None)),
        out_specs=(
            P(None, ("grp", "qa")),
            P(None, ("grp", "qa")),
            P("grp", None, None, None, None),
        ),
        check_vma=False,
    )
```

time: 179 us -> 172 us (0.961)
  blocking collectives: 61.3 us -> 0 us
  waiting for transfers between devices: 44.6 us -> 78.8 us
  starting transfers between devices: 31.8 us -> 54.2 us
  local copies, waits for them, and re-layouts: 9.61 us -> 6.63 us
    all_to_all x2 -> x0, blocking collectives: 61.3 us -> none  [swapped(): x = lax.all_to_all(x, 'qa', split_axis=0, concat_axis=0, tiled=True)]
    ppermute x24 -> x19, waiting for transfers between devices: 24.6 us -> 46.6 us  [exchange(): return lax.ppermute(x, 'qa', [(i, i ^ step) for i in range(shards)])]
    all_to_all x2 -> x4, starting transfers between devices: 12.6 us -> 27.7 us  [swapped(): x = lax.all_to_all(x, 'qa', split_axis=0, concat_axis=0, tiled=True)]
    all_to_all x2 -> x4, waiting for transfers between devices: 20 us -> 32.2 us  [swapped(): x = lax.all_to_all(x, 'qa', split_axis=0, concat_axis=0, tiled=True)]
    ppermute x24 -> x19, starting transfers between devices: 19.2 us -> 26.5 us  [exchange(): return lax.ppermute(x, 'qa', [(i, i ^ step) for i in range(shards)])]
    squeeze x9 -> x0, local copies, waits for them, and re-layouts: 2.18 us -> none  [the longest x1 1.41 us: on_device(): matrix = matrices[number]]
    pallas_call x22 -> x12, Pallas kernels: 29.1 us -> 30.7 us  [call(): pl.pallas_call(whole, out_shape=out_shape, in_specs=[*(in_specs or [VMEM]...]
    unnamed x26 -> x18, local copies, waits for them, and re-layouts: 7.43 us -> 6.58 us
  transfers between devices with their start and end apart: 26 -> 23, of which waited for: 14 -> 16; matrix products, arithmetic and copies ran while one was open for 1% -> 0% of each run, Pallas kernels for 11% -> 10%
where the time goes in v1:
time: 172 us
  waiting for transfers between devices  78.8 us (46%)
  starting transfers between devices  54.2 us (32%)
  Pallas kernels  30.7 us (18%)
  local copies, waits for them, and re-layouts  6.63 us (4%)
    ppermute x19, waiting for transfers between devices, exchange(): return lax.ppermute(x, 'qa', [(i, i ^ step) for i in range(shards)])  46.6 us
    all_to_all x4, waiting for transfers between devices, swapped(): x = lax.all_to_all(x, 'qa', split_axis=0, concat_axis=0, tiled=True)  32.2 us
    pallas_call x12, Pallas kernels, call(): pl.pallas_call(whole, out_shape=out_shape, in_specs=[*(in_specs or [VMEM]...  30.7 us
    all_to_all x4, starting transfers between devices, swapped(): x = lax.all_to_all(x, 'qa', split_axis=0, concat_axis=0, tiled=True)  27.7 us
    ppermute x19, starting transfers between devices, exchange(): return lax.ppermute(x, 'qa', [(i, i ^ step) for i in range(shards)])  26.5 us
    unnamed x18, local copies, waits for them, and re-layouts  6.58 us
  transfers between devices with their start and end apart: 23, of which 16 were waited for; matrix products, arithmetic and copies ran while one was open for 0% of the time, Pallas kernels for 10%

profile of v1, /device:TPU:0, one launch (start us, length us, event | category | flops | bytes accessed | tf_op | source)
XLA Modules:
  0.0 171.7 jit_solution(10864292393327301639)
XLA Ops:
  0.6 2.1 %shard_map.58 = f32[16,128,128]{2,1,0:T(8,128)} custom-call(f32[1024,128]{1,0:T(8,128)} %bitcast.25, f32[1024,128]{1,0:T(8,128)} %bitcast.26), custom_call_target="tpu_custom_call" | custom-call | bytes 2097152 | tf_op jit(solution)/shard_map/pallas_call | solution.py:28
  2.8 7.4 %all-to-all-start = ((f32[16,128,128]{2,1,0:T(8,128)}), f32[16,128,128]{2,1,0:T(8,128)S(1)}, u32[]{:S(2)}, u32[]{:S(2)}) async-start(f32[16,128,128]{2,1,0:T(8,128)} %shard_map.58), calls=%async_computation | async-start | bytes 2097152 | tf_op jit(solution)/shard_map/all_to_all | solution.py:287
  15.0 18.1 %all-to-all-done.refs_0_ = f32[16,128,128]{2,1,0:T(8,128)S(1)} async-done(((f32[16,128,128]{2,1,0:T(8,128)}), f32[16,128,128]{2,1,0:T(8,128)S(1)}, u32[]{:S(2)}, u32[]{:S(2)}) %all-to-all-start) | async-done | bytes 1048608 | tf_op jit(solution)/shard_map/all_to_all | solution.py:287
  33.1 3.1 %shard_map.60 = f32[16,128,128]{2,1,0:T(8,128)} custom-call(f32[16,128,128]{2,1,0:T(8,128)S(1)} %all-to-all-done.refs_0_, bf16[3,2,256,256]{3,2,1,0:T(8,128)(2,1)S(1)} %get-tuple-element.18.refs_1_), custom_call_target="tpu_custom_call" | custom-call | flops 402653184 | bytes 2883584 | tf_op jit(solution)/shard_map/pallas_call | solution.py:28
  36.2 6.9 %all-to-all-start.1 = ((f32[16,128,128]{2,1,0:T(8,128)}), f32[16,128,128]{2,1,0:T(8,128)S(1)}, u32[]{:S(2)}, u32[]{:S(2)}) async-start(f32[16,128,128]{2,1,0:T(8,128)} %shard_map.60), calls=%async_computation.1 | async-start | bytes 2097152 | tf_op jit(solution)/shard_map/all_to_all | solution.py:287
  44.3 3.2 %shard_map.61 = (f32[384,128]{1,0:T(8,128)S(1)}, f32[384,128]{1,0:T(8,128)S(1)}) custom-call(f32[16,128,128]{2,1,0:T(8,128)S(1)} %all-to-all-done.refs_0_, bf16[3,2,256,256]{3,2,1,0:T(8,128)(2,1)S(1)} %copy-done.7, s32[3]{0:T(128)S(1)} %pad_add_fusion.refs_2_.refs_0_), custom_call_target="tpu_custom_call" | custom-call | flops 402653184 | bytes 2228236 | tf_op jit(solution)/shard_map/pallas_call | solution.py:28
  49.1 2.0 %collective-permute-start.1 = (f32[192,128]{1,0:T(8,128)S(1)}, f32[192,128]{1,0:T(8,128)S(1)}, u32[]{:S(2)}, u32[]{:S(2)}) collective-permute-start(f32[192,128]{1,0:T(8,128)S(1)} %slice.57), channel_id=1, source_target_pairs={{0,2},{1,3},{2,0},{3,1},{4,6},{5,7},{6,4},{7,5},{8,10},{9,11},{10,... | collective-permute-start | bytes 294920 | tf_op jit(solution)/shard_map/ppermute | solution.py:268
  51.0 5.1 %collective-permute-done.1 = f32[192,128]{1,0:T(8,128)S(1)} collective-permute-done((f32[192,128]{1,0:T(8,128)S(1)}, f32[192,128]{1,0:T(8,128)S(1)}, u32[]{:S(2)}, u32[]{:S(2)}) %collective-permute-start.1) | collective-permute-done | bytes 98336 | tf_op jit(solution)/shard_map/ppermute | solution.py:268
  56.1 9.9 %all-to-all-done.1.refs_0_ = f32[16,128,128]{2,1,0:T(8,128)S(1)} async-done(((f32[16,128,128]{2,1,0:T(8,128)}), f32[16,128,128]{2,1,0:T(8,128)S(1)}, u32[]{:S(2)}, u32[]{:S(2)}) %all-to-all-start.1) | async-done | bytes 1048608 | tf_op jit(solution)/shard_map/all_to_all | solution.py:287
  66.0 3.1 %shard_map.62 = f32[16,128,128]{2,1,0:T(8,128)} custom-call(f32[16,128,128]{2,1,0:T(8,128)S(1)} %all-to-all-done.1.refs_0_, bf16[3,2,256,256]{3,2,1,0:T(8,128)(2,1)S(1)} %copy-done.4, f32[192,128]{1,0:T(8,128)S(1)} %slice_add_fusion.3.refs_2_), custom_call_target="tpu_custom_call" | custom-call | flops 402653184 | bytes 2883584 | tf_op jit(solution)/shard_map/pallas_call | solution.py:28
  69.1 6.9 %all-to-all-start.2 = ((f32[16,128,128]{2,1,0:T(8,128)}), f32[16,128,128]{2,1,0:T(8,128)S(1)}, u32[]{:S(2)}, u32[]{:S(2)}) async-start(f32[16,128,128]{2,1,0:T(8,128)} %shard_map.62), calls=%async_computation.2 | async-start | bytes 2097152 | tf_op jit(solution)/shard_map/all_to_all | solution.py:287
  77.1 3.2 %shard_map.63 = (f32[384,128]{1,0:T(8,128)S(1)}, f32[384,128]{1,0:T(8,128)S(1)}) custom-call(f32[16,128,128]{2,1,0:T(8,128)S(1)} %all-to-all-done.1.refs_0_, bf16[3,2,256,256]{3,2,1,0:T(8,128)(2,1)S(1)} %copy-done.5, s32[3]{0:T(128)S(1)} %pad_add_fusion.refs_2_.refs_0_), custom_call_target="tpu_custom_call" | custom-call | flops 402653184 | bytes 2228236 | tf_op jit(solution)/shard_map/pallas_call | solution.py:28
  84.1 11.0 %collective-permute-done.2 = f32[96,128]{1,0:T(8,128)S(1)} collective-permute-done((f32[96,128]{1,0:T(8,128)S(1)}, f32[96,128]{1,0:T(8,128)S(1)}, u32[]{:S(2)}, u32[]{:S(2)}) %collective-permute-start.2) | collective-permute-done | bytes 49184 | tf_op jit(solution)/shard_map/ppermute | solution.py:268
  95.1 4.2 %all-to-all-done.2.refs_0_ = f32[16,128,128]{2,1,0:T(8,128)S(1)} async-done(((f32[16,128,128]{2,1,0:T(8,128)}), f32[16,128,128]{2,1,0:T(8,128)S(1)}, u32[]{:S(2)}, u32[]{:S(2)}) %all-to-all-start.2) | async-done | bytes 1048608 | tf_op jit(solution)/shard_map/all_to_all | solution.py:287
  99.3 3.1 %shard_map.64 = f32[16,128,128]{2,1,0:T(8,128)} custom-call(f32[16,128,128]{2,1,0:T(8,128)S(1)} %all-to-all-done.2.refs_0_, bf16[3,2,256,256]{3,2,1,0:T(8,128)(2,1)S(1)} %copy-done.1, f32[96,128]{1,0:T(8,128)S(1)} %slice_add_fusion.6.refs_2_.refs_3_, f32[192,128]{1,0:T(8,128)S(1)} %slice_add_fusion.2.refs_3_), custom_call_target="tpu_custom_call" | custom-call | flops 402653184 | bytes 2883584 | tf_op jit(solution)/shard_map/pallas_call | solution.py:28
  102.4 6.5 %all-to-all-start.3 = ((f32[16,128,128]{2,1,0:T(8,128)}), f32[16,128,128]{2,1,0:T(8,128)S(1)}, u32[]{:S(2)}, u32[]{:S(2)}) async-start(f32[16,128,128]{2,1,0:T(8,128)} %shard_map.64), calls=%async_computation.3 | async-start | bytes 2097152 | tf_op jit(solution)/shard_map/all_to_all | solution.py:287
  110.0 3.2 %shard_map.65 = (f32[384,128]{1,0:T(8,128)S(1)}, f32[384,128]{1,0:T(8,128)S(1)}) custom-call(f32[16,128,128]{2,1,0:T(8,128)S(1)} %all-to-all-done.2.refs_0_, bf16[3,2,256,256]{3,2,1,0:T(8,128)(2,1)S(1)} %copy-done.2, s32[3]{0:T(128)S(1)} %pad_add_fusion.refs_2_.refs_0_), custom_call_target="tpu_custom_call" | custom-call | flops 402653184 | bytes 2228236 | tf_op jit(solution)/shard_map/pallas_call | solution.py:28
  114.8 2.0 %collective-permute-start.7 = (f32[192,128]{1,0:T(8,128)S(1)}, f32[192,128]{1,0:T(8,128)S(1)}, u32[]{:S(2)}, u32[]{:S(2)}) collective-permute-start(f32[192,128]{1,0:T(8,128)S(1)} %slice.65), channel_id=1, source_target_pairs={{0,2},{1,3},{2,0},{3,1},{4,6},{5,7},{6,4},{7,5},{8,10},{9,11},{10,... | collective-permute-start | bytes 294920 | tf_op jit(solution)/shard_map/ppermute | solution.py:268
  118.2 3.3 %collective-permute-done.7 = f32[192,128]{1,0:T(8,128)S(1)} collective-permute-done((f32[192,128]{1,0:T(8,128)S(1)}, f32[192,128]{1,0:T(8,128)S(1)}, u32[]{:S(2)}, u32[]{:S(2)}) %collective-permute-start.7) | collective-permute-done | bytes 98336 | tf_op jit(solution)/shard_map/ppermute | solution.py:268
  121.5 2.6 %collective-permute-start.8 = (f32[96,128]{1,0:T(8,128)S(1)}, f32[96,128]{1,0:T(8,128)S(1)}, u32[]{:S(2)}, u32[]{:S(2)}) collective-permute-start(f32[96,128]{1,0:T(8,128)S(1)} %slice.67), channel_id=1, source_target_pairs={{0,4},{1,5},{2,6},{3,7},{4,0},{5,1},{6,2},{7,3},{8,12},{9,13},{10,... | collective-permute-start | bytes 147464 | tf_op jit(solution)/shard_map/ppermute | solution.py:268
  124.1 4.1 %collective-permute-done.5 = f32[96,128]{1,0:T(8,128)S(1)} collective-permute-done((f32[96,128]{1,0:T(8,128)S(1)}, f32[96,128]{1,0:T(8,128)S(1)}, u32[]{:S(2)}, u32[]{:S(2)}) %collective-permute-start.5) | collective-permute-done | bytes 49184 | tf_op jit(solution)/shard_map/ppermute | solution.py:268
  129.1 4.5 %collective-permute-start.9 = (f32[288,128]{1,0:T(8,128)S(1)}, f32[288,128]{1,0:T(8,128)S(1)}, u32[]{:S(2)}, u32[]{:S(2)}) collective-permute-start(f32[288,128]{1,0:T(8,128)S(1)} %pad_maximum_fusion.3), channel_id=1, source_target_pairs={{0,8},{1,9},{2,10},{3,11},{4,12},{5,13},{6,14},{7,15},{8,0},{9,1},... | collective-permute-start | bytes 442376 | tf_op jit(solution)/shard_map/ppermute | solution.py:268
  133.6 3.2 %shard_map.67 = (f32[384,128]{1,0:T(8,128)S(1)}, f32[384,128]{1,0:T(8,128)S(1)}) custom-call(f32[16,128,128]{2,1,0:T(8,128)S(1)} %all-to-all-done.3.refs_0_, bf16[3,2,256,256]{3,2,1,0:T(8,128)(2,1)S(1)} %get-tuple-element.25.refs_1_, s32[3]{0:T(128)S(1)} %pad_add_fusion.refs_2_.refs_0_, f32[96,128]{1,0:T(8,128)S(1)} %slice_add_fusion.6.refs_2_.refs_3_, ...), custom_call_target="tpu_custom_call" | custom-call | flops 402653184 | bytes 2228236 | tf_op jit(solution)/shard_map/pallas_call | solution.py:28
  136.9 4.9 %collective-permute-done.9 = f32[288,128]{1,0:T(8,128)S(1)} collective-permute-done((f32[288,128]{1,0:T(8,128)S(1)}, f32[288,128]{1,0:T(8,128)S(1)}, u32[]{:S(2)}, u32[]{:S(2)}) %collective-permute-start.9) | collective-permute-done | bytes 147488 | tf_op jit(solution)/shard_map/ppermute | solution.py:268
  142.4 2.0 %collective-permute-start.14 = (f32[192,128]{1,0:T(8,128)S(1)}, f32[192,128]{1,0:T(8,128)S(1)}, u32[]{:S(2)}, u32[]{:S(2)}) collective-permute-start(f32[192,128]{1,0:T(8,128)S(1)} %slice.69), channel_id=1, source_target_pairs={{0,2},{1,3},{2,0},{3,1},{4,6},{5,7},{6,4},{7,5},{8,10},{9,11},{10,... | collective-permute-start | bytes 294920 | tf_op jit(solution)/shard_map/ppermute | solution.py:268
  144.4 2.8 %collective-permute-done.10 = f32[288,128]{1,0:T(8,128)S(1)} collective-permute-done((f32[288,128]{1,0:T(8,128)S(1)}, f32[288,128]{1,0:T(8,128)S(1)}, u32[]{:S(2)}, u32[]{:S(2)}) %collective-permute-start.10) | collective-permute-done | bytes 147488 | tf_op jit(solution)/shard_map/ppermute | solution.py:268
  150.2 4.7 %collective-permute-done.11 = f32[576,128]{1,0:T(8,128)S(1)} collective-permute-done((f32[576,128]{1,0:T(8,128)S(1)}, f32[576,128]{1,0:T(8,128)S(1)}, u32[]{:S(2)}, u32[]{:S(2)}) %collective-permute-start.11) | collective-permute-done | bytes 294944 | tf_op jit(solution)/shard_map/ppermute | solution.py:268
  155.1 2.1 %collective-permute-start.16 = (f32[192,128]{1,0:T(8,128)S(1)}, f32[192,128]{1,0:T(8,128)S(1)}, u32[]{:S(2)}, u32[]{:S(2)}) collective-permute-start(f32[192,128]{1,0:T(8,128)S(1)} %add.51.refs_0_), channel_id=1, source_target_pairs={{0,8},{1,9},{2,10},{3,11},{4,12},{5,13},{6,14},{7,15},{8,0},{9,1},... | collective-permute-start | bytes 294920 | tf_op jit(solution)/shard_map/ppermute | solution.py:268
  157.3 3.0 %shard_map.66 = (f32[1024,128]{1,0:T(8,128)}, f32[1024,128]{1,0:T(8,128)}, f32[8,128]{1,0:T(8,128)S(1)}) custom-call(f32[16,128,128]{2,1,0:T(8,128)S(1)} %all-to-all-done.3.refs_0_, bf16[3,2,256,256]{3,2,1,0:T(8,128)(2,1)S(1)} %get-tuple-element.25.refs_1_, f32[96,128]{1,0:T(8,128)S(1)} %slice_add_fusion.6.refs_2_.refs_3_, ...), custom_call_target="tpu_custom_call" | custom-call | flops 402653184 | bytes 2887680 | tf_op jit(solution)/shard_map/pallas_call | solution.py:28
  160.3 3.1 %collective-permute-done.16.refs_1_ = f32[192,128]{1,0:T(8,128)S(1)} collective-permute-done((f32[192,128]{1,0:T(8,128)S(1)}, f32[192,128]{1,0:T(8,128)S(1)}, u32[]{:S(2)}, u32[]{:S(2)}) %collective-permute-start.16) | collective-permute-done | bytes 98336 | tf_op jit(solution)/shard_map/ppermute | solution.py:268
  165.0 3.1 %collective-permute-done.17 = f32[192,128]{1,0:T(8,128)S(1)} collective-permute-done((f32[192,128]{1,0:T(8,128)S(1)}, f32[192,128]{1,0:T(8,128)S(1)}, u32[]{:S(2)}, u32[]{:S(2)}) %collective-permute-start.17) | collective-permute-done | bytes 98336 | tf_op jit(solution)/shard_map/ppermute | solution.py:268
  169.6 1.9 %shard_map.69 = f32[4,768,128]{2,1,0:T(8,128)} custom-call(s32[3]{0:T(128)S(1)} %pad_add_fusion.refs_2_.refs_0_, f32[1152,128]{1,0:T(8,128)S(1)} %pad_maximum_fusion.refs_1_, f32[1152,128]{1,0:T(8,128)S(1)} %collective-permute-done.12.refs_2_, f32[384,128]{1,0:T(8,128)S(1)} %pad_maximum_fusion.2.refs_3_, f32[384,128]{1,0:T(8,128)S(1)} %collective-permute-done.18.refs_4_), custom_call_target="tpu_custom_call" | custom-call | bytes 3145740 | tf_op jit(solution)/shard_map/pallas_call | solution.py:28
  (69 shorter events, 24.4 us)
Async XLA Ops:
  2.8 30.3 %all-to-all-start = ((f32[16,128,128]{2,1,0:T(8,128)}), f32[16,128,128]{2,1,0:T(8,128)S(1)}, u32[]{:S(2)}, u32[]{:S(2)}) async-start(f32[16,128,128]{2,1,0:T(8,128)} %shard_map.58), calls=%async_computation | async-start | bytes 2097152 | tf_op jit(solution)/shard_map/all_to_all | solution.py:287
  10.2 1.4 copy-start.8
  13.2 0.9 copy-start
  14.1 0.9 copy-start.3
  15.0 21.2 %copy-start.6 = (bf16[3,2,256,256]{3,2,1,0:T(8,128)(2,1)}, bf16[3,2,256,256]{3,2,1,0:T(8,128)(2,1)S(1)}, u32[]{:S(2)}) copy-start(bf16[3,2,256,256]{3,2,1,0:T(8,128)(2,1)S(1)} %get-tuple-element.18.refs_1_) | copy-start | bytes 2359300
  36.2 29.8 %all-to-all-start.1 = ((f32[16,128,128]{2,1,0:T(8,128)}), f32[16,128,128]{2,1,0:T(8,128)S(1)}, u32[]{:S(2)}, u32[]{:S(2)}) async-start(f32[16,128,128]{2,1,0:T(8,128)} %shard_map.60), calls=%async_computation.1 | async-start | bytes 2097152 | tf_op jit(solution)/shard_map/all_to_all | solution.py:287
  43.2 1.1 copy-start.7
  47.5 18.5 %copy-start.4 = (bf16[3,2,256,256]{3,2,1,0:T(8,128)(2,1)S(1)}, bf16[3,2,256,256]{3,2,1,0:T(8,128)(2,1)}, u32[]{:S(2)}) copy-start(bf16[3,2,256,256]{3,2,1,0:T(8,128)(2,1)} %copy-done.3) | copy-start | bytes 2359300
  47.5 1.5 collective-permute-start
  49.1 7.0 %collective-permute-start.1 = (f32[192,128]{1,0:T(8,128)S(1)}, f32[192,128]{1,0:T(8,128)S(1)}, u32[]{:S(2)}, u32[]{:S(2)}) collective-permute-start(f32[192,128]{1,0:T(8,128)S(1)} %slice.57), channel_id=1, source_target_pairs={{0,2},{1,3},{2,0},{3,1},{4,6},{5,7},{6,4},{7,5},{8,10},{9,11},{10,... | collective-permute-start | bytes 294920 | tf_op jit(solution)/shard_map/ppermute | solution.py:268
  69.1 30.2 %all-to-all-start.2 = ((f32[16,128,128]{2,1,0:T(8,128)}), f32[16,128,128]{2,1,0:T(8,128)S(1)}, u32[]{:S(2)}, u32[]{:S(2)}) async-start(f32[16,128,128]{2,1,0:T(8,128)} %shard_map.62), calls=%async_computation.2 | async-start | bytes 2097152 | tf_op jit(solution)/shard_map/all_to_all | solution.py:287
  76.0 1.1 copy-start.5
  80.3 19.0 %copy-start.1 = (bf16[3,2,256,256]{3,2,1,0:T(8,128)(2,1)S(1)}, bf16[3,2,256,256]{3,2,1,0:T(8,128)(2,1)}, u32[]{:S(2)}) copy-start(bf16[3,2,256,256]{3,2,1,0:T(8,128)(2,1)} %copy-done) | copy-start | bytes 2359300
  80.3 2.2 %collective-permute-start.3 = (f32[384,128]{1,0:T(8,128)S(1)}, f32[384,128]{1,0:T(8,128)S(1)}, u32[]{:S(2)}, u32[]{:S(2)}) collective-permute-start(f32[384,128]{1,0:T(8,128)S(1)} %get-tuple-element.24), channel_id=1, source_target_pairs={{0,1},{1,0},{2,3},{3,2},{4,5},{5,4},{6,7},{7,6},{8,9},{9,8},{10,11... | collective-permute-start | bytes 589832 | tf_op jit(solution)/shard_map/ppermute | solution.py:268
  80.8 14.3 %collective-permute-start.2 = (f32[96,128]{1,0:T(8,128)S(1)}, f32[96,128]{1,0:T(8,128)S(1)}, u32[]{:S(2)}, u32[]{:S(2)}) collective-permute-start(f32[96,128]{1,0:T(8,128)S(1)} %slice.59), channel_id=1, source_target_pairs={{0,4},{1,5},{2,6},{3,7},{4,0},{5,1},{6,2},{7,3},{8,12},{9,13},{10,... | collective-permute-start | bytes 147464 | tf_op jit(solution)/shard_map/ppermute | solution.py:268
  82.5 12.6 %collective-permute-start.4 = (f32[192,128]{1,0:T(8,128)S(1)}, f32[192,128]{1,0:T(8,128)S(1)}, u32[]{:S(2)}, u32[]{:S(2)}) collective-permute-start(f32[192,128]{1,0:T(8,128)S(1)} %slice.61), channel_id=1, source_target_pairs={{0,2},{1,3},{2,0},{3,1},{4,6},{5,7},{6,4},{7,5},{8,10},{9,11},{10,... | collective-permute-start | bytes 294920 | tf_op jit(solution)/shard_map/ppermute | solution.py:268
  102.4 31.2 %all-to-all-start.3 = ((f32[16,128,128]{2,1,0:T(8,128)}), f32[16,128,128]{2,1,0:T(8,128)S(1)}, u32[]{:S(2)}, u32[]{:S(2)}) async-start(f32[16,128,128]{2,1,0:T(8,128)} %shard_map.64), calls=%async_computation.3 | async-start | bytes 2097152 | tf_op jit(solution)/shard_map/all_to_all | solution.py:287
  108.9 1.1 copy-start.2
  113.2 1.5 collective-permute-start.6
  114.8 6.7 %collective-permute-start.7 = (f32[192,128]{1,0:T(8,128)S(1)}, f32[192,128]{1,0:T(8,128)S(1)}, u32[]{:S(2)}, u32[]{:S(2)}) collective-permute-start(f32[192,128]{1,0:T(8,128)S(1)} %slice.65), channel_id=1, source_target_pairs={{0,2},{1,3},{2,0},{3,1},{4,6},{5,7},{6,4},{7,5},{8,10},{9,11},{10,... | collective-permute-start | bytes 294920 | tf_op jit(solution)/shard_map/ppermute | solution.py:268
  116.8 11.4 %collective-permute-start.5 = (f32[96,128]{1,0:T(8,128)S(1)}, f32[96,128]{1,0:T(8,128)S(1)}, u32[]{:S(2)}, u32[]{:S(2)}) collective-permute-start(f32[96,128]{1,0:T(8,128)S(1)} %slice.63), channel_id=1, source_target_pairs={{0,4},{1,5},{2,6},{3,7},{4,0},{5,1},{6,2},{7,3},{8,12},{9,13},{10,... | collective-permute-start | bytes 147464 | tf_op jit(solution)/shard_map/ppermute | solution.py:268
  121.5 7.5 %collective-permute-start.8 = (f32[96,128]{1,0:T(8,128)S(1)}, f32[96,128]{1,0:T(8,128)S(1)}, u32[]{:S(2)}, u32[]{:S(2)}) collective-permute-start(f32[96,128]{1,0:T(8,128)S(1)} %slice.67), channel_id=1, source_target_pairs={{0,4},{1,5},{2,6},{3,7},{4,0},{5,1},{6,2},{7,3},{8,12},{9,13},{10,... | collective-permute-start | bytes 147464 | tf_op jit(solution)/shard_map/ppermute | solution.py:268
  129.1 12.7 %collective-permute-start.9 = (f32[288,128]{1,0:T(8,128)S(1)}, f32[288,128]{1,0:T(8,128)S(1)}, u32[]{:S(2)}, u32[]{:S(2)}) collective-permute-start(f32[288,128]{1,0:T(8,128)S(1)} %pad_maximum_fusion.3), channel_id=1, source_target_pairs={{0,8},{1,9},{2,10},{3,11},{4,12},{5,13},{6,14},{7,15},{8,0},{9,1},... | collective-permute-start | bytes 442376 | tf_op jit(solution)/shard_map/ppermute | solution.py:268
  136.8 5.5 %collective-permute-start.13 = (f32[384,128]{1,0:T(8,128)S(1)}, f32[384,128]{1,0:T(8,128)S(1)}, u32[]{:S(2)}, u32[]{:S(2)}) collective-permute-start(f32[384,128]{1,0:T(8,128)S(1)} %get-tuple-element.31), channel_id=1, source_target_pairs={{0,1},{1,0},{2,3},{3,2},{4,5},{5,4},{6,7},{7,6},{8,9},{9,8},{10,11... | collective-permute-start | bytes 589832 | tf_op jit(solution)/shard_map/ppermute | solution.py:268
  141.8 5.5 %collective-permute-start.10 = (f32[288,128]{1,0:T(8,128)S(1)}, f32[288,128]{1,0:T(8,128)S(1)}, u32[]{:S(2)}, u32[]{:S(2)}) collective-permute-start(f32[288,128]{1,0:T(8,128)S(1)} %fusion), channel_id=1, source_target_pairs={{0,4},{1,5},{2,6},{3,7},{4,0},{5,1},{6,2},{7,3},{8,12},{9,13},{10,... | collective-permute-start | bytes 442376 | tf_op jit(solution)/shard_map/ppermute | solution.py:268
  142.4 6.5 %collective-permute-start.14 = (f32[192,128]{1,0:T(8,128)S(1)}, f32[192,128]{1,0:T(8,128)S(1)}, u32[]{:S(2)}, u32[]{:S(2)}) collective-permute-start(f32[192,128]{1,0:T(8,128)S(1)} %slice.69), channel_id=1, source_target_pairs={{0,2},{1,3},{2,0},{3,1},{4,6},{5,7},{6,4},{7,5},{8,10},{9,11},{10,... | collective-permute-start | bytes 294920 | tf_op jit(solution)/shard_map/ppermute | solution.py:268
  147.3 7.7 %collective-permute-start.11 = (f32[576,128]{1,0:T(8,128)S(1)}, f32[576,128]{1,0:T(8,128)S(1)}, u32[]{:S(2)}, u32[]{:S(2)}) collective-permute-start(f32[576,128]{1,0:T(8,128)S(1)} %pad_maximum_fusion.1), channel_id=1, source_target_pairs={{0,2},{1,3},{2,0},{3,1},{4,6},{5,7},{6,4},{7,5},{8,10},{9,11},{10,... | collective-permute-start | bytes 884744 | tf_op jit(solution)/shard_map/ppermute | solution.py:268
  148.8 6.3 %collective-permute-start.15 = (f32[192,128]{1,0:T(8,128)S(1)}, f32[192,128]{1,0:T(8,128)S(1)}, u32[]{:S(2)}, u32[]{:S(2)}) collective-permute-start(f32[192,128]{1,0:T(8,128)S(1)} %slice_add_fusion), channel_id=1, source_target_pairs={{0,4},{1,5},{2,6},{3,7},{4,0},{5,1},{6,2},{7,3},{8,12},{9,13},{10,... | collective-permute-start | bytes 294920 | tf_op jit(solution)/shard_map/ppermute | solution.py:268
  155.0 13.2 %collective-permute-start.12 = (f32[1152,128]{1,0:T(8,128)S(1)}, f32[1152,128]{1,0:T(8,128)S(1)}, u32[]{:S(2)}, u32[]{:S(2)}) collective-permute-start(f32[1152,128]{1,0:T(8,128)S(1)} %pad_maximum_fusion.refs_1_), channel_id=1, source_target_pairs={{0,1},{1,0},{2,3},{3,2},{4,5},{5,4},{6,7},{7,6},{8,9},{9,8},{10,11... | collective-permute-start | bytes 1769480 | tf_op jit(solution)/shard_map/ppermute | solution.py:268
  155.1 8.3 %collective-permute-start.16 = (f32[192,128]{1,0:T(8,128)S(1)}, f32[192,128]{1,0:T(8,128)S(1)}, u32[]{:S(2)}, u32[]{:S(2)}) collective-permute-start(f32[192,128]{1,0:T(8,128)S(1)} %add.51.refs_0_), channel_id=1, source_target_pairs={{0,8},{1,9},{2,10},{3,11},{4,12},{5,13},{6,14},{7,15},{8,0},{9,1},... | collective-permute-start | bytes 294920 | tf_op jit(solution)/shard_map/ppermute | solution.py:268
  163.4 4.7 %collective-permute-start.17 = (f32[192,128]{1,0:T(8,128)S(1)}, f32[192,128]{1,0:T(8,128)S(1)}, u32[]{:S(2)}, u32[]{:S(2)}) collective-permute-start(f32[192,128]{1,0:T(8,128)S(1)} %shard_map.68), channel_id=1, source_target_pairs={{0,2},{1,3},{2,0},{3,1},{4,6},{5,7},{6,4},{7,5},{8,10},{9,11},{10,... | collective-permute-start | bytes 294920 | tf_op jit(solution)/shard_map/ppermute | solution.py:268
  168.1 1.5 collective-permute-start.18

commit v2 on v1

--- a/solution.py
+++ b/solution.py
@@ -301,7 +301,7 @@
     rows = blocks * gate
     flat = jax.ShapeDtypeStruct((2 * rows, gate), F32)
     tiled = jax.ShapeDtypeStruct((tiles, 4 * blocks * TILE, gate), F32)
-    work = 12 * 2 * 3 * 4 * local_size * gate // 6
+    work = 48 * local_size * gate
 
     matrices = call(
         functools.partial(prepare_body, rounds, gate, blocks),
@@ -309,7 +309,10 @@
         (gates,),
         rounds * 12 * 2 * gate**3,
     )
-    bits = jnp.stack([index >> k & 1 for k in range(max(DEPTHS))]).astype(jnp.int32)
+    steps = [1 << k for k in range(shards.bit_length() - 1)]
+    early_depth, late_depth = DEPTHS
+    stepwise = shards == 1 << len(steps) and len(steps) >= max(DEPTHS)
+    bits = jnp.stack([index >> k & 1 if stepwise else index * 0 for k in range(max(DEPTHS))]).astype(jnp.int32)
 
     def entering(x):
         return x.reshape(2, rows, gate).swapaxes(0, 1).reshape(2 * rows, gate)
@@ -330,9 +333,7 @@
             pltpu.SemaphoreType.DMA((4,)),
         ],
     )
-    steps = [1 << k for k in range(shards.bit_length() - 1)]
-    early_depth, late_depth = DEPTHS
-    totals, left_over = [], []
+    totals, left_over, plain = [], [], []
     for number in reversed(range(rounds)):
         x = swapped(x, shards, gate)
         if number < rounds - 1:
@@ -350,7 +351,10 @@
             scratch=[pltpu.VMEM((6 * gate, gate), F32)],
             after=totals if number == 0 else (),
         )
-        total = own + exchange(other, shards, steps[0])
+        if stepwise:
+            total = own + exchange(other, shards, steps[0])
+        else:
+            plain.append(lax.psum(jnp.concatenate([own, other]), "qa"))
         if number > 0:
             x = call(
                 functools.partial(undo_body, gate, blocks),
@@ -361,27 +365,36 @@
                 scratch=[pltpu.VMEM(tiled.shape, F32), pltpu.SemaphoreType.DMA((2,))],
                 after=totals,
             )
-            totals.append(halved(total, shards, steps[1]))
-            left_over.append(steps[2:early_depth])
+            if stepwise:
+                totals.append(halved(total, shards, steps[1]))
+                left_over.append(steps[2:early_depth])
     token = jax.ShapeDtypeStruct((TILE, gate), F32)
     state, adjoint, over = call(
         functools.partial(leave_body, gate, blocks), [flat, flat, token], (x, matrices[0]), work, after=totals
     )
-    early, late = jnp.concatenate(totals), total
+    if not stepwise:
+        return leaving(state), leaving(adjoint), jnp.stack(plain[::-1]).reshape(gates.shape)
+    groups = (tuple(reversed(range(2, rounds))), (1,))
+    early = []
+    for group in groups:
+        part = jnp.concatenate([totals[rounds - 1 - number] for number in group])
+        for step in steps[early_depth:]:
+            part = part + exchange(part, shards, step)
+        early.append(doubled(part, shards, early_depth))
+    late = total
     for step in steps[1:late_depth]:
         late = halved(late, shards, step)
-    for step in steps[early_depth:]:
-        early = early + exchange(early, shards, step)
     for step in steps[late_depth:-1]:
         late = late + exchange(late, shards, step)
     late = add(late, exchange(late, shards, steps[-1]), over)
-    groups = ((tuple(reversed(range(1, rounds))), early_depth), ((0,), late_depth))
+    finished = [*early, doubled(late, shards, late_depth)]
+    groups = (*((group, early_depth) for group in groups), ((0,), late_depth))
     grads = call(
         functools.partial(place_body, groups),
         jax.ShapeDtypeStruct((rounds, 6 * gate, gate), F32),
-        (bits, *doubled(early, shards, early_depth), *doubled(late, shards, late_depth)),
+        (bits, *(half for pair_of in finished for half in pair_of)),
         0,
-        [SMEM] + [ANY] * 4,
+        [SMEM] + [ANY] * (2 * len(groups)),
         ANY,
         [pltpu.SemaphoreType.DMA((rounds << early_depth,))],
     )

time: 172 us -> 169 us (0.983)
  waiting for transfers between devices: 78.8 us -> 74 us
    ppermute x19 -> x23, waiting for transfers between devices: 46.6 us -> 41.8 us  [exchange(): return lax.ppermute(x, 'qa', [(i, i ^ step) for i in range(shards)])]
    ppermute x19 -> x23, starting transfers between devices: 26.5 us -> 27.7 us  [exchange(): return lax.ppermute(x, 'qa', [(i, i ^ step) for i in range(shards)])]
  transfers between devices with their start and end apart: 23 -> 27, of which waited for: 16 -> 15; matrix products, arithmetic and copies ran while one was open for 0% -> 0% of each run, Pallas kernels for 10% -> 10%
where the time goes in v2:
time: 169 us; the launch traced here: 168 us
  waiting for transfers between devices  74 us (44%)
  starting transfers between devices  55.4 us (33%)
  Pallas kernels  30.7 us (18%)
  local copies, waits for them, and re-layouts  6.62 us (4%)
    ppermute x23, waiting for transfers between devices, exchange(): return lax.ppermute(x, 'qa', [(i, i ^ step) for i in range(shards)])  41.8 us
    all_to_all x4, waiting for transfers between devices, swapped(): x = lax.all_to_all(x, 'qa', split_axis=0, concat_axis=0, tiled=True)  32.2 us
    pallas_call x12, Pallas kernels, call(): pl.pallas_call(whole, out_shape=out_shape, in_specs=[*(in_specs or [VMEM]...  30.7 us
    ppermute x23, starting transfers between devices, exchange(): return lax.ppermute(x, 'qa', [(i, i ^ step) for i in range(shards)])  27.7 us
    all_to_all x4, starting transfers between devices, swapped(): x = lax.all_to_all(x, 'qa', split_axis=0, concat_axis=0, tiled=True)  27.7 us
    unnamed x18, local copies, waits for them, and re-layouts  6.57 us
  transfers between devices with their start and end apart: 27, of which 15 were waited for; matrix products, arithmetic and copies ran while one was open for 0% of the time, Pallas kernels for 10%

profile of v2, /device:TPU:0, one launch (start us, length us, event | category | flops | bytes accessed | tf_op | source)
XLA Modules:
  0.0 168.2 jit_solution(12813765428088724627)
XLA Ops:
  0.6 2.1 %shard_map.58 = f32[16,128,128]{2,1,0:T(8,128)} custom-call(f32[1024,128]{1,0:T(8,128)} %bitcast.25, f32[1024,128]{1,0:T(8,128)} %bitcast.26), custom_call_target="tpu_custom_call" | custom-call | bytes 2097152 | tf_op jit(solution)/shard_map/pallas_call | solution.py:28
  2.8 7.4 %all-to-all-start = ((f32[16,128,128]{2,1,0:T(8,128)}), f32[16,128,128]{2,1,0:T(8,128)S(1)}, u32[]{:S(2)}, u32[]{:S(2)}) async-start(f32[16,128,128]{2,1,0:T(8,128)} %shard_map.58), calls=%async_computation | async-start | bytes 2097152 | tf_op jit(solution)/shard_map/all_to_all | solution.py:287
  15.0 18.1 %all-to-all-done.refs_0_ = f32[16,128,128]{2,1,0:T(8,128)S(1)} async-done(((f32[16,128,128]{2,1,0:T(8,128)}), f32[16,128,128]{2,1,0:T(8,128)S(1)}, u32[]{:S(2)}, u32[]{:S(2)}) %all-to-all-start) | async-done | bytes 1048608 | tf_op jit(solution)/shard_map/all_to_all | solution.py:287
  33.1 3.1 %shard_map.60 = f32[16,128,128]{2,1,0:T(8,128)} custom-call(f32[16,128,128]{2,1,0:T(8,128)S(1)} %all-to-all-done.refs_0_, bf16[3,2,256,256]{3,2,1,0:T(8,128)(2,1)S(1)} %get-tuple-element.18.refs_1_), custom_call_target="tpu_custom_call" | custom-call | flops 402653184 | bytes 2883584 | tf_op jit(solution)/shard_map/pallas_call | solution.py:28
  36.2 6.9 %all-to-all-start.1 = ((f32[16,128,128]{2,1,0:T(8,128)}), f32[16,128,128]{2,1,0:T(8,128)S(1)}, u32[]{:S(2)}, u32[]{:S(2)}) async-start(f32[16,128,128]{2,1,0:T(8,128)} %shard_map.60), calls=%async_computation.1 | async-start | bytes 2097152 | tf_op jit(solution)/shard_map/all_to_all | solution.py:287
  44.3 3.2 %shard_map.61 = (f32[384,128]{1,0:T(8,128)S(1)}, f32[384,128]{1,0:T(8,128)S(1)}) custom-call(f32[16,128,128]{2,1,0:T(8,128)S(1)} %all-to-all-done.refs_0_, bf16[3,2,256,256]{3,2,1,0:T(8,128)(2,1)S(1)} %copy-done.7, s32[3]{0:T(128)S(1)} %pad_add_fusion.refs_2_.refs_0_), custom_call_target="tpu_custom_call" | custom-call | flops 402653184 | bytes 2228236 | tf_op jit(solution)/shard_map/pallas_call | solution.py:28
  49.1 2.0 %collective-permute-start.1 = (f32[192,128]{1,0:T(8,128)S(1)}, f32[192,128]{1,0:T(8,128)S(1)}, u32[]{:S(2)}, u32[]{:S(2)}) collective-permute-start(f32[192,128]{1,0:T(8,128)S(1)} %slice.57), channel_id=1, source_target_pairs={{0,2},{1,3},{2,0},{3,1},{4,6},{5,7},{6,4},{7,5},{8,10},{9,11},{10,... | collective-permute-start | bytes 294920 | tf_op jit(solution)/shard_map/ppermute | solution.py:268
  51.0 5.1 %collective-permute-done.1 = f32[192,128]{1,0:T(8,128)S(1)} collective-permute-done((f32[192,128]{1,0:T(8,128)S(1)}, f32[192,128]{1,0:T(8,128)S(1)}, u32[]{:S(2)}, u32[]{:S(2)}) %collective-permute-start.1) | collective-permute-done | bytes 98336 | tf_op jit(solution)/shard_map/ppermute | solution.py:268
  56.1 9.9 %all-to-all-done.1.refs_0_ = f32[16,128,128]{2,1,0:T(8,128)S(1)} async-done(((f32[16,128,128]{2,1,0:T(8,128)}), f32[16,128,128]{2,1,0:T(8,128)S(1)}, u32[]{:S(2)}, u32[]{:S(2)}) %all-to-all-start.1) | async-done | bytes 1048608 | tf_op jit(solution)/shard_map/all_to_all | solution.py:287
  66.0 3.1 %shard_map.62 = f32[16,128,128]{2,1,0:T(8,128)} custom-call(f32[16,128,128]{2,1,0:T(8,128)S(1)} %all-to-all-done.1.refs_0_, bf16[3,2,256,256]{3,2,1,0:T(8,128)(2,1)S(1)} %copy-done.4, f32[192,128]{1,0:T(8,128)S(1)} %slice_add_fusion.3.refs_2_), custom_call_target="tpu_custom_call" | custom-call | flops 402653184 | bytes 2883584 | tf_op jit(solution)/shard_map/pallas_call | solution.py:28
  69.1 6.9 %all-to-all-start.2 = ((f32[16,128,128]{2,1,0:T(8,128)}), f32[16,128,128]{2,1,0:T(8,128)S(1)}, u32[]{:S(2)}, u32[]{:S(2)}) async-start(f32[16,128,128]{2,1,0:T(8,128)} %shard_map.62), calls=%async_computation.2 | async-start | bytes 2097152 | tf_op jit(solution)/shard_map/all_to_all | solution.py:287
  77.1 3.2 %shard_map.63 = (f32[384,128]{1,0:T(8,128)S(1)}, f32[384,128]{1,0:T(8,128)S(1)}) custom-call(f32[16,128,128]{2,1,0:T(8,128)S(1)} %all-to-all-done.1.refs_0_, bf16[3,2,256,256]{3,2,1,0:T(8,128)(2,1)S(1)} %copy-done.5, s32[3]{0:T(128)S(1)} %pad_add_fusion.refs_2_.refs_0_), custom_call_target="tpu_custom_call" | custom-call | flops 402653184 | bytes 2228236 | tf_op jit(solution)/shard_map/pallas_call | solution.py:28
  80.8 1.7 collective-permute-start.2
  84.1 11.0 %collective-permute-done.2 = f32[96,128]{1,0:T(8,128)S(1)} collective-permute-done((f32[96,128]{1,0:T(8,128)S(1)}, f32[96,128]{1,0:T(8,128)S(1)}, u32[]{:S(2)}, u32[]{:S(2)}) %collective-permute-start.2) | collective-permute-done | bytes 49184 | tf_op jit(solution)/shard_map/ppermute | solution.py:268
  95.1 4.2 %all-to-all-done.2.refs_0_ = f32[16,128,128]{2,1,0:T(8,128)S(1)} async-done(((f32[16,128,128]{2,1,0:T(8,128)}), f32[16,128,128]{2,1,0:T(8,128)S(1)}, u32[]{:S(2)}, u32[]{:S(2)}) %all-to-all-start.2) | async-done | bytes 1048608 | tf_op jit(solution)/shard_map/all_to_all | solution.py:287
  99.3 3.1 %shard_map.64 = f32[16,128,128]{2,1,0:T(8,128)} custom-call(f32[16,128,128]{2,1,0:T(8,128)S(1)} %all-to-all-done.2.refs_0_, bf16[3,2,256,256]{3,2,1,0:T(8,128)(2,1)S(1)} %copy-done.1, f32[96,128]{1,0:T(8,128)S(1)} %slice_add_fusion.6.refs_2_.refs_3_, f32[192,128]{1,0:T(8,128)S(1)} %slice_add_fusion.2.refs_3_), custom_call_target="tpu_custom_call" | custom-call | flops 402653184 | bytes 2883584 | tf_op jit(solution)/shard_map/pallas_call | solution.py:28
  102.4 6.5 %all-to-all-start.3 = ((f32[16,128,128]{2,1,0:T(8,128)}), f32[16,128,128]{2,1,0:T(8,128)S(1)}, u32[]{:S(2)}, u32[]{:S(2)}) async-start(f32[16,128,128]{2,1,0:T(8,128)} %shard_map.64), calls=%async_computation.3 | async-start | bytes 2097152 | tf_op jit(solution)/shard_map/all_to_all | solution.py:287
  110.0 3.2 %shard_map.65 = (f32[384,128]{1,0:T(8,128)S(1)}, f32[384,128]{1,0:T(8,128)S(1)}) custom-call(f32[16,128,128]{2,1,0:T(8,128)S(1)} %all-to-all-done.2.refs_0_, bf16[3,2,256,256]{3,2,1,0:T(8,128)(2,1)S(1)} %copy-done.2, s32[3]{0:T(128)S(1)} %pad_add_fusion.refs_2_.refs_0_), custom_call_target="tpu_custom_call" | custom-call | flops 402653184 | bytes 2228236 | tf_op jit(solution)/shard_map/pallas_call | solution.py:28
  113.7 1.7 collective-permute-start.5
  117.0 11.0 %collective-permute-done.5 = f32[96,128]{1,0:T(8,128)S(1)} collective-permute-done((f32[96,128]{1,0:T(8,128)S(1)}, f32[96,128]{1,0:T(8,128)S(1)}, u32[]{:S(2)}, u32[]{:S(2)}) %collective-permute-start.5) | collective-permute-done | bytes 49184 | tf_op jit(solution)/shard_map/ppermute | solution.py:268
  128.0 2.5 %collective-permute-start.8 = (f32[96,128]{1,0:T(8,128)S(1)}, f32[96,128]{1,0:T(8,128)S(1)}, u32[]{:S(2)}, u32[]{:S(2)}) collective-permute-start(f32[96,128]{1,0:T(8,128)S(1)} %slice.67), channel_id=1, source_target_pairs={{0,4},{1,5},{2,6},{3,7},{4,0},{5,1},{6,2},{7,3},{8,12},{9,13},{10,... | collective-permute-start | bytes 147464 | tf_op jit(solution)/shard_map/ppermute | solution.py:268
  130.6 2.1 %collective-permute-start.9 = (f32[192,128]{1,0:T(8,128)S(1)}, f32[192,128]{1,0:T(8,128)S(1)}, u32[]{:S(2)}, u32[]{:S(2)}) collective-permute-start(f32[192,128]{1,0:T(8,128)S(1)} %pad_maximum_fusion.4), channel_id=1, source_target_pairs={{0,8},{1,9},{2,10},{3,11},{4,12},{5,13},{6,14},{7,15},{8,0},{9,1},... | collective-permute-start | bytes 294920 | tf_op jit(solution)/shard_map/ppermute | solution.py:268
  133.7 3.2 %shard_map.67 = (f32[384,128]{1,0:T(8,128)S(1)}, f32[384,128]{1,0:T(8,128)S(1)}) custom-call(f32[16,128,128]{2,1,0:T(8,128)S(1)} %all-to-all-done.3.refs_0_, bf16[3,2,256,256]{3,2,1,0:T(8,128)(2,1)S(1)} %get-tuple-element.25.refs_1_, s32[3]{0:T(128)S(1)} %pad_add_fusion.refs_2_.refs_0_, f32[96,128]{1,0:T(8,128)S(1)} %slice_add_fusion.6.refs_2_.refs_3_, ...), custom_call_target="tpu_custom_call" | custom-call | flops 402653184 | bytes 2228236 | tf_op jit(solution)/shard_map/pallas_call | solution.py:28
  137.0 2.6 %collective-permute-done.9 = f32[192,128]{1,0:T(8,128)S(1)} collective-permute-done((f32[192,128]{1,0:T(8,128)S(1)}, f32[192,128]{1,0:T(8,128)S(1)}, u32[]{:S(2)}, u32[]{:S(2)}) %collective-permute-start.9) | collective-permute-done | bytes 98336 | tf_op jit(solution)/shard_map/ppermute | solution.py:268
  139.7 2.1 %collective-permute-start.13 = (f32[96,128]{1,0:T(8,128)S(1)}, f32[96,128]{1,0:T(8,128)S(1)}, u32[]{:S(2)}, u32[]{:S(2)}) collective-permute-start(f32[96,128]{1,0:T(8,128)S(1)} %slice_add_fusion.4.refs_4_.refs_5_), channel_id=1, source_target_pairs={{0,8},{1,9},{2,10},{3,11},{4,12},{5,13},{6,14},{7,15},{8,0},{9,1},... | collective-permute-start | bytes 147464 | tf_op jit(solution)/shard_map/ppermute | solution.py:268
  141.9 2.6 %collective-permute-start.18 = (f32[192,128]{1,0:T(8,128)S(1)}, f32[192,128]{1,0:T(8,128)S(1)}, u32[]{:S(2)}, u32[]{:S(2)}) collective-permute-start(f32[192,128]{1,0:T(8,128)S(1)} %slice.69), channel_id=1, source_target_pairs={{0,2},{1,3},{2,0},{3,1},{4,6},{5,7},{6,4},{7,5},{8,10},{9,11},{10,... | collective-permute-start | bytes 294920 | tf_op jit(solution)/shard_map/ppermute | solution.py:268
  146.3 2.3 %collective-permute-start.14 = (f32[96,128]{1,0:T(8,128)S(1)}, f32[96,128]{1,0:T(8,128)S(1)}, u32[]{:S(2)}, u32[]{:S(2)}) collective-permute-start(f32[96,128]{1,0:T(8,128)S(1)} %add.52), channel_id=1, source_target_pairs={{0,4},{1,5},{2,6},{3,7},{4,0},{5,1},{6,2},{7,3},{8,12},{9,13},{10,... | collective-permute-start | bytes 147464 | tf_op jit(solution)/shard_map/ppermute | solution.py:268
  148.8 2.4 %collective-permute-done.14 = f32[96,128]{1,0:T(8,128)S(1)} collective-permute-done((f32[96,128]{1,0:T(8,128)S(1)}, f32[96,128]{1,0:T(8,128)S(1)}, u32[]{:S(2)}, u32[]{:S(2)}) %collective-permute-start.14) | collective-permute-done | bytes 49184 | tf_op jit(solution)/shard_map/ppermute | solution.py:268
  153.4 1.7 %collective-permute-start.20 = (f32[192,128]{1,0:T(8,128)S(1)}, f32[192,128]{1,0:T(8,128)S(1)}, u32[]{:S(2)}, u32[]{:S(2)}) collective-permute-start(f32[192,128]{1,0:T(8,128)S(1)} %add.55.refs_0_), channel_id=1, source_target_pairs={{0,8},{1,9},{2,10},{3,11},{4,12},{5,13},{6,14},{7,15},{8,0},{9,1},... | collective-permute-start | bytes 294920 | tf_op jit(solution)/shard_map/ppermute | solution.py:268
  155.2 3.0 %shard_map.66 = (f32[1024,128]{1,0:T(8,128)}, f32[1024,128]{1,0:T(8,128)}, f32[8,128]{1,0:T(8,128)S(1)}) custom-call(f32[16,128,128]{2,1,0:T(8,128)S(1)} %all-to-all-done.3.refs_0_, bf16[3,2,256,256]{3,2,1,0:T(8,128)(2,1)S(1)} %get-tuple-element.25.refs_1_, f32[96,128]{1,0:T(8,128)S(1)} %slice_add_fusion.6.refs_2_.refs_3_, ...), custom_call_target="tpu_custom_call" | custom-call | flops 402653184 | bytes 2887680 | tf_op jit(solution)/shard_map/pallas_call | solution.py:28
  161.4 3.2 %collective-permute-done.21 = f32[192,128]{1,0:T(8,128)S(1)} collective-permute-done((f32[192,128]{1,0:T(8,128)S(1)}, f32[192,128]{1,0:T(8,128)S(1)}, u32[]{:S(2)}, u32[]{:S(2)}) %collective-permute-start.21) | collective-permute-done | bytes 98336 | tf_op jit(solution)/shard_map/ppermute | solution.py:268
  166.1 1.9 %shard_map.69 = f32[4,768,128]{2,1,0:T(8,128)} custom-call(s32[3]{0:T(128)S(1)} %pad_add_fusion.refs_2_.refs_0_, f32[768,128]{1,0:T(8,128)S(1)} %pad_maximum_fusion.refs_1_, f32[768,128]{1,0:T(8,128)S(1)} %collective-permute-done.12.refs_2_, f32[384,128]{1,0:T(8,128)S(1)} %pad_maximum_fusion.2.refs_3_, f32[384,128]{1,0:T(8,128)S(1)} %collective-permute-done.16.refs_4_, ...), custom_call_target="tpu_custom_call" | custom-call | bytes 3145740 | tf_op jit(solution)/shard_map/pallas_call | solution.py:28
  (80 shorter events, 24.1 us)
Async XLA Ops:
  2.8 30.3 %all-to-all-start = ((f32[16,128,128]{2,1,0:T(8,128)}), f32[16,128,128]{2,1,0:T(8,128)S(1)}, u32[]{:S(2)}, u32[]{:S(2)}) async-start(f32[16,128,128]{2,1,0:T(8,128)} %shard_map.58), calls=%async_computation | async-start | bytes 2097152 | tf_op jit(solution)/shard_map/all_to_all | solution.py:287
  10.2 1.4 copy-start.8
  15.0 21.2 %copy-start.6 = (bf16[3,2,256,256]{3,2,1,0:T(8,128)(2,1)}, bf16[3,2,256,256]{3,2,1,0:T(8,128)(2,1)S(1)}, u32[]{:S(2)}) copy-start(bf16[3,2,256,256]{3,2,1,0:T(8,128)(2,1)S(1)} %get-tuple-element.18.refs_1_) | copy-start | bytes 2359300
  36.2 29.8 %all-to-all-start.1 = ((f32[16,128,128]{2,1,0:T(8,128)}), f32[16,128,128]{2,1,0:T(8,128)S(1)}, u32[]{:S(2)}, u32[]{:S(2)}) async-start(f32[16,128,128]{2,1,0:T(8,128)} %shard_map.60), calls=%async_computation.1 | async-start | bytes 2097152 | tf_op jit(solution)/shard_map/all_to_all | solution.py:287
  43.2 1.1 copy-start.7
  47.5 18.5 %copy-start.4 = (bf16[3,2,256,256]{3,2,1,0:T(8,128)(2,1)S(1)}, bf16[3,2,256,256]{3,2,1,0:T(8,128)(2,1)}, u32[]{:S(2)}) copy-start(bf16[3,2,256,256]{3,2,1,0:T(8,128)(2,1)} %copy-done.3) | copy-start | bytes 2359300
  47.5 1.5 collective-permute-start
  49.1 7.0 %collective-permute-start.1 = (f32[192,128]{1,0:T(8,128)S(1)}, f32[192,128]{1,0:T(8,128)S(1)}, u32[]{:S(2)}, u32[]{:S(2)}) collective-permute-start(f32[192,128]{1,0:T(8,128)S(1)} %slice.57), channel_id=1, source_target_pairs={{0,2},{1,3},{2,0},{3,1},{4,6},{5,7},{6,4},{7,5},{8,10},{9,11},{10,... | collective-permute-start | bytes 294920 | tf_op jit(solution)/shard_map/ppermute | solution.py:268
  69.1 30.2 %all-to-all-start.2 = ((f32[16,128,128]{2,1,0:T(8,128)}), f32[16,128,128]{2,1,0:T(8,128)S(1)}, u32[]{:S(2)}, u32[]{:S(2)}) async-start(f32[16,128,128]{2,1,0:T(8,128)} %shard_map.62), calls=%async_computation.2 | async-start | bytes 2097152 | tf_op jit(solution)/shard_map/all_to_all | solution.py:287
  80.3 19.0 %copy-start.1 = (bf16[3,2,256,256]{3,2,1,0:T(8,128)(2,1)S(1)}, bf16[3,2,256,256]{3,2,1,0:T(8,128)(2,1)}, u32[]{:S(2)}) copy-start(bf16[3,2,256,256]{3,2,1,0:T(8,128)(2,1)} %copy-done) | copy-start | bytes 2359300
  80.3 2.2 %collective-permute-start.3 = (f32[384,128]{1,0:T(8,128)S(1)}, f32[384,128]{1,0:T(8,128)S(1)}, u32[]{:S(2)}, u32[]{:S(2)}) collective-permute-start(f32[384,128]{1,0:T(8,128)S(1)} %get-tuple-element.24), channel_id=1, source_target_pairs={{0,1},{1,0},{2,3},{3,2},{4,5},{5,4},{6,7},{7,6},{8,9},{9,8},{10,11... | collective-permute-start | bytes 589832 | tf_op jit(solution)/shard_map/ppermute | solution.py:268
  80.8 14.3 %collective-permute-start.2 = (f32[96,128]{1,0:T(8,128)S(1)}, f32[96,128]{1,0:T(8,128)S(1)}, u32[]{:S(2)}, u32[]{:S(2)}) collective-permute-start(f32[96,128]{1,0:T(8,128)S(1)} %slice.59), channel_id=1, source_target_pairs={{0,4},{1,5},{2,6},{3,7},{4,0},{5,1},{6,2},{7,3},{8,12},{9,13},{10,... | collective-permute-start | bytes 147464 | tf_op jit(solution)/shard_map/ppermute | solution.py:268
  82.5 12.6 %collective-permute-start.4 = (f32[192,128]{1,0:T(8,128)S(1)}, f32[192,128]{1,0:T(8,128)S(1)}, u32[]{:S(2)}, u32[]{:S(2)}) collective-permute-start(f32[192,128]{1,0:T(8,128)S(1)} %slice.61), channel_id=1, source_target_pairs={{0,2},{1,3},{2,0},{3,1},{4,6},{5,7},{6,4},{7,5},{8,10},{9,11},{10,... | collective-permute-start | bytes 294920 | tf_op jit(solution)/shard_map/ppermute | solution.py:268
  102.4 31.3 %all-to-all-start.3 = ((f32[16,128,128]{2,1,0:T(8,128)}), f32[16,128,128]{2,1,0:T(8,128)S(1)}, u32[]{:S(2)}, u32[]{:S(2)}) async-start(f32[16,128,128]{2,1,0:T(8,128)} %shard_map.64), calls=%async_computation.3 | async-start | bytes 2097152 | tf_op jit(solution)/shard_map/all_to_all | solution.py:287
  113.2 2.1 %collective-permute-start.6 = (f32[384,128]{1,0:T(8,128)S(1)}, f32[384,128]{1,0:T(8,128)S(1)}, u32[]{:S(2)}, u32[]{:S(2)}) collective-permute-start(f32[384,128]{1,0:T(8,128)S(1)} %get-tuple-element.27), channel_id=1, source_target_pairs={{0,1},{1,0},{2,3},{3,2},{4,5},{5,4},{6,7},{7,6},{8,9},{9,8},{10,11... | collective-permute-start | bytes 589832 | tf_op jit(solution)/shard_map/ppermute | solution.py:268
  113.7 14.3 %collective-permute-start.5 = (f32[96,128]{1,0:T(8,128)S(1)}, f32[96,128]{1,0:T(8,128)S(1)}, u32[]{:S(2)}, u32[]{:S(2)}) collective-permute-start(f32[96,128]{1,0:T(8,128)S(1)} %slice.63), channel_id=1, source_target_pairs={{0,4},{1,5},{2,6},{3,7},{4,0},{5,1},{6,2},{7,3},{8,12},{9,13},{10,... | collective-permute-start | bytes 147464 | tf_op jit(solution)/shard_map/ppermute | solution.py:268
  115.4 12.6 %collective-permute-start.7 = (f32[192,128]{1,0:T(8,128)S(1)}, f32[192,128]{1,0:T(8,128)S(1)}, u32[]{:S(2)}, u32[]{:S(2)}) collective-permute-start(f32[192,128]{1,0:T(8,128)S(1)} %slice.65), channel_id=1, source_target_pairs={{0,2},{1,3},{2,0},{3,1},{4,6},{5,7},{6,4},{7,5},{8,10},{9,11},{10,... | collective-permute-start | bytes 294920 | tf_op jit(solution)/shard_map/ppermute | solution.py:268
  128.0 5.7 %collective-permute-start.8 = (f32[96,128]{1,0:T(8,128)S(1)}, f32[96,128]{1,0:T(8,128)S(1)}, u32[]{:S(2)}, u32[]{:S(2)}) collective-permute-start(f32[96,128]{1,0:T(8,128)S(1)} %slice.67), channel_id=1, source_target_pairs={{0,4},{1,5},{2,6},{3,7},{4,0},{5,1},{6,2},{7,3},{8,12},{9,13},{10,... | collective-permute-start | bytes 147464 | tf_op jit(solution)/shard_map/ppermute | solution.py:268
  130.6 9.1 %collective-permute-start.9 = (f32[192,128]{1,0:T(8,128)S(1)}, f32[192,128]{1,0:T(8,128)S(1)}, u32[]{:S(2)}, u32[]{:S(2)}) collective-permute-start(f32[192,128]{1,0:T(8,128)S(1)} %pad_maximum_fusion.4), channel_id=1, source_target_pairs={{0,8},{1,9},{2,10},{3,11},{4,12},{5,13},{6,14},{7,15},{8,0},{9,1},... | collective-permute-start | bytes 294920 | tf_op jit(solution)/shard_map/ppermute | solution.py:268
  136.9 4.9 %collective-permute-start.17 = (f32[384,128]{1,0:T(8,128)S(1)}, f32[384,128]{1,0:T(8,128)S(1)}, u32[]{:S(2)}, u32[]{:S(2)}) collective-permute-start(f32[384,128]{1,0:T(8,128)S(1)} %get-tuple-element.31), channel_id=1, source_target_pairs={{0,1},{1,0},{2,3},{3,2},{4,5},{5,4},{6,7},{7,6},{8,9},{9,8},{10,11... | collective-permute-start | bytes 589832 | tf_op jit(solution)/shard_map/ppermute | solution.py:268
  139.7 5.5 %collective-permute-start.10 = (f32[192,128]{1,0:T(8,128)S(1)}, f32[192,128]{1,0:T(8,128)S(1)}, u32[]{:S(2)}, u32[]{:S(2)}) collective-permute-start(f32[192,128]{1,0:T(8,128)S(1)} %fusion), channel_id=1, source_target_pairs={{0,4},{1,5},{2,6},{3,7},{4,0},{5,1},{6,2},{7,3},{8,12},{9,13},{10,... | collective-permute-start | bytes 294920 | tf_op jit(solution)/shard_map/ppermute | solution.py:268
  139.7 6.6 %collective-permute-start.13 = (f32[96,128]{1,0:T(8,128)S(1)}, f32[96,128]{1,0:T(8,128)S(1)}, u32[]{:S(2)}, u32[]{:S(2)}) collective-permute-start(f32[96,128]{1,0:T(8,128)S(1)} %slice_add_fusion.4.refs_4_.refs_5_), channel_id=1, source_target_pairs={{0,8},{1,9},{2,10},{3,11},{4,12},{5,13},{6,14},{7,15},{8,0},{9,1},... | collective-permute-start | bytes 147464 | tf_op jit(solution)/shard_map/ppermute | solution.py:268
  141.9 6.8 %collective-permute-start.18 = (f32[192,128]{1,0:T(8,128)S(1)}, f32[192,128]{1,0:T(8,128)S(1)}, u32[]{:S(2)}, u32[]{:S(2)}) collective-permute-start(f32[192,128]{1,0:T(8,128)S(1)} %slice.69), channel_id=1, source_target_pairs={{0,2},{1,3},{2,0},{3,1},{4,6},{5,7},{6,4},{7,5},{8,10},{9,11},{10,... | collective-permute-start | bytes 294920 | tf_op jit(solution)/shard_map/ppermute | solution.py:268
  145.1 9.9 %collective-permute-start.11 = (f32[384,128]{1,0:T(8,128)S(1)}, f32[384,128]{1,0:T(8,128)S(1)}, u32[]{:S(2)}, u32[]{:S(2)}) collective-permute-start(f32[384,128]{1,0:T(8,128)S(1)} %pad_maximum_fusion.1), channel_id=1, source_target_pairs={{0,2},{1,3},{2,0},{3,1},{4,6},{5,7},{6,4},{7,5},{8,10},{9,11},{10,... | collective-permute-start | bytes 589832 | tf_op jit(solution)/shard_map/ppermute | solution.py:268
  146.3 4.8 %collective-permute-start.14 = (f32[96,128]{1,0:T(8,128)S(1)}, f32[96,128]{1,0:T(8,128)S(1)}, u32[]{:S(2)}, u32[]{:S(2)}) collective-permute-start(f32[96,128]{1,0:T(8,128)S(1)} %add.52), channel_id=1, source_target_pairs={{0,4},{1,5},{2,6},{3,7},{4,0},{5,1},{6,2},{7,3},{8,12},{9,13},{10,... | collective-permute-start | bytes 147464 | tf_op jit(solution)/shard_map/ppermute | solution.py:268
  148.7 4.7 %collective-permute-start.19 = (f32[192,128]{1,0:T(8,128)S(1)}, f32[192,128]{1,0:T(8,128)S(1)}, u32[]{:S(2)}, u32[]{:S(2)}) collective-permute-start(f32[192,128]{1,0:T(8,128)S(1)} %slice_add_fusion), channel_id=1, source_target_pairs={{0,4},{1,5},{2,6},{3,7},{4,0},{5,1},{6,2},{7,3},{8,12},{9,13},{10,... | collective-permute-start | bytes 294920 | tf_op jit(solution)/shard_map/ppermute | solution.py:268
  151.2 10.1 %collective-permute-start.15 = (f32[192,128]{1,0:T(8,128)S(1)}, f32[192,128]{1,0:T(8,128)S(1)}, u32[]{:S(2)}, u32[]{:S(2)}) collective-permute-start(f32[192,128]{1,0:T(8,128)S(1)} %pad_maximum_fusion.5), channel_id=1, source_target_pairs={{0,2},{1,3},{2,0},{3,1},{4,6},{5,7},{6,4},{7,5},{8,10},{9,11},{10,... | collective-permute-start | bytes 294920 | tf_op jit(solution)/shard_map/ppermute | solution.py:268
  153.4 6.5 %collective-permute-start.20 = (f32[192,128]{1,0:T(8,128)S(1)}, f32[192,128]{1,0:T(8,128)S(1)}, u32[]{:S(2)}, u32[]{:S(2)}) collective-permute-start(f32[192,128]{1,0:T(8,128)S(1)} %add.55.refs_0_), channel_id=1, source_target_pairs={{0,8},{1,9},{2,10},{3,11},{4,12},{5,13},{6,14},{7,15},{8,0},{9,1},... | collective-permute-start | bytes 294920 | tf_op jit(solution)/shard_map/ppermute | solution.py:268
  155.1 9.6 %collective-permute-start.12 = (f32[768,128]{1,0:T(8,128)S(1)}, f32[768,128]{1,0:T(8,128)S(1)}, u32[]{:S(2)}, u32[]{:S(2)}) collective-permute-start(f32[768,128]{1,0:T(8,128)S(1)} %pad_maximum_fusion.refs_1_), channel_id=1, source_target_pairs={{0,1},{1,0},{2,3},{3,2},{4,5},{5,4},{6,7},{7,6},{8,9},{9,8},{10,11... | collective-permute-start | bytes 1179656 | tf_op jit(solution)/shard_map/ppermute | solution.py:268
  159.9 4.7 %collective-permute-start.21 = (f32[192,128]{1,0:T(8,128)S(1)}, f32[192,128]{1,0:T(8,128)S(1)}, u32[]{:S(2)}, u32[]{:S(2)}) collective-permute-start(f32[192,128]{1,0:T(8,128)S(1)} %shard_map.68), channel_id=1, source_target_pairs={{0,2},{1,3},{2,0},{3,1},{4,6},{5,7},{6,4},{7,5},{8,10},{9,11},{10,... | collective-permute-start | bytes 294920 | tf_op jit(solution)/shard_map/ppermute | solution.py:268
  161.3 3.4 %collective-permute-start.16 = (f32[384,128]{1,0:T(8,128)S(1)}, f32[384,128]{1,0:T(8,128)S(1)}, u32[]{:S(2)}, u32[]{:S(2)}) collective-permute-start(f32[384,128]{1,0:T(8,128)S(1)} %pad_maximum_fusion.2.refs_3_), channel_id=1, source_target_pairs={{0,1},{1,0},{2,3},{3,2},{4,5},{5,4},{6,7},{7,6},{8,9},{9,8},{10,11... | collective-permute-start | bytes 589832 | tf_op jit(solution)/shard_map/ppermute | solution.py:268
  164.6 1.5 collective-permute-start.22
  (4 other events, 4.0 us)

commit v3 on v2

--- a/solution.py
+++ b/solution.py
@@ -384,9 +384,9 @@
     late = total
     for step in steps[1:late_depth]:
         late = halved(late, shards, step)
-    for step in steps[late_depth:-1]:
+    for step in steps[late_depth + 1 :]:
         late = late + exchange(late, shards, step)
-    late = add(late, exchange(late, shards, steps[-1]), over)
+    late = add(late, exchange(late, shards, steps[late_depth]), over)
     finished = [*early, doubled(late, shards, late_depth)]
     groups = (*((group, early_depth) for group in groups), ((0,), late_depth))
     grads = call(

time: 169 us -> 168 us (level)
  no operation moved by 1% of the time
where the time goes in v3:
time: 168 us
  waiting for transfers between devices  72.7 us (43%)
  starting transfers between devices  56.3 us (34%)
  Pallas kernels  30.7 us (18%)
  local copies, waits for them, and re-layouts  6.62 us (4%)
    ppermute x23, waiting for transfers between devices, exchange(): return lax.ppermute(x, 'qa', [(i, i ^ step) for i in range(shards)])  40.5 us
    all_to_all x4, waiting for transfers between devices, swapped(): x = lax.all_to_all(x, 'qa', split_axis=0, concat_axis=0, tiled=True)  32.2 us
    pallas_call x12, Pallas kernels, call(): pl.pallas_call(whole, out_shape=out_shape, in_specs=[*(in_specs or [VMEM]...  30.7 us
    ppermute x23, starting transfers between devices, exchange(): return lax.ppermute(x, 'qa', [(i, i ^ step) for i in range(shards)])  28.6 us
    all_to_all x4, starting transfers between devices, swapped(): x = lax.all_to_all(x, 'qa', split_axis=0, concat_axis=0, tiled=True)  27.7 us
    unnamed x18, local copies, waits for them, and re-layouts  6.57 us
  transfers between devices with their start and end apart: 27, of which 15 were waited for; matrix products, arithmetic and copies ran while one was open for 0% of the time, Pallas kernels for 10%

profile of v3, /device:TPU:0, one launch (start us, length us, event | category | flops | bytes accessed | tf_op | source)
XLA Modules:
  0.0 167.8 jit_solution(6286589038809338117)
XLA Ops:
  0.6 2.1 %shard_map.58 = f32[16,128,128]{2,1,0:T(8,128)} custom-call(f32[1024,128]{1,0:T(8,128)} %bitcast.25, f32[1024,128]{1,0:T(8,128)} %bitcast.26), custom_call_target="tpu_custom_call" | custom-call | bytes 2097152 | tf_op jit(solution)/shard_map/pallas_call | solution.py:28
  2.8 7.4 %all-to-all-start = ((f32[16,128,128]{2,1,0:T(8,128)}), f32[16,128,128]{2,1,0:T(8,128)S(1)}, u32[]{:S(2)}, u32[]{:S(2)}) async-start(f32[16,128,128]{2,1,0:T(8,128)} %shard_map.58), calls=%async_computation | async-start | bytes 2097152 | tf_op jit(solution)/shard_map/all_to_all | solution.py:287
  15.0 18.1 %all-to-all-done.refs_0_ = f32[16,128,128]{2,1,0:T(8,128)S(1)} async-done(((f32[16,128,128]{2,1,0:T(8,128)}), f32[16,128,128]{2,1,0:T(8,128)S(1)}, u32[]{:S(2)}, u32[]{:S(2)}) %all-to-all-start) | async-done | bytes 1048608 | tf_op jit(solution)/shard_map/all_to_all | solution.py:287
  33.1 3.1 %shard_map.60 = f32[16,128,128]{2,1,0:T(8,128)} custom-call(f32[16,128,128]{2,1,0:T(8,128)S(1)} %all-to-all-done.refs_0_, bf16[3,2,256,256]{3,2,1,0:T(8,128)(2,1)S(1)} %get-tuple-element.18.refs_1_), custom_call_target="tpu_custom_call" | custom-call | flops 402653184 | bytes 2883584 | tf_op jit(solution)/shard_map/pallas_call | solution.py:28
  36.2 6.9 %all-to-all-start.1 = ((f32[16,128,128]{2,1,0:T(8,128)}), f32[16,128,128]{2,1,0:T(8,128)S(1)}, u32[]{:S(2)}, u32[]{:S(2)}) async-start(f32[16,128,128]{2,1,0:T(8,128)} %shard_map.60), calls=%async_computation.1 | async-start | bytes 2097152 | tf_op jit(solution)/shard_map/all_to_all | solution.py:287
  44.3 3.2 %shard_map.61 = (f32[384,128]{1,0:T(8,128)S(1)}, f32[384,128]{1,0:T(8,128)S(1)}) custom-call(f32[16,128,128]{2,1,0:T(8,128)S(1)} %all-to-all-done.refs_0_, bf16[3,2,256,256]{3,2,1,0:T(8,128)(2,1)S(1)} %copy-done.7, s32[3]{0:T(128)S(1)} %pad_add_fusion.refs_2_.refs_0_), custom_call_target="tpu_custom_call" | custom-call | flops 402653184 | bytes 2228236 | tf_op jit(solution)/shard_map/pallas_call | solution.py:28
  49.1 2.0 %collective-permute-start.1 = (f32[192,128]{1,0:T(8,128)S(1)}, f32[192,128]{1,0:T(8,128)S(1)}, u32[]{:S(2)}, u32[]{:S(2)}) collective-permute-start(f32[192,128]{1,0:T(8,128)S(1)} %slice.57), channel_id=1, source_target_pairs={{0,2},{1,3},{2,0},{3,1},{4,6},{5,7},{6,4},{7,5},{8,10},{9,11},{10,... | collective-permute-start | bytes 294920 | tf_op jit(solution)/shard_map/ppermute | solution.py:268
  51.0 5.1 %collective-permute-done.1 = f32[192,128]{1,0:T(8,128)S(1)} collective-permute-done((f32[192,128]{1,0:T(8,128)S(1)}, f32[192,128]{1,0:T(8,128)S(1)}, u32[]{:S(2)}, u32[]{:S(2)}) %collective-permute-start.1) | collective-permute-done | bytes 98336 | tf_op jit(solution)/shard_map/ppermute | solution.py:268
  56.1 9.9 %all-to-all-done.1.refs_0_ = f32[16,128,128]{2,1,0:T(8,128)S(1)} async-done(((f32[16,128,128]{2,1,0:T(8,128)}), f32[16,128,128]{2,1,0:T(8,128)S(1)}, u32[]{:S(2)}, u32[]{:S(2)}) %all-to-all-start.1) | async-done | bytes 1048608 | tf_op jit(solution)/shard_map/all_to_all | solution.py:287
  66.0 3.1 %shard_map.62 = f32[16,128,128]{2,1,0:T(8,128)} custom-call(f32[16,128,128]{2,1,0:T(8,128)S(1)} %all-to-all-done.1.refs_0_, bf16[3,2,256,256]{3,2,1,0:T(8,128)(2,1)S(1)} %copy-done.4, f32[192,128]{1,0:T(8,128)S(1)} %slice_add_fusion.3.refs_2_), custom_call_target="tpu_custom_call" | custom-call | flops 402653184 | bytes 2883584 | tf_op jit(solution)/shard_map/pallas_call | solution.py:28
  69.1 6.9 %all-to-all-start.2 = ((f32[16,128,128]{2,1,0:T(8,128)}), f32[16,128,128]{2,1,0:T(8,128)S(1)}, u32[]{:S(2)}, u32[]{:S(2)}) async-start(f32[16,128,128]{2,1,0:T(8,128)} %shard_map.62), calls=%async_computation.2 | async-start | bytes 2097152 | tf_op jit(solution)/shard_map/all_to_all | solution.py:287
  77.1 3.2 %shard_map.63 = (f32[384,128]{1,0:T(8,128)S(1)}, f32[384,128]{1,0:T(8,128)S(1)}) custom-call(f32[16,128,128]{2,1,0:T(8,128)S(1)} %all-to-all-done.1.refs_0_, bf16[3,2,256,256]{3,2,1,0:T(8,128)(2,1)S(1)} %copy-done.5, s32[3]{0:T(128)S(1)} %pad_add_fusion.refs_2_.refs_0_), custom_call_target="tpu_custom_call" | custom-call | flops 402653184 | bytes 2228236 | tf_op jit(solution)/shard_map/pallas_call | solution.py:28
  84.1 11.0 %collective-permute-done.2 = f32[96,128]{1,0:T(8,128)S(1)} collective-permute-done((f32[96,128]{1,0:T(8,128)S(1)}, f32[96,128]{1,0:T(8,128)S(1)}, u32[]{:S(2)}, u32[]{:S(2)}) %collective-permute-start.2) | collective-permute-done | bytes 49184 | tf_op jit(solution)/shard_map/ppermute | solution.py:268
  95.1 4.2 %all-to-all-done.2.refs_0_ = f32[16,128,128]{2,1,0:T(8,128)S(1)} async-done(((f32[16,128,128]{2,1,0:T(8,128)}), f32[16,128,128]{2,1,0:T(8,128)S(1)}, u32[]{:S(2)}, u32[]{:S(2)}) %all-to-all-start.2) | async-done | bytes 1048608 | tf_op jit(solution)/shard_map/all_to_all | solution.py:287
  99.3 3.1 %shard_map.64 = f32[16,128,128]{2,1,0:T(8,128)} custom-call(f32[16,128,128]{2,1,0:T(8,128)S(1)} %all-to-all-done.2.refs_0_, bf16[3,2,256,256]{3,2,1,0:T(8,128)(2,1)S(1)} %copy-done.1, f32[96,128]{1,0:T(8,128)S(1)} %slice_add_fusion.6.refs_2_.refs_3_, f32[192,128]{1,0:T(8,128)S(1)} %slice_add_fusion.2.refs_3_), custom_call_target="tpu_custom_call" | custom-call | flops 402653184 | bytes 2883584 | tf_op jit(solution)/shard_map/pallas_call | solution.py:28
  102.4 6.5 %all-to-all-start.3 = ((f32[16,128,128]{2,1,0:T(8,128)}), f32[16,128,128]{2,1,0:T(8,128)S(1)}, u32[]{:S(2)}, u32[]{:S(2)}) async-start(f32[16,128,128]{2,1,0:T(8,128)} %shard_map.64), calls=%async_computation.3 | async-start | bytes 2097152 | tf_op jit(solution)/shard_map/all_to_all | solution.py:287
  110.0 3.2 %shard_map.65 = (f32[384,128]{1,0:T(8,128)S(1)}, f32[384,128]{1,0:T(8,128)S(1)}) custom-call(f32[16,128,128]{2,1,0:T(8,128)S(1)} %all-to-all-done.2.refs_0_, bf16[3,2,256,256]{3,2,1,0:T(8,128)(2,1)S(1)} %copy-done.2, s32[3]{0:T(128)S(1)} %pad_add_fusion.refs_2_.refs_0_), custom_call_target="tpu_custom_call" | custom-call | flops 402653184 | bytes 2228236 | tf_op jit(solution)/shard_map/pallas_call | solution.py:28
  117.0 11.0 %collective-permute-done.5 = f32[96,128]{1,0:T(8,128)S(1)} collective-permute-done((f32[96,128]{1,0:T(8,128)S(1)}, f32[96,128]{1,0:T(8,128)S(1)}, u32[]{:S(2)}, u32[]{:S(2)}) %collective-permute-start.5) | collective-permute-done | bytes 49184 | tf_op jit(solution)/shard_map/ppermute | solution.py:268
  128.0 2.5 %collective-permute-start.8 = (f32[96,128]{1,0:T(8,128)S(1)}, f32[96,128]{1,0:T(8,128)S(1)}, u32[]{:S(2)}, u32[]{:S(2)}) collective-permute-start(f32[96,128]{1,0:T(8,128)S(1)} %slice.67), channel_id=1, source_target_pairs={{0,4},{1,5},{2,6},{3,7},{4,0},{5,1},{6,2},{7,3},{8,12},{9,13},{10,... | collective-permute-start | bytes 147464 | tf_op jit(solution)/shard_map/ppermute | solution.py:268
  130.6 2.1 %collective-permute-start.9 = (f32[192,128]{1,0:T(8,128)S(1)}, f32[192,128]{1,0:T(8,128)S(1)}, u32[]{:S(2)}, u32[]{:S(2)}) collective-permute-start(f32[192,128]{1,0:T(8,128)S(1)} %pad_maximum_fusion.4), channel_id=1, source_target_pairs={{0,8},{1,9},{2,10},{3,11},{4,12},{5,13},{6,14},{7,15},{8,0},{9,1},... | collective-permute-start | bytes 294920 | tf_op jit(solution)/shard_map/ppermute | solution.py:268
  133.7 3.2 %shard_map.67 = (f32[384,128]{1,0:T(8,128)S(1)}, f32[384,128]{1,0:T(8,128)S(1)}) custom-call(f32[16,128,128]{2,1,0:T(8,128)S(1)} %all-to-all-done.3.refs_0_, bf16[3,2,256,256]{3,2,1,0:T(8,128)(2,1)S(1)} %get-tuple-element.25.refs_1_, s32[3]{0:T(128)S(1)} %pad_add_fusion.refs_2_.refs_0_, f32[96,128]{1,0:T(8,128)S(1)} %slice_add_fusion.6.refs_2_.refs_3_, ...), custom_call_target="tpu_custom_call" | custom-call | flops 402653184 | bytes 2228236 | tf_op jit(solution)/shard_map/pallas_call | solution.py:28
  137.0 2.6 %collective-permute-done.9 = f32[192,128]{1,0:T(8,128)S(1)} collective-permute-done((f32[192,128]{1,0:T(8,128)S(1)}, f32[192,128]{1,0:T(8,128)S(1)}, u32[]{:S(2)}, u32[]{:S(2)}) %collective-permute-start.9) | collective-permute-done | bytes 98336 | tf_op jit(solution)/shard_map/ppermute | solution.py:268
  139.7 2.1 %collective-permute-start.13 = (f32[96,128]{1,0:T(8,128)S(1)}, f32[96,128]{1,0:T(8,128)S(1)}, u32[]{:S(2)}, u32[]{:S(2)}) collective-permute-start(f32[96,128]{1,0:T(8,128)S(1)} %slice_add_fusion.4.refs_4_.refs_5_), channel_id=1, source_target_pairs={{0,8},{1,9},{2,10},{3,11},{4,12},{5,13},{6,14},{7,15},{8,0},{9,1},... | collective-permute-start | bytes 147464 | tf_op jit(solution)/shard_map/ppermute | solution.py:268
  141.9 2.6 %collective-permute-start.18 = (f32[192,128]{1,0:T(8,128)S(1)}, f32[192,128]{1,0:T(8,128)S(1)}, u32[]{:S(2)}, u32[]{:S(2)}) collective-permute-start(f32[192,128]{1,0:T(8,128)S(1)} %slice.69), channel_id=1, source_target_pairs={{0,2},{1,3},{2,0},{3,1},{4,6},{5,7},{6,4},{7,5},{8,10},{9,11},{10,... | collective-permute-start | bytes 294920 | tf_op jit(solution)/shard_map/ppermute | solution.py:268
  146.3 2.3 %collective-permute-start.14 = (f32[96,128]{1,0:T(8,128)S(1)}, f32[96,128]{1,0:T(8,128)S(1)}, u32[]{:S(2)}, u32[]{:S(2)}) collective-permute-start(f32[96,128]{1,0:T(8,128)S(1)} %add.52), channel_id=1, source_target_pairs={{0,4},{1,5},{2,6},{3,7},{4,0},{5,1},{6,2},{7,3},{8,12},{9,13},{10,... | collective-permute-start | bytes 147464 | tf_op jit(solution)/shard_map/ppermute | solution.py:268
  148.7 1.7 %collective-permute-start.19 = (f32[192,128]{1,0:T(8,128)S(1)}, f32[192,128]{1,0:T(8,128)S(1)}, u32[]{:S(2)}, u32[]{:S(2)}) collective-permute-start(f32[192,128]{1,0:T(8,128)S(1)} %slice_add_fusion), channel_id=1, source_target_pairs={{0,8},{1,9},{2,10},{3,11},{4,12},{5,13},{6,14},{7,15},{8,0},{9,1},... | collective-permute-start | bytes 294920 | tf_op jit(solution)/shard_map/ppermute | solution.py:268
  150.7 2.1 %collective-permute-start.15 = (f32[192,128]{1,0:T(8,128)S(1)}, f32[192,128]{1,0:T(8,128)S(1)}, u32[]{:S(2)}, u32[]{:S(2)}) collective-permute-start(f32[192,128]{1,0:T(8,128)S(1)} %pad_maximum_fusion.5), channel_id=1, source_target_pairs={{0,2},{1,3},{2,0},{3,1},{4,6},{5,7},{6,4},{7,5},{8,10},{9,11},{10,... | collective-permute-start | bytes 294920 | tf_op jit(solution)/shard_map/ppermute | solution.py:268
  152.8 1.9 %collective-permute-done.19 = f32[192,128]{1,0:T(8,128)S(1)} collective-permute-done((f32[192,128]{1,0:T(8,128)S(1)}, f32[192,128]{1,0:T(8,128)S(1)}, u32[]{:S(2)}, u32[]{:S(2)}) %collective-permute-start.19) | collective-permute-done | bytes 98336 | tf_op jit(solution)/shard_map/ppermute | solution.py:268
  155.0 3.0 %shard_map.66 = (f32[1024,128]{1,0:T(8,128)}, f32[1024,128]{1,0:T(8,128)}, f32[8,128]{1,0:T(8,128)S(1)}) custom-call(f32[16,128,128]{2,1,0:T(8,128)S(1)} %all-to-all-done.3.refs_0_, bf16[3,2,256,256]{3,2,1,0:T(8,128)(2,1)S(1)} %get-tuple-element.25.refs_1_, f32[96,128]{1,0:T(8,128)S(1)} %slice_add_fusion.6.refs_2_.refs_3_, ...), custom_call_target="tpu_custom_call" | custom-call | flops 402653184 | bytes 2887680 | tf_op jit(solution)/shard_map/pallas_call | solution.py:28
  159.5 1.8 %collective-permute-start.21 = (f32[192,128]{1,0:T(8,128)S(1)}, f32[192,128]{1,0:T(8,128)S(1)}, u32[]{:S(2)}, u32[]{:S(2)}) collective-permute-start(f32[192,128]{1,0:T(8,128)S(1)} %shard_map.68), channel_id=1, source_target_pairs={{0,2},{1,3},{2,0},{3,1},{4,6},{5,7},{6,4},{7,5},{8,10},{9,11},{10,... | collective-permute-start | bytes 294920 | tf_op jit(solution)/shard_map/ppermute | solution.py:268
  161.4 2.8 %collective-permute-done.21 = f32[192,128]{1,0:T(8,128)S(1)} collective-permute-done((f32[192,128]{1,0:T(8,128)S(1)}, f32[192,128]{1,0:T(8,128)S(1)}, u32[]{:S(2)}, u32[]{:S(2)}) %collective-permute-start.21) | collective-permute-done | bytes 98336 | tf_op jit(solution)/shard_map/ppermute | solution.py:268
  165.7 1.9 %shard_map.69 = f32[4,768,128]{2,1,0:T(8,128)} custom-call(s32[3]{0:T(128)S(1)} %pad_add_fusion.refs_2_.refs_0_, f32[768,128]{1,0:T(8,128)S(1)} %pad_maximum_fusion.refs_1_, f32[768,128]{1,0:T(8,128)S(1)} %collective-permute-done.12.refs_2_, f32[384,128]{1,0:T(8,128)S(1)} %pad_maximum_fusion.2.refs_3_, f32[384,128]{1,0:T(8,128)S(1)} %collective-permute-done.16.refs_4_, ...), custom_call_target="tpu_custom_call" | custom-call | bytes 3145740 | tf_op jit(solution)/shard_map/pallas_call | solution.py:28
  (80 shorter events, 24.0 us)
Async XLA Ops:
  2.8 30.3 %all-to-all-start = ((f32[16,128,128]{2,1,0:T(8,128)}), f32[16,128,128]{2,1,0:T(8,128)S(1)}, u32[]{:S(2)}, u32[]{:S(2)}) async-start(f32[16,128,128]{2,1,0:T(8,128)} %shard_map.58), calls=%async_computation | async-start | bytes 2097152 | tf_op jit(solution)/shard_map/all_to_all | solution.py:287
  10.2 1.4 copy-start.8
  15.0 21.2 %copy-start.6 = (bf16[3,2,256,256]{3,2,1,0:T(8,128)(2,1)}, bf16[3,2,256,256]{3,2,1,0:T(8,128)(2,1)S(1)}, u32[]{:S(2)}) copy-start(bf16[3,2,256,256]{3,2,1,0:T(8,128)(2,1)S(1)} %get-tuple-element.18.refs_1_) | copy-start | bytes 2359300
  36.2 29.8 %all-to-all-start.1 = ((f32[16,128,128]{2,1,0:T(8,128)}), f32[16,128,128]{2,1,0:T(8,128)S(1)}, u32[]{:S(2)}, u32[]{:S(2)}) async-start(f32[16,128,128]{2,1,0:T(8,128)} %shard_map.60), calls=%async_computation.1 | async-start | bytes 2097152 | tf_op jit(solution)/shard_map/all_to_all | solution.py:287
  43.2 1.1 copy-start.7
  47.5 18.5 %copy-start.4 = (bf16[3,2,256,256]{3,2,1,0:T(8,128)(2,1)S(1)}, bf16[3,2,256,256]{3,2,1,0:T(8,128)(2,1)}, u32[]{:S(2)}) copy-start(bf16[3,2,256,256]{3,2,1,0:T(8,128)(2,1)} %copy-done.3) | copy-start | bytes 2359300
  47.5 1.5 collective-permute-start
  49.1 7.0 %collective-permute-start.1 = (f32[192,128]{1,0:T(8,128)S(1)}, f32[192,128]{1,0:T(8,128)S(1)}, u32[]{:S(2)}, u32[]{:S(2)}) collective-permute-start(f32[192,128]{1,0:T(8,128)S(1)} %slice.57), channel_id=1, source_target_pairs={{0,2},{1,3},{2,0},{3,1},{4,6},{5,7},{6,4},{7,5},{8,10},{9,11},{10,... | collective-permute-start | bytes 294920 | tf_op jit(solution)/shard_map/ppermute | solution.py:268
  69.1 30.2 %all-to-all-start.2 = ((f32[16,128,128]{2,1,0:T(8,128)}), f32[16,128,128]{2,1,0:T(8,128)S(1)}, u32[]{:S(2)}, u32[]{:S(2)}) async-start(f32[16,128,128]{2,1,0:T(8,128)} %shard_map.62), calls=%async_computation.2 | async-start | bytes 2097152 | tf_op jit(solution)/shard_map/all_to_all | solution.py:287
  80.3 19.0 %copy-start.1 = (bf16[3,2,256,256]{3,2,1,0:T(8,128)(2,1)S(1)}, bf16[3,2,256,256]{3,2,1,0:T(8,128)(2,1)}, u32[]{:S(2)}) copy-start(bf16[3,2,256,256]{3,2,1,0:T(8,128)(2,1)} %copy-done) | copy-start | bytes 2359300
  80.3 2.2 %collective-permute-start.3 = (f32[384,128]{1,0:T(8,128)S(1)}, f32[384,128]{1,0:T(8,128)S(1)}, u32[]{:S(2)}, u32[]{:S(2)}) collective-permute-start(f32[384,128]{1,0:T(8,128)S(1)} %get-tuple-element.24), channel_id=1, source_target_pairs={{0,1},{1,0},{2,3},{3,2},{4,5},{5,4},{6,7},{7,6},{8,9},{9,8},{10,11... | collective-permute-start | bytes 589832 | tf_op jit(solution)/shard_map/ppermute | solution.py:268
  80.8 14.3 %collective-permute-start.2 = (f32[96,128]{1,0:T(8,128)S(1)}, f32[96,128]{1,0:T(8,128)S(1)}, u32[]{:S(2)}, u32[]{:S(2)}) collective-permute-start(f32[96,128]{1,0:T(8,128)S(1)} %slice.59), channel_id=1, source_target_pairs={{0,4},{1,5},{2,6},{3,7},{4,0},{5,1},{6,2},{7,3},{8,12},{9,13},{10,... | collective-permute-start | bytes 147464 | tf_op jit(solution)/shard_map/ppermute | solution.py:268
  82.5 12.6 %collective-permute-start.4 = (f32[192,128]{1,0:T(8,128)S(1)}, f32[192,128]{1,0:T(8,128)S(1)}, u32[]{:S(2)}, u32[]{:S(2)}) collective-permute-start(f32[192,128]{1,0:T(8,128)S(1)} %slice.61), channel_id=1, source_target_pairs={{0,2},{1,3},{2,0},{3,1},{4,6},{5,7},{6,4},{7,5},{8,10},{9,11},{10,... | collective-permute-start | bytes 294920 | tf_op jit(solution)/shard_map/ppermute | solution.py:268
  102.4 31.3 %all-to-all-start.3 = ((f32[16,128,128]{2,1,0:T(8,128)}), f32[16,128,128]{2,1,0:T(8,128)S(1)}, u32[]{:S(2)}, u32[]{:S(2)}) async-start(f32[16,128,128]{2,1,0:T(8,128)} %shard_map.64), calls=%async_computation.3 | async-start | bytes 2097152 | tf_op jit(solution)/shard_map/all_to_all | solution.py:287
  113.2 2.1 %collective-permute-start.6 = (f32[384,128]{1,0:T(8,128)S(1)}, f32[384,128]{1,0:T(8,128)S(1)}, u32[]{:S(2)}, u32[]{:S(2)}) collective-permute-start(f32[384,128]{1,0:T(8,128)S(1)} %get-tuple-element.27), channel_id=1, source_target_pairs={{0,1},{1,0},{2,3},{3,2},{4,5},{5,4},{6,7},{7,6},{8,9},{9,8},{10,11... | collective-permute-start | bytes 589832 | tf_op jit(solution)/shard_map/ppermute | solution.py:268
  113.7 14.3 %collective-permute-start.5 = (f32[96,128]{1,0:T(8,128)S(1)}, f32[96,128]{1,0:T(8,128)S(1)}, u32[]{:S(2)}, u32[]{:S(2)}) collective-permute-start(f32[96,128]{1,0:T(8,128)S(1)} %slice.63), channel_id=1, source_target_pairs={{0,4},{1,5},{2,6},{3,7},{4,0},{5,1},{6,2},{7,3},{8,12},{9,13},{10,... | collective-permute-start | bytes 147464 | tf_op jit(solution)/shard_map/ppermute | solution.py:268
  115.4 12.6 %collective-permute-start.7 = (f32[192,128]{1,0:T(8,128)S(1)}, f32[192,128]{1,0:T(8,128)S(1)}, u32[]{:S(2)}, u32[]{:S(2)}) collective-permute-start(f32[192,128]{1,0:T(8,128)S(1)} %slice.65), channel_id=1, source_target_pairs={{0,2},{1,3},{2,0},{3,1},{4,6},{5,7},{6,4},{7,5},{8,10},{9,11},{10,... | collective-permute-start | bytes 294920 | tf_op jit(solution)/shard_map/ppermute | solution.py:268
  128.0 5.7 %collective-permute-start.8 = (f32[96,128]{1,0:T(8,128)S(1)}, f32[96,128]{1,0:T(8,128)S(1)}, u32[]{:S(2)}, u32[]{:S(2)}) collective-permute-start(f32[96,128]{1,0:T(8,128)S(1)} %slice.67), channel_id=1, source_target_pairs={{0,4},{1,5},{2,6},{3,7},{4,0},{5,1},{6,2},{7,3},{8,12},{9,13},{10,... | collective-permute-start | bytes 147464 | tf_op jit(solution)/shard_map/ppermute | solution.py:268
  130.6 9.1 %collective-permute-start.9 = (f32[192,128]{1,0:T(8,128)S(1)}, f32[192,128]{1,0:T(8,128)S(1)}, u32[]{:S(2)}, u32[]{:S(2)}) collective-permute-start(f32[192,128]{1,0:T(8,128)S(1)} %pad_maximum_fusion.4), channel_id=1, source_target_pairs={{0,8},{1,9},{2,10},{3,11},{4,12},{5,13},{6,14},{7,15},{8,0},{9,1},... | collective-permute-start | bytes 294920 | tf_op jit(solution)/shard_map/ppermute | solution.py:268
  136.9 4.9 %collective-permute-start.17 = (f32[384,128]{1,0:T(8,128)S(1)}, f32[384,128]{1,0:T(8,128)S(1)}, u32[]{:S(2)}, u32[]{:S(2)}) collective-permute-start(f32[384,128]{1,0:T(8,128)S(1)} %get-tuple-element.31), channel_id=1, source_target_pairs={{0,1},{1,0},{2,3},{3,2},{4,5},{5,4},{6,7},{7,6},{8,9},{9,8},{10,11... | collective-permute-start | bytes 589832 | tf_op jit(solution)/shard_map/ppermute | solution.py:268
  139.7 5.5 %collective-permute-start.10 = (f32[192,128]{1,0:T(8,128)S(1)}, f32[192,128]{1,0:T(8,128)S(1)}, u32[]{:S(2)}, u32[]{:S(2)}) collective-permute-start(f32[192,128]{1,0:T(8,128)S(1)} %fusion), channel_id=1, source_target_pairs={{0,4},{1,5},{2,6},{3,7},{4,0},{5,1},{6,2},{7,3},{8,12},{9,13},{10,... | collective-permute-start | bytes 294920 | tf_op jit(solution)/shard_map/ppermute | solution.py:268
  139.7 6.6 %collective-permute-start.13 = (f32[96,128]{1,0:T(8,128)S(1)}, f32[96,128]{1,0:T(8,128)S(1)}, u32[]{:S(2)}, u32[]{:S(2)}) collective-permute-start(f32[96,128]{1,0:T(8,128)S(1)} %slice_add_fusion.4.refs_4_.refs_5_), channel_id=1, source_target_pairs={{0,8},{1,9},{2,10},{3,11},{4,12},{5,13},{6,14},{7,15},{8,0},{9,1},... | collective-permute-start | bytes 147464 | tf_op jit(solution)/shard_map/ppermute | solution.py:268
  141.9 6.8 %collective-permute-start.18 = (f32[192,128]{1,0:T(8,128)S(1)}, f32[192,128]{1,0:T(8,128)S(1)}, u32[]{:S(2)}, u32[]{:S(2)}) collective-permute-start(f32[192,128]{1,0:T(8,128)S(1)} %slice.69), channel_id=1, source_target_pairs={{0,2},{1,3},{2,0},{3,1},{4,6},{5,7},{6,4},{7,5},{8,10},{9,11},{10,... | collective-permute-start | bytes 294920 | tf_op jit(solution)/shard_map/ppermute | solution.py:268
  145.1 9.7 %collective-permute-start.11 = (f32[384,128]{1,0:T(8,128)S(1)}, f32[384,128]{1,0:T(8,128)S(1)}, u32[]{:S(2)}, u32[]{:S(2)}) collective-permute-start(f32[384,128]{1,0:T(8,128)S(1)} %pad_maximum_fusion.1), channel_id=1, source_target_pairs={{0,2},{1,3},{2,0},{3,1},{4,6},{5,7},{6,4},{7,5},{8,10},{9,11},{10,... | collective-permute-start | bytes 589832 | tf_op jit(solution)/shard_map/ppermute | solution.py:268
  146.3 4.4 %collective-permute-start.14 = (f32[96,128]{1,0:T(8,128)S(1)}, f32[96,128]{1,0:T(8,128)S(1)}, u32[]{:S(2)}, u32[]{:S(2)}) collective-permute-start(f32[96,128]{1,0:T(8,128)S(1)} %add.52), channel_id=1, source_target_pairs={{0,4},{1,5},{2,6},{3,7},{4,0},{5,1},{6,2},{7,3},{8,12},{9,13},{10,... | collective-permute-start | bytes 147464 | tf_op jit(solution)/shard_map/ppermute | solution.py:268
  148.7 6.1 %collective-permute-start.19 = (f32[192,128]{1,0:T(8,128)S(1)}, f32[192,128]{1,0:T(8,128)S(1)}, u32[]{:S(2)}, u32[]{:S(2)}) collective-permute-start(f32[192,128]{1,0:T(8,128)S(1)} %slice_add_fusion), channel_id=1, source_target_pairs={{0,8},{1,9},{2,10},{3,11},{4,12},{5,13},{6,14},{7,15},{8,0},{9,1},... | collective-permute-start | bytes 294920 | tf_op jit(solution)/shard_map/ppermute | solution.py:268
  150.7 10.6 %collective-permute-start.15 = (f32[192,128]{1,0:T(8,128)S(1)}, f32[192,128]{1,0:T(8,128)S(1)}, u32[]{:S(2)}, u32[]{:S(2)}) collective-permute-start(f32[192,128]{1,0:T(8,128)S(1)} %pad_maximum_fusion.5), channel_id=1, source_target_pairs={{0,2},{1,3},{2,0},{3,1},{4,6},{5,7},{6,4},{7,5},{8,10},{9,11},{10,... | collective-permute-start | bytes 294920 | tf_op jit(solution)/shard_map/ppermute | solution.py:268
  154.8 4.7 %collective-permute-start.20 = (f32[192,128]{1,0:T(8,128)S(1)}, f32[192,128]{1,0:T(8,128)S(1)}, u32[]{:S(2)}, u32[]{:S(2)}) collective-permute-start(f32[192,128]{1,0:T(8,128)S(1)} %add.55.refs_0_), channel_id=1, source_target_pairs={{0,4},{1,5},{2,6},{3,7},{4,0},{5,1},{6,2},{7,3},{8,12},{9,13},{10,... | collective-permute-start | bytes 294920 | tf_op jit(solution)/shard_map/ppermute | solution.py:268
  154.9 9.4 %collective-permute-start.12 = (f32[768,128]{1,0:T(8,128)S(1)}, f32[768,128]{1,0:T(8,128)S(1)}, u32[]{:S(2)}, u32[]{:S(2)}) collective-permute-start(f32[768,128]{1,0:T(8,128)S(1)} %pad_maximum_fusion.refs_1_), channel_id=1, source_target_pairs={{0,1},{1,0},{2,3},{3,2},{4,5},{5,4},{6,7},{7,6},{8,9},{9,8},{10,11... | collective-permute-start | bytes 1179656 | tf_op jit(solution)/shard_map/ppermute | solution.py:268
  159.5 4.7 %collective-permute-start.21 = (f32[192,128]{1,0:T(8,128)S(1)}, f32[192,128]{1,0:T(8,128)S(1)}, u32[]{:S(2)}, u32[]{:S(2)}) collective-permute-start(f32[192,128]{1,0:T(8,128)S(1)} %shard_map.68), channel_id=1, source_target_pairs={{0,2},{1,3},{2,0},{3,1},{4,6},{5,7},{6,4},{7,5},{8,10},{9,11},{10,... | collective-permute-start | bytes 294920 | tf_op jit(solution)/shard_map/ppermute | solution.py:268
  161.3 3.0 %collective-permute-start.16 = (f32[384,128]{1,0:T(8,128)S(1)}, f32[384,128]{1,0:T(8,128)S(1)}, u32[]{:S(2)}, u32[]{:S(2)}) collective-permute-start(f32[384,128]{1,0:T(8,128)S(1)} %pad_maximum_fusion.2.refs_3_), channel_id=1, source_target_pairs={{0,1},{1,0},{2,3},{3,2},{4,5},{5,4},{6,7},{7,6},{8,9},{9,8},{10,11... | collective-permute-start | bytes 589832 | tf_op jit(solution)/shard_map/ppermute | solution.py:268
  164.2 1.5 collective-permute-start.22
  (4 other events, 4.0 us)

commit v4 on v3

--- a/solution.py
+++ b/solution.py
@@ -82,15 +82,20 @@
                 real, imag = (
                     exact(exact(permutation, u, ((0,), (0,))), permutation, ((1,), (0,))) for u in (real, imag)
                 )
-            if position == 1:
-                quarters = ((real, -imag), (imag, real))
-            else:
+            if position != 1:
                 real, imag = real.T, imag.T
-                quarters = ((real, imag), (-imag, real))
-            for i in range(2):
-                for j in range(2):
-                    for half, value in enumerate(halves(quarters[i][j])):
-                        out_refs[number][position, half, pl.ds(i * gate, gate), pl.ds(j * gate, gate)] = value
+            for part, value in enumerate((real, imag)):
+                for half, bits in enumerate(halves(value)):
+                    out_refs[number][position, half, part] = bits
+
+
+def united(gates_ref, position):
+    for half in range(2):
+        real, imag = gates_ref[position, half, 0], gates_ref[position, half, 1]
+        above, below = (-imag, imag) if position == 1 else (imag, -imag)
+        yield jnp.concatenate(
+            [jnp.concatenate([real, above], axis=1), jnp.concatenate([below, real], axis=1)], axis=0
+        )
 
 
 def enter_body(gate, blocks, state_ref, adjoint_ref, out_ref, held_ref, tiles_ref, sems):
@@ -147,9 +152,9 @@
 
 
 def undone(x_ref, gates_ref, gate, blocks):
-    x = left(gates_ref[2], last_input(x_ref, gate, blocks))
-    x = right(middle_input(x, gate), gates_ref[1])
-    return left(gates_ref[0], first_input(x, gate, blocks))
+    x = left(tuple(united(gates_ref, 2)), last_input(x_ref, gate, blocks))
+    x = right(middle_input(x, gate), tuple(united(gates_ref, 1)))
+    return left(tuple(united(gates_ref, 0)), first_input(x, gate, blocks))
 
 
 def piece(x, gate, blocks, array, part, c):
@@ -191,13 +196,13 @@
 def gradient_body(gate, blocks, factor, depth, x_ref, gates_ref, bits_ref, own_ref, other_ref, all_ref):
     size = blocks * gate
     raw = last_input(x_ref, gate, blocks)
-    x = left(gates_ref[2], raw)
+    x = left(tuple(united(gates_ref, 2)), raw)
     last = contract(halves(raw[:, size:]), halves(x[:, :size]), ((1,), (1,)))
     x = middle_input(x, gate)
-    y = right(x, gates_ref[1])
+    y = right(x, tuple(united(gates_ref, 1)))
     middle = contract(halves(x[size:]), halves(y[:size]), ((0,), (0,)))
     x = first_input(y, gate, blocks)
-    first = contract(halves(x[:, size:]), halves(left(gates_ref[0], x[:, :size])), ((1,), (1,)))
+    first = contract(halves(x[:, size:]), halves(left(tuple(united(gates_ref, 0)), x[:, :size])), ((1,), (1,)))
     for position, grads in enumerate((first, middle)):
         for part, value in enumerate(pair(grads, gate)):
             all_ref[pl.ds((position * 2 + part) * gate, gate), :] = factor * value
@@ -305,7 +310,7 @@
 
     matrices = call(
         functools.partial(prepare_body, rounds, gate, blocks),
-        [jax.ShapeDtypeStruct((3, 2, 2 * gate, 2 * gate), BF16)] * rounds,
+        [jax.ShapeDtypeStruct((3, 2, 2, gate, gate), BF16)] * rounds,
         (gates,),
         rounds * 12 * 2 * gate**3,
     )
@@ -388,15 +393,26 @@
         late = late + exchange(late, shards, step)
     late = add(late, exchange(late, shards, steps[late_depth]), over)
     finished = [*early, doubled(late, shards, late_depth)]
-    groups = (*((group, early_depth) for group in groups), ((0,), late_depth))
+    placed = jax.ShapeDtypeStruct((rounds, 6 * gate, gate), F32)
+    first = [half for pair_of in finished[:-1] for half in pair_of]
     grads = call(
-        functools.partial(place_body, groups),
-        jax.ShapeDtypeStruct((rounds, 6 * gate, gate), F32),
-        (bits, *(half for pair_of in finished for half in pair_of)),
+        functools.partial(place_body, tuple((group, early_depth) for group in groups)),
+        placed,
+        (bits, *first),
         0,
-        [SMEM] + [ANY] * (2 * len(groups)),
+        [SMEM] + [ANY] * len(first),
         ANY,
         [pltpu.SemaphoreType.DMA((rounds << early_depth,))],
+    )
+    grads = call(
+        functools.partial(place_body, (((0,), late_depth),)),
+        placed,
+        (bits, *finished[-1], grads),
+        0,
+        [SMEM] + [ANY] * 3,
+        ANY,
+        [pltpu.SemaphoreType.DMA((1 << late_depth,))],
+        aliases={3: 0},
     )
     return leaving(state), leaving(adjoint), grads.reshape(gates.shape)
 

time: 168 us -> 168 us (level)
  local copies, waits for them, and re-layouts: 6.62 us -> 2.45 us
  waiting for transfers between devices: 72.7 us -> 75.7 us
    unnamed x18 -> x6, local copies, waits for them, and re-layouts: 6.57 us -> 2.41 us
    all_to_all x4, waiting for transfers between devices: 32.2 us -> 34.7 us  [swapped(): x = lax.all_to_all(x, 'qa', split_axis=0, concat_axis=0, tiled=True)]
    pallas_call x12 -> x13, Pallas kernels: 30.7 us -> 31.7 us  [call(): pl.pallas_call(whole, out_shape=out_shape, in_specs=[*(in_specs or [VMEM]...]
  transfers between devices with their start and end apart: 27 -> 27, of which waited for: 15 -> 14; matrix products, arithmetic and copies ran while one was open for 0% -> 0% of each run, Pallas kernels for 10% -> 11%
where the time goes in v4:
time: 168 us
  waiting for transfers between devices  75.7 us (45%)
  starting transfers between devices  56.3 us (34%)
  Pallas kernels  31.7 us (19%)
  local copies, waits for them, and re-layouts  2.45 us (1%)
    ppermute x23, waiting for transfers between devices, exchange(): return lax.ppermute(x, 'qa', [(i, i ^ step) for i in range(shards)])  41 us
    all_to_all x4, waiting for transfers between devices, swapped(): x = lax.all_to_all(x, 'qa', split_axis=0, concat_axis=0, tiled=True)  34.7 us
    pallas_call x13, Pallas kernels, call(): pl.pallas_call(whole, out_shape=out_shape, in_specs=[*(in_specs or [VMEM]...  31.7 us
    ppermute x23, starting transfers between devices, exchange(): return lax.ppermute(x, 'qa', [(i, i ^ step) for i in range(shards)])  28.6 us
    all_to_all x4, starting transfers between devices, swapped(): x = lax.all_to_all(x, 'qa', split_axis=0, concat_axis=0, tiled=True)  27.7 us
  transfers between devices with their start and end apart: 27, of which 14 were waited for; matrix products, arithmetic and copies ran while one was open for 0% of the time, Pallas kernels for 11%

profile of v4, /device:TPU:0, one launch (start us, length us, event | category | flops | bytes accessed | tf_op | source)
XLA Modules:
  0.0 167.6 jit_solution(16512992579034544169)
XLA Ops:
  0.6 2.1 %shard_map.58 = f32[16,128,128]{2,1,0:T(8,128)} custom-call(f32[1024,128]{1,0:T(8,128)} %bitcast.25, f32[1024,128]{1,0:T(8,128)} %bitcast.26), custom_call_target="tpu_custom_call" | custom-call | bytes 2097152 | tf_op jit(solution)/shard_map/pallas_call | solution.py:28
  2.8 7.4 %all-to-all-start = ((f32[16,128,128]{2,1,0:T(8,128)}), f32[16,128,128]{2,1,0:T(8,128)S(1)}, u32[]{:S(2)}, u32[]{:S(2)}) async-start(f32[16,128,128]{2,1,0:T(8,128)} %shard_map.58), calls=%async_computation | async-start | bytes 2097152 | tf_op jit(solution)/shard_map/all_to_all | solution.py:292
  13.0 20.1 %all-to-all-done.refs_0_ = f32[16,128,128]{2,1,0:T(8,128)S(1)} async-done(((f32[16,128,128]{2,1,0:T(8,128)}), f32[16,128,128]{2,1,0:T(8,128)S(1)}, u32[]{:S(2)}, u32[]{:S(2)}) %all-to-all-start) | async-done | bytes 1048608 | tf_op jit(solution)/shard_map/all_to_all | solution.py:292
  33.1 3.1 %shard_map.60 = f32[16,128,128]{2,1,0:T(8,128)} custom-call(f32[16,128,128]{2,1,0:T(8,128)S(1)} %all-to-all-done.refs_0_, bf16[3,2,2,128,128]{4,3,2,1,0:T(8,128)(2,1)S(1)} %get-tuple-element.18.refs_1_), custom_call_target="tpu_custom_call" | custom-call | flops 402653184 | bytes 2490368 | tf_op jit(solution)/shard_map/pallas_call | solution.py:28
  36.2 6.9 %all-to-all-start.1 = ((f32[16,128,128]{2,1,0:T(8,128)}), f32[16,128,128]{2,1,0:T(8,128)S(1)}, u32[]{:S(2)}, u32[]{:S(2)}) async-start(f32[16,128,128]{2,1,0:T(8,128)} %shard_map.60), calls=%async_computation.1 | async-start | bytes 2097152 | tf_op jit(solution)/shard_map/all_to_all | solution.py:292
  44.2 3.2 %shard_map.61 = (f32[384,128]{1,0:T(8,128)S(1)}, f32[384,128]{1,0:T(8,128)S(1)}) custom-call(f32[16,128,128]{2,1,0:T(8,128)S(1)} %all-to-all-done.refs_0_, bf16[3,2,2,128,128]{4,3,2,1,0:T(8,128)(2,1)S(1)} %copy-done.2, s32[3]{0:T(128)S(1)} %pad_add_fusion.refs_2_.refs_0_), custom_call_target="tpu_custom_call" | custom-call | flops 402653184 | bytes 1835020 | tf_op jit(solution)/shard_map/pallas_call | solution.py:28
  49.0 2.0 %collective-permute-start.1 = (f32[192,128]{1,0:T(8,128)S(1)}, f32[192,128]{1,0:T(8,128)S(1)}, u32[]{:S(2)}, u32[]{:S(2)}) collective-permute-start(f32[192,128]{1,0:T(8,128)S(1)} %slice.57), channel_id=1, source_target_pairs={{0,2},{1,3},{2,0},{3,1},{4,6},{5,7},{6,4},{7,5},{8,10},{9,11},{10,... | collective-permute-start | bytes 294920 | tf_op jit(solution)/shard_map/ppermute | solution.py:273
  50.9 4.8 %collective-permute-done.1 = f32[192,128]{1,0:T(8,128)S(1)} collective-permute-done((f32[192,128]{1,0:T(8,128)S(1)}, f32[192,128]{1,0:T(8,128)S(1)}, u32[]{:S(2)}, u32[]{:S(2)}) %collective-permute-start.1) | collective-permute-done | bytes 98336 | tf_op jit(solution)/shard_map/ppermute | solution.py:273
  55.7 10.3 %all-to-all-done.1.refs_0_ = f32[16,128,128]{2,1,0:T(8,128)S(1)} async-done(((f32[16,128,128]{2,1,0:T(8,128)}), f32[16,128,128]{2,1,0:T(8,128)S(1)}, u32[]{:S(2)}, u32[]{:S(2)}) %all-to-all-start.1) | async-done | bytes 1048608 | tf_op jit(solution)/shard_map/all_to_all | solution.py:292
  66.0 3.1 %shard_map.62 = f32[16,128,128]{2,1,0:T(8,128)} custom-call(f32[16,128,128]{2,1,0:T(8,128)S(1)} %all-to-all-done.1.refs_0_, bf16[3,2,2,128,128]{4,3,2,1,0:T(8,128)(2,1)S(1)} %get-tuple-element.19.refs_1_, f32[192,128]{1,0:T(8,128)S(1)} %slice_add_fusion.3.refs_2_), custom_call_target="tpu_custom_call" | custom-call | flops 402653184 | bytes 2490368 | tf_op jit(solution)/shard_map/pallas_call | solution.py:28
  69.1 6.9 %all-to-all-start.2 = ((f32[16,128,128]{2,1,0:T(8,128)}), f32[16,128,128]{2,1,0:T(8,128)S(1)}, u32[]{:S(2)}, u32[]{:S(2)}) async-start(f32[16,128,128]{2,1,0:T(8,128)} %shard_map.62), calls=%async_computation.2 | async-start | bytes 2097152 | tf_op jit(solution)/shard_map/all_to_all | solution.py:292
  76.0 3.2 %shard_map.63 = (f32[384,128]{1,0:T(8,128)S(1)}, f32[384,128]{1,0:T(8,128)S(1)}) custom-call(f32[16,128,128]{2,1,0:T(8,128)S(1)} %all-to-all-done.1.refs_0_, bf16[3,2,2,128,128]{4,3,2,1,0:T(8,128)(2,1)S(1)} %get-tuple-element.19.refs_1_, s32[3]{0:T(128)S(1)} %pad_add_fusion.refs_2_.refs_0_), custom_call_target="tpu_custom_call" | custom-call | flops 402653184 | bytes 1835020 | tf_op jit(solution)/shard_map/pallas_call | solution.py:28
  82.9 12.2 %collective-permute-done.2 = f32[96,128]{1,0:T(8,128)S(1)} collective-permute-done((f32[96,128]{1,0:T(8,128)S(1)}, f32[96,128]{1,0:T(8,128)S(1)}, u32[]{:S(2)}, u32[]{:S(2)}) %collective-permute-start.2) | collective-permute-done | bytes 49184 | tf_op jit(solution)/shard_map/ppermute | solution.py:273
  95.1 4.2 %all-to-all-done.2.refs_0_ = f32[16,128,128]{2,1,0:T(8,128)S(1)} async-done(((f32[16,128,128]{2,1,0:T(8,128)}), f32[16,128,128]{2,1,0:T(8,128)S(1)}, u32[]{:S(2)}, u32[]{:S(2)}) %all-to-all-start.2) | async-done | bytes 1048608 | tf_op jit(solution)/shard_map/all_to_all | solution.py:292
  99.3 3.1 %shard_map.64 = f32[16,128,128]{2,1,0:T(8,128)} custom-call(f32[16,128,128]{2,1,0:T(8,128)S(1)} %all-to-all-done.2.refs_0_, bf16[3,2,2,128,128]{4,3,2,1,0:T(8,128)(2,1)S(1)} %get-tuple-element.22.refs_1_, f32[96,128]{1,0:T(8,128)S(1)} %slice_add_fusion.6.refs_2_.refs_3_, f32[192,128]{1,0:T(8,128)S(1)} %slice_add_fusion.2.refs_3_), custom_call_target="tpu_custom_call" | custom-call | flops 402653184 | bytes 2490368 | tf_op jit(solution)/shard_map/pallas_call | solution.py:28
  102.4 6.5 %all-to-all-start.3 = ((f32[16,128,128]{2,1,0:T(8,128)}), f32[16,128,128]{2,1,0:T(8,128)S(1)}, u32[]{:S(2)}, u32[]{:S(2)}) async-start(f32[16,128,128]{2,1,0:T(8,128)} %shard_map.64), calls=%async_computation.3 | async-start | bytes 2097152 | tf_op jit(solution)/shard_map/all_to_all | solution.py:292
  108.9 3.2 %shard_map.65 = (f32[384,128]{1,0:T(8,128)S(1)}, f32[384,128]{1,0:T(8,128)S(1)}) custom-call(f32[16,128,128]{2,1,0:T(8,128)S(1)} %all-to-all-done.2.refs_0_, bf16[3,2,2,128,128]{4,3,2,1,0:T(8,128)(2,1)S(1)} %get-tuple-element.22.refs_1_, s32[3]{0:T(128)S(1)} %pad_add_fusion.refs_2_.refs_0_), custom_call_target="tpu_custom_call" | custom-call | flops 402653184 | bytes 1835020 | tf_op jit(solution)/shard_map/pallas_call | solution.py:28
  115.8 12.2 %collective-permute-done.5 = f32[96,128]{1,0:T(8,128)S(1)} collective-permute-done((f32[96,128]{1,0:T(8,128)S(1)}, f32[96,128]{1,0:T(8,128)S(1)}, u32[]{:S(2)}, u32[]{:S(2)}) %collective-permute-start.5) | collective-permute-done | bytes 49184 | tf_op jit(solution)/shard_map/ppermute | solution.py:273
  128.0 2.5 %collective-permute-start.8 = (f32[96,128]{1,0:T(8,128)S(1)}, f32[96,128]{1,0:T(8,128)S(1)}, u32[]{:S(2)}, u32[]{:S(2)}) collective-permute-start(f32[96,128]{1,0:T(8,128)S(1)} %slice.67), channel_id=1, source_target_pairs={{0,4},{1,5},{2,6},{3,7},{4,0},{5,1},{6,2},{7,3},{8,12},{9,13},{10,... | collective-permute-start | bytes 147464 | tf_op jit(solution)/shard_map/ppermute | solution.py:273
  130.6 2.1 %collective-permute-start.15 = (f32[192,128]{1,0:T(8,128)S(1)}, f32[192,128]{1,0:T(8,128)S(1)}, u32[]{:S(2)}, u32[]{:S(2)}) collective-permute-start(f32[192,128]{1,0:T(8,128)S(1)} %pad_maximum_fusion.4), channel_id=1, source_target_pairs={{0,8},{1,9},{2,10},{3,11},{4,12},{5,13},{6,14},{7,15},{8,0},{9,1},... | collective-permute-start | bytes 294920 | tf_op jit(solution)/shard_map/ppermute | solution.py:273
  133.7 3.2 %shard_map.67 = (f32[384,128]{1,0:T(8,128)S(1)}, f32[384,128]{1,0:T(8,128)S(1)}) custom-call(f32[16,128,128]{2,1,0:T(8,128)S(1)} %all-to-all-done.3.refs_0_, bf16[3,2,2,128,128]{4,3,2,1,0:T(8,128)(2,1)S(1)} %get-tuple-element.25.refs_1_, s32[3]{0:T(128)S(1)} %pad_add_fusion.refs_2_.refs_0_, f32[96,128]{1,0:T(8,128)S(1)} %slice_add_fusion.6.refs_2_.refs_3_, ...), custom_call_target="tpu_custom_call" | custom-call | flops 402653184 | bytes 1835020 | tf_op jit(solution)/shard_map/pallas_call | solution.py:28
  137.0 2.6 %collective-permute-done.15 = f32[192,128]{1,0:T(8,128)S(1)} collective-permute-done((f32[192,128]{1,0:T(8,128)S(1)}, f32[192,128]{1,0:T(8,128)S(1)}, u32[]{:S(2)}, u32[]{:S(2)}) %collective-permute-start.15) | collective-permute-done | bytes 98336 | tf_op jit(solution)/shard_map/ppermute | solution.py:273
  139.8 2.1 %collective-permute-start.19 = (f32[96,128]{1,0:T(8,128)S(1)}, f32[96,128]{1,0:T(8,128)S(1)}, u32[]{:S(2)}, u32[]{:S(2)}) collective-permute-start(f32[96,128]{1,0:T(8,128)S(1)} %slice_add_fusion.4.refs_4_.refs_5_), channel_id=1, source_target_pairs={{0,8},{1,9},{2,10},{3,11},{4,12},{5,13},{6,14},{7,15},{8,0},{9,1},... | collective-permute-start | bytes 147464 | tf_op jit(solution)/shard_map/ppermute | solution.py:273
  141.9 2.6 %collective-permute-start.10 = (f32[192,128]{1,0:T(8,128)S(1)}, f32[192,128]{1,0:T(8,128)S(1)}, u32[]{:S(2)}, u32[]{:S(2)}) collective-permute-start(f32[192,128]{1,0:T(8,128)S(1)} %slice.69), channel_id=1, source_target_pairs={{0,2},{1,3},{2,0},{3,1},{4,6},{5,7},{6,4},{7,5},{8,10},{9,11},{10,... | collective-permute-start | bytes 294920 | tf_op jit(solution)/shard_map/ppermute | solution.py:273
  146.3 2.3 %collective-permute-start.20 = (f32[96,128]{1,0:T(8,128)S(1)}, f32[96,128]{1,0:T(8,128)S(1)}, u32[]{:S(2)}, u32[]{:S(2)}) collective-permute-start(f32[96,128]{1,0:T(8,128)S(1)} %add.55), channel_id=1, source_target_pairs={{0,4},{1,5},{2,6},{3,7},{4,0},{5,1},{6,2},{7,3},{8,12},{9,13},{10,... | collective-permute-start | bytes 147464 | tf_op jit(solution)/shard_map/ppermute | solution.py:273
  148.7 1.7 %collective-permute-start.11 = (f32[192,128]{1,0:T(8,128)S(1)}, f32[192,128]{1,0:T(8,128)S(1)}, u32[]{:S(2)}, u32[]{:S(2)}) collective-permute-start(f32[192,128]{1,0:T(8,128)S(1)} %slice_add_fusion), channel_id=1, source_target_pairs={{0,8},{1,9},{2,10},{3,11},{4,12},{5,13},{6,14},{7,15},{8,0},{9,1},... | collective-permute-start | bytes 294920 | tf_op jit(solution)/shard_map/ppermute | solution.py:273
  150.7 2.1 %collective-permute-start.21 = (f32[192,128]{1,0:T(8,128)S(1)}, f32[192,128]{1,0:T(8,128)S(1)}, u32[]{:S(2)}, u32[]{:S(2)}) collective-permute-start(f32[192,128]{1,0:T(8,128)S(1)} %pad_maximum_fusion.5), channel_id=1, source_target_pairs={{0,2},{1,3},{2,0},{3,1},{4,6},{5,7},{6,4},{7,5},{8,10},{9,11},{10,... | collective-permute-start | bytes 294920 | tf_op jit(solution)/shard_map/ppermute | solution.py:273
  152.8 1.9 %collective-permute-done.11 = f32[192,128]{1,0:T(8,128)S(1)} collective-permute-done((f32[192,128]{1,0:T(8,128)S(1)}, f32[192,128]{1,0:T(8,128)S(1)}, u32[]{:S(2)}, u32[]{:S(2)}) %collective-permute-start.11) | collective-permute-done | bytes 98336 | tf_op jit(solution)/shard_map/ppermute | solution.py:273
  155.0 3.1 %shard_map.66 = (f32[1024,128]{1,0:T(8,128)}, f32[1024,128]{1,0:T(8,128)}, f32[8,128]{1,0:T(8,128)S(1)}) custom-call(f32[16,128,128]{2,1,0:T(8,128)S(1)} %all-to-all-done.3.refs_0_, bf16[3,2,2,128,128]{4,3,2,1,0:T(8,128)(2,1)S(1)} %get-tuple-element.25.refs_1_, f32[96,128]{1,0:T(8,128)S(1)} %slice_add_fusion.6.refs_2_.refs_3_, ...), custom_call_target="tpu_custom_call" | custom-call | flops 402653184 | bytes 2494464 | tf_op jit(solution)/shard_map/pallas_call | solution.py:28
  159.5 1.8 %collective-permute-start.13 = (f32[192,128]{1,0:T(8,128)S(1)}, f32[192,128]{1,0:T(8,128)S(1)}, u32[]{:S(2)}, u32[]{:S(2)}) collective-permute-start(f32[192,128]{1,0:T(8,128)S(1)} %shard_map.68), channel_id=1, source_target_pairs={{0,2},{1,3},{2,0},{3,1},{4,6},{5,7},{6,4},{7,5},{8,10},{9,11},{10,... | collective-permute-start | bytes 294920 | tf_op jit(solution)/shard_map/ppermute | solution.py:273
  161.4 2.8 %collective-permute-done.13 = f32[192,128]{1,0:T(8,128)S(1)} collective-permute-done((f32[192,128]{1,0:T(8,128)S(1)}, f32[192,128]{1,0:T(8,128)S(1)}, u32[]{:S(2)}, u32[]{:S(2)}) %collective-permute-start.13) | collective-permute-done | bytes 98336 | tf_op jit(solution)/shard_map/ppermute | solution.py:273
  164.3 1.8 %shard_map.69.refs_3_ = f32[4,768,128]{2,1,0:T(8,128)} custom-call(s32[3]{0:T(128)S(1)} %pad_add_fusion.refs_2_.refs_0_, f32[768,128]{1,0:T(8,128)S(1)} %pad_maximum_fusion.refs_1_, f32[768,128]{1,0:T(8,128)S(1)} %collective-permute-done.18.refs_2_, f32[384,128]{1,0:T(8,128)S(1)} %pad_maximum_fusion.3.refs_3_, f32[384,128]{1,0:T(8,128)S(1)} %collective-permute-done.22.refs_4_), custom_call_target="tpu_custom_call" | custom-call | bytes 2752524 | tf_op jit(solution)/shard_map/pallas_call | solution.py:28
  (69 shorter events, 19.6 us)
Async XLA Ops:
  2.8 30.3 %all-to-all-start = ((f32[16,128,128]{2,1,0:T(8,128)}), f32[16,128,128]{2,1,0:T(8,128)S(1)}, u32[]{:S(2)}, u32[]{:S(2)}) async-start(f32[16,128,128]{2,1,0:T(8,128)} %shard_map.58), calls=%async_computation | async-start | bytes 2097152 | tf_op jit(solution)/shard_map/all_to_all | solution.py:292
  10.2 1.4 copy-start
  13.0 23.2 %copy-start.1 = (bf16[3,2,2,128,128]{4,3,2,1,0:T(8,128)(2,1)}, bf16[3,2,2,128,128]{4,3,2,1,0:T(8,128)(2,1)S(1)}, u32[]{:S(2)}) copy-start(bf16[3,2,2,128,128]{4,3,2,1,0:T(8,128)(2,1)S(1)} %get-tuple-element.18.refs_1_) | copy-start | bytes 1179652
  36.2 29.8 %all-to-all-start.1 = ((f32[16,128,128]{2,1,0:T(8,128)}), f32[16,128,128]{2,1,0:T(8,128)S(1)}, u32[]{:S(2)}, u32[]{:S(2)}) async-start(f32[16,128,128]{2,1,0:T(8,128)} %shard_map.60), calls=%async_computation.1 | async-start | bytes 2097152 | tf_op jit(solution)/shard_map/all_to_all | solution.py:292
  43.2 1.0 copy-start.2
  47.4 1.5 collective-permute-start
  49.0 6.7 %collective-permute-start.1 = (f32[192,128]{1,0:T(8,128)S(1)}, f32[192,128]{1,0:T(8,128)S(1)}, u32[]{:S(2)}, u32[]{:S(2)}) collective-permute-start(f32[192,128]{1,0:T(8,128)S(1)} %slice.57), channel_id=1, source_target_pairs={{0,2},{1,3},{2,0},{3,1},{4,6},{5,7},{6,4},{7,5},{8,10},{9,11},{10,... | collective-permute-start | bytes 294920 | tf_op jit(solution)/shard_map/ppermute | solution.py:273
  69.1 30.2 %all-to-all-start.2 = ((f32[16,128,128]{2,1,0:T(8,128)}), f32[16,128,128]{2,1,0:T(8,128)S(1)}, u32[]{:S(2)}, u32[]{:S(2)}) async-start(f32[16,128,128]{2,1,0:T(8,128)} %shard_map.62), calls=%async_computation.2 | async-start | bytes 2097152 | tf_op jit(solution)/shard_map/all_to_all | solution.py:292
  79.2 2.2 %collective-permute-start.3 = (f32[384,128]{1,0:T(8,128)S(1)}, f32[384,128]{1,0:T(8,128)S(1)}, u32[]{:S(2)}, u32[]{:S(2)}) collective-permute-start(f32[384,128]{1,0:T(8,128)S(1)} %get-tuple-element.24), channel_id=1, source_target_pairs={{0,1},{1,0},{2,3},{3,2},{4,5},{5,4},{6,7},{7,6},{8,9},{9,8},{10,11... | collective-permute-start | bytes 589832 | tf_op jit(solution)/shard_map/ppermute | solution.py:273
  79.7 15.4 %collective-permute-start.2 = (f32[96,128]{1,0:T(8,128)S(1)}, f32[96,128]{1,0:T(8,128)S(1)}, u32[]{:S(2)}, u32[]{:S(2)}) collective-permute-start(f32[96,128]{1,0:T(8,128)S(1)} %slice.59), channel_id=1, source_target_pairs={{0,4},{1,5},{2,6},{3,7},{4,0},{5,1},{6,2},{7,3},{8,12},{9,13},{10,... | collective-permute-start | bytes 147464 | tf_op jit(solution)/shard_map/ppermute | solution.py:273
  81.4 13.7 %collective-permute-start.4 = (f32[192,128]{1,0:T(8,128)S(1)}, f32[192,128]{1,0:T(8,128)S(1)}, u32[]{:S(2)}, u32[]{:S(2)}) collective-permute-start(f32[192,128]{1,0:T(8,128)S(1)} %slice.61), channel_id=1, source_target_pairs={{0,2},{1,3},{2,0},{3,1},{4,6},{5,7},{6,4},{7,5},{8,10},{9,11},{10,... | collective-permute-start | bytes 294920 | tf_op jit(solution)/shard_map/ppermute | solution.py:273
  102.4 31.3 %all-to-all-start.3 = ((f32[16,128,128]{2,1,0:T(8,128)}), f32[16,128,128]{2,1,0:T(8,128)S(1)}, u32[]{:S(2)}, u32[]{:S(2)}) async-start(f32[16,128,128]{2,1,0:T(8,128)} %shard_map.64), calls=%async_computation.3 | async-start | bytes 2097152 | tf_op jit(solution)/shard_map/all_to_all | solution.py:292
  112.1 2.2 %collective-permute-start.6 = (f32[384,128]{1,0:T(8,128)S(1)}, f32[384,128]{1,0:T(8,128)S(1)}, u32[]{:S(2)}, u32[]{:S(2)}) collective-permute-start(f32[384,128]{1,0:T(8,128)S(1)} %get-tuple-element.27), channel_id=1, source_target_pairs={{0,1},{1,0},{2,3},{3,2},{4,5},{5,4},{6,7},{7,6},{8,9},{9,8},{10,11... | collective-permute-start | bytes 589832 | tf_op jit(solution)/shard_map/ppermute | solution.py:273
  112.6 15.4 %collective-permute-start.5 = (f32[96,128]{1,0:T(8,128)S(1)}, f32[96,128]{1,0:T(8,128)S(1)}, u32[]{:S(2)}, u32[]{:S(2)}) collective-permute-start(f32[96,128]{1,0:T(8,128)S(1)} %slice.63), channel_id=1, source_target_pairs={{0,4},{1,5},{2,6},{3,7},{4,0},{5,1},{6,2},{7,3},{8,12},{9,13},{10,... | collective-permute-start | bytes 147464 | tf_op jit(solution)/shard_map/ppermute | solution.py:273
  114.3 13.7 %collective-permute-start.7 = (f32[192,128]{1,0:T(8,128)S(1)}, f32[192,128]{1,0:T(8,128)S(1)}, u32[]{:S(2)}, u32[]{:S(2)}) collective-permute-start(f32[192,128]{1,0:T(8,128)S(1)} %slice.65), channel_id=1, source_target_pairs={{0,2},{1,3},{2,0},{3,1},{4,6},{5,7},{6,4},{7,5},{8,10},{9,11},{10,... | collective-permute-start | bytes 294920 | tf_op jit(solution)/shard_map/ppermute | solution.py:273
  128.0 5.7 %collective-permute-start.8 = (f32[96,128]{1,0:T(8,128)S(1)}, f32[96,128]{1,0:T(8,128)S(1)}, u32[]{:S(2)}, u32[]{:S(2)}) collective-permute-start(f32[96,128]{1,0:T(8,128)S(1)} %slice.67), channel_id=1, source_target_pairs={{0,4},{1,5},{2,6},{3,7},{4,0},{5,1},{6,2},{7,3},{8,12},{9,13},{10,... | collective-permute-start | bytes 147464 | tf_op jit(solution)/shard_map/ppermute | solution.py:273
  130.6 9.1 %collective-permute-start.15 = (f32[192,128]{1,0:T(8,128)S(1)}, f32[192,128]{1,0:T(8,128)S(1)}, u32[]{:S(2)}, u32[]{:S(2)}) collective-permute-start(f32[192,128]{1,0:T(8,128)S(1)} %pad_maximum_fusion.4), channel_id=1, source_target_pairs={{0,8},{1,9},{2,10},{3,11},{4,12},{5,13},{6,14},{7,15},{8,0},{9,1},... | collective-permute-start | bytes 294920 | tf_op jit(solution)/shard_map/ppermute | solution.py:273
  136.9 4.9 %collective-permute-start.9 = (f32[384,128]{1,0:T(8,128)S(1)}, f32[384,128]{1,0:T(8,128)S(1)}, u32[]{:S(2)}, u32[]{:S(2)}) collective-permute-start(f32[384,128]{1,0:T(8,128)S(1)} %get-tuple-element.31), channel_id=1, source_target_pairs={{0,1},{1,0},{2,3},{3,2},{4,5},{5,4},{6,7},{7,6},{8,9},{9,8},{10,11... | collective-permute-start | bytes 589832 | tf_op jit(solution)/shard_map/ppermute | solution.py:273
  139.7 5.5 %collective-permute-start.16 = (f32[192,128]{1,0:T(8,128)S(1)}, f32[192,128]{1,0:T(8,128)S(1)}, u32[]{:S(2)}, u32[]{:S(2)}) collective-permute-start(f32[192,128]{1,0:T(8,128)S(1)} %fusion), channel_id=1, source_target_pairs={{0,4},{1,5},{2,6},{3,7},{4,0},{5,1},{6,2},{7,3},{8,12},{9,13},{10,... | collective-permute-start | bytes 294920 | tf_op jit(solution)/shard_map/ppermute | solution.py:273
  139.8 6.6 %collective-permute-start.19 = (f32[96,128]{1,0:T(8,128)S(1)}, f32[96,128]{1,0:T(8,128)S(1)}, u32[]{:S(2)}, u32[]{:S(2)}) collective-permute-start(f32[96,128]{1,0:T(8,128)S(1)} %slice_add_fusion.4.refs_4_.refs_5_), channel_id=1, source_target_pairs={{0,8},{1,9},{2,10},{3,11},{4,12},{5,13},{6,14},{7,15},{8,0},{9,1},... | collective-permute-start | bytes 147464 | tf_op jit(solution)/shard_map/ppermute | solution.py:273
  141.9 6.8 %collective-permute-start.10 = (f32[192,128]{1,0:T(8,128)S(1)}, f32[192,128]{1,0:T(8,128)S(1)}, u32[]{:S(2)}, u32[]{:S(2)}) collective-permute-start(f32[192,128]{1,0:T(8,128)S(1)} %slice.69), channel_id=1, source_target_pairs={{0,2},{1,3},{2,0},{3,1},{4,6},{5,7},{6,4},{7,5},{8,10},{9,11},{10,... | collective-permute-start | bytes 294920 | tf_op jit(solution)/shard_map/ppermute | solution.py:273
  145.2 9.7 %collective-permute-start.17 = (f32[384,128]{1,0:T(8,128)S(1)}, f32[384,128]{1,0:T(8,128)S(1)}, u32[]{:S(2)}, u32[]{:S(2)}) collective-permute-start(f32[384,128]{1,0:T(8,128)S(1)} %pad_maximum_fusion.2), channel_id=1, source_target_pairs={{0,2},{1,3},{2,0},{3,1},{4,6},{5,7},{6,4},{7,5},{8,10},{9,11},{10,... | collective-permute-start | bytes 589832 | tf_op jit(solution)/shard_map/ppermute | solution.py:273
  146.3 4.4 %collective-permute-start.20 = (f32[96,128]{1,0:T(8,128)S(1)}, f32[96,128]{1,0:T(8,128)S(1)}, u32[]{:S(2)}, u32[]{:S(2)}) collective-permute-start(f32[96,128]{1,0:T(8,128)S(1)} %add.55), channel_id=1, source_target_pairs={{0,4},{1,5},{2,6},{3,7},{4,0},{5,1},{6,2},{7,3},{8,12},{9,13},{10,... | collective-permute-start | bytes 147464 | tf_op jit(solution)/shard_map/ppermute | solution.py:273
  148.7 6.1 %collective-permute-start.11 = (f32[192,128]{1,0:T(8,128)S(1)}, f32[192,128]{1,0:T(8,128)S(1)}, u32[]{:S(2)}, u32[]{:S(2)}) collective-permute-start(f32[192,128]{1,0:T(8,128)S(1)} %slice_add_fusion), channel_id=1, source_target_pairs={{0,8},{1,9},{2,10},{3,11},{4,12},{5,13},{6,14},{7,15},{8,0},{9,1},... | collective-permute-start | bytes 294920 | tf_op jit(solution)/shard_map/ppermute | solution.py:273
  150.7 10.6 %collective-permute-start.21 = (f32[192,128]{1,0:T(8,128)S(1)}, f32[192,128]{1,0:T(8,128)S(1)}, u32[]{:S(2)}, u32[]{:S(2)}) collective-permute-start(f32[192,128]{1,0:T(8,128)S(1)} %pad_maximum_fusion.5), channel_id=1, source_target_pairs={{0,2},{1,3},{2,0},{3,1},{4,6},{5,7},{6,4},{7,5},{8,10},{9,11},{10,... | collective-permute-start | bytes 294920 | tf_op jit(solution)/shard_map/ppermute | solution.py:273
  154.8 4.7 %collective-permute-start.12 = (f32[192,128]{1,0:T(8,128)S(1)}, f32[192,128]{1,0:T(8,128)S(1)}, u32[]{:S(2)}, u32[]{:S(2)}) collective-permute-start(f32[192,128]{1,0:T(8,128)S(1)} %add.53.refs_0_), channel_id=1, source_target_pairs={{0,4},{1,5},{2,6},{3,7},{4,0},{5,1},{6,2},{7,3},{8,12},{9,13},{10,... | collective-permute-start | bytes 294920 | tf_op jit(solution)/shard_map/ppermute | solution.py:273
  154.9 9.4 %collective-permute-start.18 = (f32[768,128]{1,0:T(8,128)S(1)}, f32[768,128]{1,0:T(8,128)S(1)}, u32[]{:S(2)}, u32[]{:S(2)}) collective-permute-start(f32[768,128]{1,0:T(8,128)S(1)} %pad_maximum_fusion.refs_1_), channel_id=1, source_target_pairs={{0,1},{1,0},{2,3},{3,2},{4,5},{5,4},{6,7},{7,6},{8,9},{9,8},{10,11... | collective-permute-start | bytes 1179656 | tf_op jit(solution)/shard_map/ppermute | solution.py:273
  159.5 4.7 %collective-permute-start.13 = (f32[192,128]{1,0:T(8,128)S(1)}, f32[192,128]{1,0:T(8,128)S(1)}, u32[]{:S(2)}, u32[]{:S(2)}) collective-permute-start(f32[192,128]{1,0:T(8,128)S(1)} %shard_map.68), channel_id=1, source_target_pairs={{0,2},{1,3},{2,0},{3,1},{4,6},{5,7},{6,4},{7,5},{8,10},{9,11},{10,... | collective-permute-start | bytes 294920 | tf_op jit(solution)/shard_map/ppermute | solution.py:273
  161.3 3.0 %collective-permute-start.22 = (f32[384,128]{1,0:T(8,128)S(1)}, f32[384,128]{1,0:T(8,128)S(1)}, u32[]{:S(2)}, u32[]{:S(2)}) collective-permute-start(f32[384,128]{1,0:T(8,128)S(1)} %pad_maximum_fusion.3.refs_3_), channel_id=1, source_target_pairs={{0,1},{1,0},{2,3},{3,2},{4,5},{5,4},{6,7},{7,6},{8,9},{9,8},{10,11... | collective-permute-start | bytes 589832 | tf_op jit(solution)/shard_map/ppermute | solution.py:273
  164.2 1.9 %collective-permute-start.14 = (f32[384,128]{1,0:T(8,128)S(1)}, f32[384,128]{1,0:T(8,128)S(1)}, u32[]{:S(2)}, u32[]{:S(2)}) collective-permute-start(f32[384,128]{1,0:T(8,128)S(1)} %pad_maximum_fusion.1.refs_1_), channel_id=1, source_target_pairs={{0,1},{1,0},{2,3},{3,2},{4,5},{5,4},{6,7},{7,6},{8,9},{9,8},{10,11... | collective-permute-start | bytes 589832 | tf_op jit(solution)/shard_map/ppermute | solution.py:273

commit v5 on v4

--- a/solution.py
+++ b/solution.py
@@ -306,7 +306,7 @@
     rows = blocks * gate
     flat = jax.ShapeDtypeStruct((2 * rows, gate), F32)
     tiled = jax.ShapeDtypeStruct((tiles, 4 * blocks * TILE, gate), F32)
-    work = 48 * local_size * gate
+    work = 72 * local_size * gate
 
     matrices = call(
         functools.partial(prepare_body, rounds, gate, blocks),
@@ -351,7 +351,7 @@
             functools.partial(gradient_body, gate, blocks, factor, early_depth if number > 0 else late_depth),
             [jax.ShapeDtypeStruct((3 * gate, gate), F32)] * 2,
             (x, matrices[number], bits),
-            work,
+            0,
             [VMEM, VMEM, SMEM],
             scratch=[pltpu.VMEM((6 * gate, gate), F32)],
             after=totals if number == 0 else (),
@@ -365,7 +365,7 @@
                 functools.partial(undo_body, gate, blocks),
                 tiled,
                 (x, matrices[number]),
-                work,
+                0,
                 out_spec=ANY,
                 scratch=[pltpu.VMEM(tiled.shape, F32), pltpu.SemaphoreType.DMA((2,))],
                 after=totals,

time: 168 us -> 168 us (level)
  no operation moved by 1% of the time
where the time goes in v5:
time: 168 us
  waiting for transfers between devices  75.9 us (45%)
  starting transfers between devices  56.3 us (34%)
  Pallas kernels  31.7 us (19%)
  local copies, waits for them, and re-layouts  2.2 us (1%)
    ppermute x23, waiting for transfers between devices, exchange(): return lax.ppermute(x, 'qa', [(i, i ^ step) for i in range(shards)])  41.6 us
    all_to_all x4, waiting for transfers between devices, swapped(): x = lax.all_to_all(x, 'qa', split_axis=0, concat_axis=0, tiled=True)  34.3 us
    pallas_call x13, Pallas kernels, call(): pl.pallas_call(whole, out_shape=out_shape, in_specs=[*(in_specs or [VMEM]...  31.7 us
    ppermute x23, starting transfers between devices, exchange(): return lax.ppermute(x, 'qa', [(i, i ^ step) for i in range(shards)])  28.6 us
    all_to_all x4, starting transfers between devices, swapped(): x = lax.all_to_all(x, 'qa', split_axis=0, concat_axis=0, tiled=True)  27.7 us
  transfers between devices with their start and end apart: 27, of which 14 were waited for; matrix products, arithmetic and copies ran while one was open for 0% of the time, Pallas kernels for 11%

profile of v5, /device:TPU:0, one launch (start us, length us, event | category | flops | bytes accessed | tf_op | source)
XLA Modules:
  0.0 167.6 jit_solution(15079431769968588498)
XLA Ops:
  0.6 2.1 %shard_map.58 = f32[16,128,128]{2,1,0:T(8,128)} custom-call(f32[1024,128]{1,0:T(8,128)} %bitcast.25, f32[1024,128]{1,0:T(8,128)} %bitcast.26), custom_call_target="tpu_custom_call" | custom-call | bytes 2097152 | tf_op jit(solution)/shard_map/pallas_call | solution.py:28
  2.8 7.4 %all-to-all-start = ((f32[16,128,128]{2,1,0:T(8,128)}), f32[16,128,128]{2,1,0:T(8,128)S(1)}, u32[]{:S(2)}, u32[]{:S(2)}) async-start(f32[16,128,128]{2,1,0:T(8,128)} %shard_map.58), calls=%async_computation | async-start | bytes 2097152 | tf_op jit(solution)/shard_map/all_to_all | solution.py:292
  13.7 19.4 %all-to-all-done.refs_0_ = f32[16,128,128]{2,1,0:T(8,128)S(1)} async-done(((f32[16,128,128]{2,1,0:T(8,128)}), f32[16,128,128]{2,1,0:T(8,128)S(1)}, u32[]{:S(2)}, u32[]{:S(2)}) %all-to-all-start) | async-done | bytes 1048608 | tf_op jit(solution)/shard_map/all_to_all | solution.py:292
  33.1 3.1 %shard_map.60 = f32[16,128,128]{2,1,0:T(8,128)} custom-call(f32[16,128,128]{2,1,0:T(8,128)S(1)} %all-to-all-done.refs_0_, bf16[3,2,2,128,128]{4,3,2,1,0:T(8,128)(2,1)S(1)} %get-tuple-element.18.refs_1_), custom_call_target="tpu_custom_call" | custom-call | bytes 2490368 | tf_op jit(solution)/shard_map/pallas_call | solution.py:28
  36.2 6.9 %all-to-all-start.1 = ((f32[16,128,128]{2,1,0:T(8,128)}), f32[16,128,128]{2,1,0:T(8,128)S(1)}, u32[]{:S(2)}, u32[]{:S(2)}) async-start(f32[16,128,128]{2,1,0:T(8,128)} %shard_map.60), calls=%async_computation.1 | async-start | bytes 2097152 | tf_op jit(solution)/shard_map/all_to_all | solution.py:292
  43.2 3.2 %shard_map.61 = (f32[384,128]{1,0:T(8,128)S(1)}, f32[384,128]{1,0:T(8,128)S(1)}) custom-call(f32[16,128,128]{2,1,0:T(8,128)S(1)} %all-to-all-done.refs_0_, bf16[3,2,2,128,128]{4,3,2,1,0:T(8,128)(2,1)S(1)} %get-tuple-element.18.refs_1_, s32[3]{0:T(128)S(1)} %pad_add_fusion.refs_2_.refs_0_), custom_call_target="tpu_custom_call" | custom-call | bytes 1835020 | tf_op jit(solution)/shard_map/pallas_call | solution.py:28
  48.0 2.0 %collective-permute-start.1 = (f32[192,128]{1,0:T(8,128)S(1)}, f32[192,128]{1,0:T(8,128)S(1)}, u32[]{:S(2)}, u32[]{:S(2)}) collective-permute-start(f32[192,128]{1,0:T(8,128)S(1)} %slice.57), channel_id=1, source_target_pairs={{0,2},{1,3},{2,0},{3,1},{4,6},{5,7},{6,4},{7,5},{8,10},{9,11},{10,... | collective-permute-start | bytes 294920 | tf_op jit(solution)/shard_map/ppermute | solution.py:273
  49.9 5.4 %collective-permute-done.1 = f32[192,128]{1,0:T(8,128)S(1)} collective-permute-done((f32[192,128]{1,0:T(8,128)S(1)}, f32[192,128]{1,0:T(8,128)S(1)}, u32[]{:S(2)}, u32[]{:S(2)}) %collective-permute-start.1) | collective-permute-done | bytes 98336 | tf_op jit(solution)/shard_map/ppermute | solution.py:273
  55.3 10.7 %all-to-all-done.1.refs_0_ = f32[16,128,128]{2,1,0:T(8,128)S(1)} async-done(((f32[16,128,128]{2,1,0:T(8,128)}), f32[16,128,128]{2,1,0:T(8,128)S(1)}, u32[]{:S(2)}, u32[]{:S(2)}) %all-to-all-start.1) | async-done | bytes 1048608 | tf_op jit(solution)/shard_map/all_to_all | solution.py:292
  66.0 3.1 %shard_map.62 = f32[16,128,128]{2,1,0:T(8,128)} custom-call(f32[16,128,128]{2,1,0:T(8,128)S(1)} %all-to-all-done.1.refs_0_, bf16[3,2,2,128,128]{4,3,2,1,0:T(8,128)(2,1)S(1)} %get-tuple-element.19.refs_1_, f32[192,128]{1,0:T(8,128)S(1)} %slice_add_fusion.3.refs_2_), custom_call_target="tpu_custom_call" | custom-call | bytes 2490368 | tf_op jit(solution)/shard_map/pallas_call | solution.py:28
  69.1 6.9 %all-to-all-start.2 = ((f32[16,128,128]{2,1,0:T(8,128)}), f32[16,128,128]{2,1,0:T(8,128)S(1)}, u32[]{:S(2)}, u32[]{:S(2)}) async-start(f32[16,128,128]{2,1,0:T(8,128)} %shard_map.62), calls=%async_computation.2 | async-start | bytes 2097152 | tf_op jit(solution)/shard_map/all_to_all | solution.py:292
  76.0 3.2 %shard_map.63 = (f32[384,128]{1,0:T(8,128)S(1)}, f32[384,128]{1,0:T(8,128)S(1)}) custom-call(f32[16,128,128]{2,1,0:T(8,128)S(1)} %all-to-all-done.1.refs_0_, bf16[3,2,2,128,128]{4,3,2,1,0:T(8,128)(2,1)S(1)} %get-tuple-element.19.refs_1_, s32[3]{0:T(128)S(1)} %pad_add_fusion.refs_2_.refs_0_), custom_call_target="tpu_custom_call" | custom-call | bytes 1835020 | tf_op jit(solution)/shard_map/pallas_call | solution.py:28
  82.9 12.2 %collective-permute-done.2 = f32[96,128]{1,0:T(8,128)S(1)} collective-permute-done((f32[96,128]{1,0:T(8,128)S(1)}, f32[96,128]{1,0:T(8,128)S(1)}, u32[]{:S(2)}, u32[]{:S(2)}) %collective-permute-start.2) | collective-permute-done | bytes 49184 | tf_op jit(solution)/shard_map/ppermute | solution.py:273
  95.1 4.2 %all-to-all-done.2.refs_0_ = f32[16,128,128]{2,1,0:T(8,128)S(1)} async-done(((f32[16,128,128]{2,1,0:T(8,128)}), f32[16,128,128]{2,1,0:T(8,128)S(1)}, u32[]{:S(2)}, u32[]{:S(2)}) %all-to-all-start.2) | async-done | bytes 1048608 | tf_op jit(solution)/shard_map/all_to_all | solution.py:292
  99.3 3.1 %shard_map.64 = f32[16,128,128]{2,1,0:T(8,128)} custom-call(f32[16,128,128]{2,1,0:T(8,128)S(1)} %all-to-all-done.2.refs_0_, bf16[3,2,2,128,128]{4,3,2,1,0:T(8,128)(2,1)S(1)} %get-tuple-element.22.refs_1_, f32[96,128]{1,0:T(8,128)S(1)} %slice_add_fusion.6.refs_2_.refs_3_, f32[192,128]{1,0:T(8,128)S(1)} %slice_add_fusion.2.refs_3_), custom_call_target="tpu_custom_call" | custom-call | bytes 2490368 | tf_op jit(solution)/shard_map/pallas_call | solution.py:28
  102.4 6.5 %all-to-all-start.3 = ((f32[16,128,128]{2,1,0:T(8,128)}), f32[16,128,128]{2,1,0:T(8,128)S(1)}, u32[]{:S(2)}, u32[]{:S(2)}) async-start(f32[16,128,128]{2,1,0:T(8,128)} %shard_map.64), calls=%async_computation.3 | async-start | bytes 2097152 | tf_op jit(solution)/shard_map/all_to_all | solution.py:292
  108.9 3.2 %shard_map.65 = (f32[384,128]{1,0:T(8,128)S(1)}, f32[384,128]{1,0:T(8,128)S(1)}) custom-call(f32[16,128,128]{2,1,0:T(8,128)S(1)} %all-to-all-done.2.refs_0_, bf16[3,2,2,128,128]{4,3,2,1,0:T(8,128)(2,1)S(1)} %get-tuple-element.22.refs_1_, s32[3]{0:T(128)S(1)} %pad_add_fusion.refs_2_.refs_0_), custom_call_target="tpu_custom_call" | custom-call | bytes 1835020 | tf_op jit(solution)/shard_map/pallas_call | solution.py:28
  115.8 12.1 %collective-permute-done.5 = f32[96,128]{1,0:T(8,128)S(1)} collective-permute-done((f32[96,128]{1,0:T(8,128)S(1)}, f32[96,128]{1,0:T(8,128)S(1)}, u32[]{:S(2)}, u32[]{:S(2)}) %collective-permute-start.5) | collective-permute-done | bytes 49184 | tf_op jit(solution)/shard_map/ppermute | solution.py:273
  128.0 2.5 %collective-permute-start.8 = (f32[96,128]{1,0:T(8,128)S(1)}, f32[96,128]{1,0:T(8,128)S(1)}, u32[]{:S(2)}, u32[]{:S(2)}) collective-permute-start(f32[96,128]{1,0:T(8,128)S(1)} %slice.67), channel_id=1, source_target_pairs={{0,4},{1,5},{2,6},{3,7},{4,0},{5,1},{6,2},{7,3},{8,12},{9,13},{10,... | collective-permute-start | bytes 147464 | tf_op jit(solution)/shard_map/ppermute | solution.py:273
  130.6 2.1 %collective-permute-start.15 = (f32[192,128]{1,0:T(8,128)S(1)}, f32[192,128]{1,0:T(8,128)S(1)}, u32[]{:S(2)}, u32[]{:S(2)}) collective-permute-start(f32[192,128]{1,0:T(8,128)S(1)} %pad_maximum_fusion.4), channel_id=1, source_target_pairs={{0,8},{1,9},{2,10},{3,11},{4,12},{5,13},{6,14},{7,15},{8,0},{9,1},... | collective-permute-start | bytes 294920 | tf_op jit(solution)/shard_map/ppermute | solution.py:273
  133.7 3.2 %shard_map.67 = (f32[384,128]{1,0:T(8,128)S(1)}, f32[384,128]{1,0:T(8,128)S(1)}) custom-call(f32[16,128,128]{2,1,0:T(8,128)S(1)} %all-to-all-done.3.refs_0_, bf16[3,2,2,128,128]{4,3,2,1,0:T(8,128)(2,1)S(1)} %copy-done.2, s32[3]{0:T(128)S(1)} %pad_add_fusion.refs_2_.refs_0_, f32[96,128]{1,0:T(8,128)S(1)} %slice_add_fusion.6.refs_2_.refs_3_, ...), custom_call_target="tpu_custom_call" | custom-call | bytes 1835020 | tf_op jit(solution)/shard_map/pallas_call | solution.py:28
  137.0 2.6 %collective-permute-done.15 = f32[192,128]{1,0:T(8,128)S(1)} collective-permute-done((f32[192,128]{1,0:T(8,128)S(1)}, f32[192,128]{1,0:T(8,128)S(1)}, u32[]{:S(2)}, u32[]{:S(2)}) %collective-permute-start.15) | collective-permute-done | bytes 98336 | tf_op jit(solution)/shard_map/ppermute | solution.py:273
  139.7 2.0 %collective-permute-start.19 = (f32[96,128]{1,0:T(8,128)S(1)}, f32[96,128]{1,0:T(8,128)S(1)}, u32[]{:S(2)}, u32[]{:S(2)}) collective-permute-start(f32[96,128]{1,0:T(8,128)S(1)} %slice_add_fusion.4.refs_4_.refs_5_), channel_id=1, source_target_pairs={{0,8},{1,9},{2,10},{3,11},{4,12},{5,13},{6,14},{7,15},{8,0},{9,1},... | collective-permute-start | bytes 147464 | tf_op jit(solution)/shard_map/ppermute | solution.py:273
  141.8 2.6 %collective-permute-start.10 = (f32[192,128]{1,0:T(8,128)S(1)}, f32[192,128]{1,0:T(8,128)S(1)}, u32[]{:S(2)}, u32[]{:S(2)}) collective-permute-start(f32[192,128]{1,0:T(8,128)S(1)} %slice.69), channel_id=1, source_target_pairs={{0,2},{1,3},{2,0},{3,1},{4,6},{5,7},{6,4},{7,5},{8,10},{9,11},{10,... | collective-permute-start | bytes 294920 | tf_op jit(solution)/shard_map/ppermute | solution.py:273
  146.3 2.3 %collective-permute-start.20 = (f32[96,128]{1,0:T(8,128)S(1)}, f32[96,128]{1,0:T(8,128)S(1)}, u32[]{:S(2)}, u32[]{:S(2)}) collective-permute-start(f32[96,128]{1,0:T(8,128)S(1)} %add.55), channel_id=1, source_target_pairs={{0,4},{1,5},{2,6},{3,7},{4,0},{5,1},{6,2},{7,3},{8,12},{9,13},{10,... | collective-permute-start | bytes 147464 | tf_op jit(solution)/shard_map/ppermute | solution.py:273
  148.7 1.7 %collective-permute-start.11 = (f32[192,128]{1,0:T(8,128)S(1)}, f32[192,128]{1,0:T(8,128)S(1)}, u32[]{:S(2)}, u32[]{:S(2)}) collective-permute-start(f32[192,128]{1,0:T(8,128)S(1)} %slice_add_fusion), channel_id=1, source_target_pairs={{0,8},{1,9},{2,10},{3,11},{4,12},{5,13},{6,14},{7,15},{8,0},{9,1},... | collective-permute-start | bytes 294920 | tf_op jit(solution)/shard_map/ppermute | solution.py:273
  150.7 2.1 %collective-permute-start.21 = (f32[192,128]{1,0:T(8,128)S(1)}, f32[192,128]{1,0:T(8,128)S(1)}, u32[]{:S(2)}, u32[]{:S(2)}) collective-permute-start(f32[192,128]{1,0:T(8,128)S(1)} %pad_maximum_fusion.5), channel_id=1, source_target_pairs={{0,2},{1,3},{2,0},{3,1},{4,6},{5,7},{6,4},{7,5},{8,10},{9,11},{10,... | collective-permute-start | bytes 294920 | tf_op jit(solution)/shard_map/ppermute | solution.py:273
  152.8 1.9 %collective-permute-done.11 = f32[192,128]{1,0:T(8,128)S(1)} collective-permute-done((f32[192,128]{1,0:T(8,128)S(1)}, f32[192,128]{1,0:T(8,128)S(1)}, u32[]{:S(2)}, u32[]{:S(2)}) %collective-permute-start.11) | collective-permute-done | bytes 98336 | tf_op jit(solution)/shard_map/ppermute | solution.py:273
  155.0 3.1 %shard_map.66 = (f32[1024,128]{1,0:T(8,128)}, f32[1024,128]{1,0:T(8,128)}, f32[8,128]{1,0:T(8,128)S(1)}) custom-call(f32[16,128,128]{2,1,0:T(8,128)S(1)} %all-to-all-done.3.refs_0_, bf16[3,2,2,128,128]{4,3,2,1,0:T(8,128)(2,1)S(1)} %copy-done.2, f32[96,128]{1,0:T(8,128)S(1)} %slice_add_fusion.6.refs_2_.refs_3_, ...), custom_call_target="tpu_custom_call" | custom-call | flops 603979776 | bytes 2494464 | tf_op jit(solution)/shard_map/pallas_call | solution.py:28
  159.5 1.8 %collective-permute-start.13 = (f32[192,128]{1,0:T(8,128)S(1)}, f32[192,128]{1,0:T(8,128)S(1)}, u32[]{:S(2)}, u32[]{:S(2)}) collective-permute-start(f32[192,128]{1,0:T(8,128)S(1)} %shard_map.68), channel_id=1, source_target_pairs={{0,2},{1,3},{2,0},{3,1},{4,6},{5,7},{6,4},{7,5},{8,10},{9,11},{10,... | collective-permute-start | bytes 294920 | tf_op jit(solution)/shard_map/ppermute | solution.py:273
  161.4 2.8 %collective-permute-done.13 = f32[192,128]{1,0:T(8,128)S(1)} collective-permute-done((f32[192,128]{1,0:T(8,128)S(1)}, f32[192,128]{1,0:T(8,128)S(1)}, u32[]{:S(2)}, u32[]{:S(2)}) %collective-permute-start.13) | collective-permute-done | bytes 98336 | tf_op jit(solution)/shard_map/ppermute | solution.py:273
  164.3 1.8 %shard_map.69.refs_3_ = f32[4,768,128]{2,1,0:T(8,128)} custom-call(s32[3]{0:T(128)S(1)} %pad_add_fusion.refs_2_.refs_0_, f32[768,128]{1,0:T(8,128)S(1)} %pad_maximum_fusion.refs_1_, f32[768,128]{1,0:T(8,128)S(1)} %collective-permute-done.18.refs_2_, f32[384,128]{1,0:T(8,128)S(1)} %pad_maximum_fusion.3.refs_3_, f32[384,128]{1,0:T(8,128)S(1)} %collective-permute-done.22.refs_4_), custom_call_target="tpu_custom_call" | custom-call | bytes 2752524 | tf_op jit(solution)/shard_map/pallas_call | solution.py:28
  (69 shorter events, 19.3 us)
Async XLA Ops:
  2.8 30.3 %all-to-all-start = ((f32[16,128,128]{2,1,0:T(8,128)}), f32[16,128,128]{2,1,0:T(8,128)S(1)}, u32[]{:S(2)}, u32[]{:S(2)}) async-start(f32[16,128,128]{2,1,0:T(8,128)} %shard_map.58), calls=%async_computation | async-start | bytes 2097152 | tf_op jit(solution)/shard_map/all_to_all | solution.py:292
  10.2 1.4 copy-start
  13.0 0.7 copy-start.1
  36.2 29.8 %all-to-all-start.1 = ((f32[16,128,128]{2,1,0:T(8,128)}), f32[16,128,128]{2,1,0:T(8,128)S(1)}, u32[]{:S(2)}, u32[]{:S(2)}) async-start(f32[16,128,128]{2,1,0:T(8,128)} %shard_map.60), calls=%async_computation.1 | async-start | bytes 2097152 | tf_op jit(solution)/shard_map/all_to_all | solution.py:292
  46.4 1.5 collective-permute-start
  48.0 7.3 %collective-permute-start.1 = (f32[192,128]{1,0:T(8,128)S(1)}, f32[192,128]{1,0:T(8,128)S(1)}, u32[]{:S(2)}, u32[]{:S(2)}) collective-permute-start(f32[192,128]{1,0:T(8,128)S(1)} %slice.57), channel_id=1, source_target_pairs={{0,2},{1,3},{2,0},{3,1},{4,6},{5,7},{6,4},{7,5},{8,10},{9,11},{10,... | collective-permute-start | bytes 294920 | tf_op jit(solution)/shard_map/ppermute | solution.py:273
  69.1 30.2 %all-to-all-start.2 = ((f32[16,128,128]{2,1,0:T(8,128)}), f32[16,128,128]{2,1,0:T(8,128)S(1)}, u32[]{:S(2)}, u32[]{:S(2)}) async-start(f32[16,128,128]{2,1,0:T(8,128)} %shard_map.62), calls=%async_computation.2 | async-start | bytes 2097152 | tf_op jit(solution)/shard_map/all_to_all | solution.py:292
  79.2 2.2 %collective-permute-start.3 = (f32[384,128]{1,0:T(8,128)S(1)}, f32[384,128]{1,0:T(8,128)S(1)}, u32[]{:S(2)}, u32[]{:S(2)}) collective-permute-start(f32[384,128]{1,0:T(8,128)S(1)} %get-tuple-element.24), channel_id=1, source_target_pairs={{0,1},{1,0},{2,3},{3,2},{4,5},{5,4},{6,7},{7,6},{8,9},{9,8},{10,11... | collective-permute-start | bytes 589832 | tf_op jit(solution)/shard_map/ppermute | solution.py:273
  79.7 15.4 %collective-permute-start.2 = (f32[96,128]{1,0:T(8,128)S(1)}, f32[96,128]{1,0:T(8,128)S(1)}, u32[]{:S(2)}, u32[]{:S(2)}) collective-permute-start(f32[96,128]{1,0:T(8,128)S(1)} %slice.59), channel_id=1, source_target_pairs={{0,4},{1,5},{2,6},{3,7},{4,0},{5,1},{6,2},{7,3},{8,12},{9,13},{10,... | collective-permute-start | bytes 147464 | tf_op jit(solution)/shard_map/ppermute | solution.py:273
  81.4 13.7 %collective-permute-start.4 = (f32[192,128]{1,0:T(8,128)S(1)}, f32[192,128]{1,0:T(8,128)S(1)}, u32[]{:S(2)}, u32[]{:S(2)}) collective-permute-start(f32[192,128]{1,0:T(8,128)S(1)} %slice.61), channel_id=1, source_target_pairs={{0,2},{1,3},{2,0},{3,1},{4,6},{5,7},{6,4},{7,5},{8,10},{9,11},{10,... | collective-permute-start | bytes 294920 | tf_op jit(solution)/shard_map/ppermute | solution.py:273
  102.4 31.3 %all-to-all-start.3 = ((f32[16,128,128]{2,1,0:T(8,128)}), f32[16,128,128]{2,1,0:T(8,128)S(1)}, u32[]{:S(2)}, u32[]{:S(2)}) async-start(f32[16,128,128]{2,1,0:T(8,128)} %shard_map.64), calls=%async_computation.3 | async-start | bytes 2097152 | tf_op jit(solution)/shard_map/all_to_all | solution.py:292
  108.9 24.8 %copy-start.2 = (bf16[3,2,2,128,128]{4,3,2,1,0:T(8,128)(2,1)S(1)}, bf16[3,2,2,128,128]{4,3,2,1,0:T(8,128)(2,1)}, u32[]{:S(2)}) copy-start(bf16[3,2,2,128,128]{4,3,2,1,0:T(8,128)(2,1)} %copy-done.1) | copy-start | bytes 1179652
  112.1 2.2 %collective-permute-start.6 = (f32[384,128]{1,0:T(8,128)S(1)}, f32[384,128]{1,0:T(8,128)S(1)}, u32[]{:S(2)}, u32[]{:S(2)}) collective-permute-start(f32[384,128]{1,0:T(8,128)S(1)} %get-tuple-element.27), channel_id=1, source_target_pairs={{0,1},{1,0},{2,3},{3,2},{4,5},{5,4},{6,7},{7,6},{8,9},{9,8},{10,11... | collective-permute-start | bytes 589832 | tf_op jit(solution)/shard_map/ppermute | solution.py:273
  112.6 15.4 %collective-permute-start.5 = (f32[96,128]{1,0:T(8,128)S(1)}, f32[96,128]{1,0:T(8,128)S(1)}, u32[]{:S(2)}, u32[]{:S(2)}) collective-permute-start(f32[96,128]{1,0:T(8,128)S(1)} %slice.63), channel_id=1, source_target_pairs={{0,4},{1,5},{2,6},{3,7},{4,0},{5,1},{6,2},{7,3},{8,12},{9,13},{10,... | collective-permute-start | bytes 147464 | tf_op jit(solution)/shard_map/ppermute | solution.py:273
  114.3 13.7 %collective-permute-start.7 = (f32[192,128]{1,0:T(8,128)S(1)}, f32[192,128]{1,0:T(8,128)S(1)}, u32[]{:S(2)}, u32[]{:S(2)}) collective-permute-start(f32[192,128]{1,0:T(8,128)S(1)} %slice.65), channel_id=1, source_target_pairs={{0,2},{1,3},{2,0},{3,1},{4,6},{5,7},{6,4},{7,5},{8,10},{9,11},{10,... | collective-permute-start | bytes 294920 | tf_op jit(solution)/shard_map/ppermute | solution.py:273
  128.0 5.7 %collective-permute-start.8 = (f32[96,128]{1,0:T(8,128)S(1)}, f32[96,128]{1,0:T(8,128)S(1)}, u32[]{:S(2)}, u32[]{:S(2)}) collective-permute-start(f32[96,128]{1,0:T(8,128)S(1)} %slice.67), channel_id=1, source_target_pairs={{0,4},{1,5},{2,6},{3,7},{4,0},{5,1},{6,2},{7,3},{8,12},{9,13},{10,... | collective-permute-start | bytes 147464 | tf_op jit(solution)/shard_map/ppermute | solution.py:273
  130.6 9.1 %collective-permute-start.15 = (f32[192,128]{1,0:T(8,128)S(1)}, f32[192,128]{1,0:T(8,128)S(1)}, u32[]{:S(2)}, u32[]{:S(2)}) collective-permute-start(f32[192,128]{1,0:T(8,128)S(1)} %pad_maximum_fusion.4), channel_id=1, source_target_pairs={{0,8},{1,9},{2,10},{3,11},{4,12},{5,13},{6,14},{7,15},{8,0},{9,1},... | collective-permute-start | bytes 294920 | tf_op jit(solution)/shard_map/ppermute | solution.py:273
  136.9 4.9 %collective-permute-start.9 = (f32[384,128]{1,0:T(8,128)S(1)}, f32[384,128]{1,0:T(8,128)S(1)}, u32[]{:S(2)}, u32[]{:S(2)}) collective-permute-start(f32[384,128]{1,0:T(8,128)S(1)} %get-tuple-element.31), channel_id=1, source_target_pairs={{0,1},{1,0},{2,3},{3,2},{4,5},{5,4},{6,7},{7,6},{8,9},{9,8},{10,11... | collective-permute-start | bytes 589832 | tf_op jit(solution)/shard_map/ppermute | solution.py:273
  139.7 5.5 %collective-permute-start.16 = (f32[192,128]{1,0:T(8,128)S(1)}, f32[192,128]{1,0:T(8,128)S(1)}, u32[]{:S(2)}, u32[]{:S(2)}) collective-permute-start(f32[192,128]{1,0:T(8,128)S(1)} %fusion), channel_id=1, source_target_pairs={{0,4},{1,5},{2,6},{3,7},{4,0},{5,1},{6,2},{7,3},{8,12},{9,13},{10,... | collective-permute-start | bytes 294920 | tf_op jit(solution)/shard_map/ppermute | solution.py:273
  139.7 6.6 %collective-permute-start.19 = (f32[96,128]{1,0:T(8,128)S(1)}, f32[96,128]{1,0:T(8,128)S(1)}, u32[]{:S(2)}, u32[]{:S(2)}) collective-permute-start(f32[96,128]{1,0:T(8,128)S(1)} %slice_add_fusion.4.refs_4_.refs_5_), channel_id=1, source_target_pairs={{0,8},{1,9},{2,10},{3,11},{4,12},{5,13},{6,14},{7,15},{8,0},{9,1},... | collective-permute-start | bytes 147464 | tf_op jit(solution)/shard_map/ppermute | solution.py:273
  141.8 6.8 %collective-permute-start.10 = (f32[192,128]{1,0:T(8,128)S(1)}, f32[192,128]{1,0:T(8,128)S(1)}, u32[]{:S(2)}, u32[]{:S(2)}) collective-permute-start(f32[192,128]{1,0:T(8,128)S(1)} %slice.69), channel_id=1, source_target_pairs={{0,2},{1,3},{2,0},{3,1},{4,6},{5,7},{6,4},{7,5},{8,10},{9,11},{10,... | collective-permute-start | bytes 294920 | tf_op jit(solution)/shard_map/ppermute | solution.py:273
  145.1 9.7 %collective-permute-start.17 = (f32[384,128]{1,0:T(8,128)S(1)}, f32[384,128]{1,0:T(8,128)S(1)}, u32[]{:S(2)}, u32[]{:S(2)}) collective-permute-start(f32[384,128]{1,0:T(8,128)S(1)} %pad_maximum_fusion.2), channel_id=1, source_target_pairs={{0,2},{1,3},{2,0},{3,1},{4,6},{5,7},{6,4},{7,5},{8,10},{9,11},{10,... | collective-permute-start | bytes 589832 | tf_op jit(solution)/shard_map/ppermute | solution.py:273
  146.3 4.4 %collective-permute-start.20 = (f32[96,128]{1,0:T(8,128)S(1)}, f32[96,128]{1,0:T(8,128)S(1)}, u32[]{:S(2)}, u32[]{:S(2)}) collective-permute-start(f32[96,128]{1,0:T(8,128)S(1)} %add.55), channel_id=1, source_target_pairs={{0,4},{1,5},{2,6},{3,7},{4,0},{5,1},{6,2},{7,3},{8,12},{9,13},{10,... | collective-permute-start | bytes 147464 | tf_op jit(solution)/shard_map/ppermute | solution.py:273
  148.7 6.1 %collective-permute-start.11 = (f32[192,128]{1,0:T(8,128)S(1)}, f32[192,128]{1,0:T(8,128)S(1)}, u32[]{:S(2)}, u32[]{:S(2)}) collective-permute-start(f32[192,128]{1,0:T(8,128)S(1)} %slice_add_fusion), channel_id=1, source_target_pairs={{0,8},{1,9},{2,10},{3,11},{4,12},{5,13},{6,14},{7,15},{8,0},{9,1},... | collective-permute-start | bytes 294920 | tf_op jit(solution)/shard_map/ppermute | solution.py:273
  150.7 10.6 %collective-permute-start.21 = (f32[192,128]{1,0:T(8,128)S(1)}, f32[192,128]{1,0:T(8,128)S(1)}, u32[]{:S(2)}, u32[]{:S(2)}) collective-permute-start(f32[192,128]{1,0:T(8,128)S(1)} %pad_maximum_fusion.5), channel_id=1, source_target_pairs={{0,2},{1,3},{2,0},{3,1},{4,6},{5,7},{6,4},{7,5},{8,10},{9,11},{10,... | collective-permute-start | bytes 294920 | tf_op jit(solution)/shard_map/ppermute | solution.py:273
  154.8 4.7 %collective-permute-start.12 = (f32[192,128]{1,0:T(8,128)S(1)}, f32[192,128]{1,0:T(8,128)S(1)}, u32[]{:S(2)}, u32[]{:S(2)}) collective-permute-start(f32[192,128]{1,0:T(8,128)S(1)} %add.53.refs_0_), channel_id=1, source_target_pairs={{0,4},{1,5},{2,6},{3,7},{4,0},{5,1},{6,2},{7,3},{8,12},{9,13},{10,... | collective-permute-start | bytes 294920 | tf_op jit(solution)/shard_map/ppermute | solution.py:273
  154.9 9.4 %collective-permute-start.18 = (f32[768,128]{1,0:T(8,128)S(1)}, f32[768,128]{1,0:T(8,128)S(1)}, u32[]{:S(2)}, u32[]{:S(2)}) collective-permute-start(f32[768,128]{1,0:T(8,128)S(1)} %pad_maximum_fusion.refs_1_), channel_id=1, source_target_pairs={{0,1},{1,0},{2,3},{3,2},{4,5},{5,4},{6,7},{7,6},{8,9},{9,8},{10,11... | collective-permute-start | bytes 1179656 | tf_op jit(solution)/shard_map/ppermute | solution.py:273
  159.5 4.7 %collective-permute-start.13 = (f32[192,128]{1,0:T(8,128)S(1)}, f32[192,128]{1,0:T(8,128)S(1)}, u32[]{:S(2)}, u32[]{:S(2)}) collective-permute-start(f32[192,128]{1,0:T(8,128)S(1)} %shard_map.68), channel_id=1, source_target_pairs={{0,2},{1,3},{2,0},{3,1},{4,6},{5,7},{6,4},{7,5},{8,10},{9,11},{10,... | collective-permute-start | bytes 294920 | tf_op jit(solution)/shard_map/ppermute | solution.py:273
  161.3 3.0 %collective-permute-start.22 = (f32[384,128]{1,0:T(8,128)S(1)}, f32[384,128]{1,0:T(8,128)S(1)}, u32[]{:S(2)}, u32[]{:S(2)}) collective-permute-start(f32[384,128]{1,0:T(8,128)S(1)} %pad_maximum_fusion.3.refs_3_), channel_id=1, source_target_pairs={{0,1},{1,0},{2,3},{3,2},{4,5},{5,4},{6,7},{7,6},{8,9},{9,8},{10,11... | collective-permute-start | bytes 589832 | tf_op jit(solution)/shard_map/ppermute | solution.py:273
  164.2 1.9 %collective-permute-start.14 = (f32[384,128]{1,0:T(8,128)S(1)}, f32[384,128]{1,0:T(8,128)S(1)}, u32[]{:S(2)}, u32[]{:S(2)}) collective-permute-start(f32[384,128]{1,0:T(8,128)S(1)} %pad_maximum_fusion.1.refs_1_), channel_id=1, source_target_pairs={{0,1},{1,0},{2,3},{3,2},{4,5},{5,4},{6,7},{7,6},{8,9},{9,8},{10,11... | collective-permute-start | bytes 589832 | tf_op jit(solution)/shard_map/ppermute | solution.py:273
